TPU v7x, 32 devices: a whole 2x2x4 slice. The times are simulated.
32 devices in a mesh: pipe: 4 (over y, x), expert: 8 (over z, core).
Axes of the slice: x: 2, y: 2, z: 4, core: 2. Of those that a mesh axis runs over, the one named last changes fastest.
Arguments:
- streams: bfloat16 [4, 2, 512, 3584], P('pipe', None, 'expert'), may hold values from -6 to 6
- norm_gain: float32 [4, 3584], P('pipe'), may hold values from 0.25 to 1.75
- w_gate: bfloat16 [4, 8, 3584, 512], P('pipe', 'expert'), may hold values from -0.09375 to 0.09375
- w_up: bfloat16 [4, 8, 3584, 512], P('pipe', 'expert'), may hold values from -0.09375 to 0.09375
- w_down: bfloat16 [4, 8, 512, 3584], P('pipe', 'expert'), may hold values from -0.1875 to 0.1875
- routes: int32 [4, 2, 512, 2], P('pipe', None, 'expert'), may hold values from 0 to 3, all different within a row; in each aligned block of 64 rows (0 to 63, 64 to 127, ..., all dimensions but the last counted through in order) at most 64 rows name the same one
- gate_weights: float32 [4, 2, 512, 2], P('pipe', None, 'expert'), may hold values from 0.2 to 1.2
Outputs:
- next_streams: bfloat16 [4, 2, 512, 3584], P('pipe', None, 'expert')
Inputs may be any that keep to these rules, and one draw needn't show every extreme that they name: `routes`: each token names 2 different experts. Within each aligned block of 64 tokens of a micro-batch (the tokens of one device of the expert axis), at most 64 tokens name the same expert, a bound that some block reaches.
All inputs are finite; a program needn't handle non-finite values.
Results may differ from a plain program's by a relative error of at most 0.0051.
Values may be sent and summed in bfloat16 or wider, within the bound.
No kernel may reach another device: no remote copies, remote signals or barrier semaphores. Data moves between devices by JAX's collectives and lax.ppermute only.
A program may use at most 128 MiB of HBM per device.

v0:
```python
import jax
import jax.numpy as jnp
from jax import lax
from jax.sharding import PartitionSpec as P


def partner_2(block, axis, bit):
    count = lax.axis_size(axis)
    route = []
    for low in range(count):
        high = low | 1 << bit
        if high != low and high < count:
            route += [(low, high), (high, low)]
    return lax.ppermute(block, axis, route)


def from_behind(value, axis, steps):
    count = lax.axis_size(axis)
    pairs = [(source, (source + steps) % count) for source in range(count)]
    return lax.ppermute(value, axis, pairs)


def shard_ffn(row_block, gate_local, up_local, down_local):
    gate_val = jnp.dot(row_block, gate_local, preferred_element_type=jnp.float32)
    up_val = jnp.dot(row_block, up_local, preferred_element_type=jnp.float32)
    hidden = (jax.nn.silu(gate_val) * up_val).astype(jnp.bfloat16)
    return jnp.dot(hidden, down_local, preferred_element_type=jnp.float32).astype(jnp.bfloat16)


def expert_pass(outgoing, gate_local, up_local, down_local, shards, capacity, width):
    experts = shards // 2
    half_cap = capacity // 2
    outbound = outgoing.reshape(shards, half_cap, width)
    arrived = lax.all_to_all(outbound, "expert", split_axis=0, concat_axis=0, tiled=True)
    partner = partner_2(arrived, "expert", 0)
    even_side = lax.axis_index("expert") % 2 == 0
    front_rows = jnp.where(even_side, arrived, partner)
    second = jnp.where(even_side, partner, arrived)
    assembled = jnp.concatenate([front_rows, second], axis=1)
    partial_value = shard_ffn(
        assembled.reshape(shards * capacity, width), gate_local, up_local, down_local
    )
    partial_value = partial_value.reshape(shards, capacity, width)
    head_part = partial_value[:, :half_cap]
    tail_part = partial_value[:, half_cap:]
    kept_part = jnp.where(even_side, head_part, tail_part)
    given_part = jnp.where(even_side, tail_part, head_part)
    received = partner_2(given_part, "expert", 0)
    summed = kept_part.astype(jnp.float32) + received.astype(jnp.float32)
    returned = lax.all_to_all(summed, "expert", split_axis=0, concat_axis=0, tiled=True)
    return returned.reshape(experts, capacity, width)


def body(streams, norm_gain, w_gate, w_up, w_down, routes, gate_weights):
    shards = lax.axis_size("expert")
    experts = shards // 2
    gate_local = w_gate[0, 0]
    up_local = w_up[0, 0]
    down_local = w_down[0, 0]
    gain_row = norm_gain[0]
    tok_rows = streams.shape[2]
    width = streams.shape[3]
    top_count = routes.shape[3]
    capacity = 2 * tok_rows * top_count // experts
    lane_count = experts * capacity
    lane_index = jnp.arange(lane_count, dtype=jnp.int32)
    expert_index = jnp.arange(experts, dtype=jnp.int32)
    results = []
    for stream in range(2):
        state = streams[0, stream].astype(jnp.float32)
        normed = (
            state * lax.rsqrt(jnp.mean(state * state, axis=-1, keepdims=True) + 1e-06) * gain_row
        ).astype(jnp.bfloat16)
        chosen = routes[0, stream].reshape(-1)
        onehot = (chosen[:, None] == expert_index[None, :]).astype(jnp.int32)
        slot_rank = jnp.sum((jnp.cumsum(onehot, axis=0) - onehot) * onehot, axis=1)
        lane_of = chosen * capacity + slot_rank
        matches = lane_index[:, None] == lane_of[None, :]
        send_matrix = jnp.sum(
            matches.reshape(lane_count, tok_rows, top_count).astype(jnp.float32), axis=-1
        ).astype(jnp.bfloat16)
        outgoing = jnp.dot(send_matrix, normed, preferred_element_type=jnp.float32).astype(
            jnp.bfloat16
        )
        outgoing = outgoing.reshape(experts, capacity, width)
        weights = gate_weights[0, stream].reshape(-1)
        combine = jnp.sum(
            (matches.astype(jnp.float32) * weights[None, :]).reshape(
                lane_count, tok_rows, top_count
            ),
            axis=-1,
        ).T
        expert_rows = expert_pass(
            outgoing, gate_local, up_local, down_local, shards, capacity, width
        )
        mixed = state + jnp.dot(
            combine,
            expert_rows.reshape(lane_count, width),
            precision=lax.Precision.HIGHEST,
            preferred_element_type=jnp.float32,
        )
        results.append(mixed.astype(jnp.bfloat16))
    forward = from_behind(results[0], "pipe", 1)
    backward = from_behind(results[1], "pipe", -1)
    return jnp.stack([forward, backward])[None]


def solution(mesh):
    return jax.shard_map(
        body,
        mesh=mesh,
        in_specs=(
            P("pipe", None, "expert", None),
            P("pipe", None),
            P("pipe", "expert", None, None),
            P("pipe", "expert", None, None),
            P("pipe", "expert", None, None),
            P("pipe", None, "expert", None),
            P("pipe", None, "expert", None),
        ),
        out_specs=P("pipe", None, "expert", None),
        check_vma=False,
    )
```

profile of v0, /device:TPU:0, one launch (start us, length us, event | category | flops | bytes accessed | tf_op | source)
XLA Modules:
  0.0 304.7 jit_solution(712597059593163562)
XLA Ops:
  3.2 1.4 fusion.12
  5.4 0.8 reduce
  6.3 1.7 convolution_convert_fusion.2
  8.0 49.7 %all_to_all.20 = bf16[8,32,3584]{2,1,0:T(8,128)(2,1)} all-to-all(bf16[8,32,3584]{2,1,0:T(8,128)(2,1)S(1)} %bitcast.77), channel_id=1, replica_groups=mesh['pipe'=4,'expert'=8] {'expert'}, dimensions={0} | all-to-all | bytes 3670016 | tf_op jit(solution)/shard_map/all_to_all | solution.py:34
  57.7 2.0 convolution_convert_fusion.3
  59.7 3.6 %all-to-all-start = ((bf16[8,32,3584]{2,1,0:T(8,128)(2,1)}), bf16[8,32,3584]{2,1,0:T(8,128)(2,1)S(1)}, u32[]{:S(2)}, u32[]{:S(2)}) async-start(bf16[8,32,3584]{2,1,0:T(8,128)(2,1)} %bitcast.4), calls=%async_computation | async-start | bytes 3670016 | tf_op jit(solution)/shard_map/all_to_all | solution.py:34
  63.3 2.3 broadcast_select_fusion.2
  65.9 1.9 copy-done.2
  67.8 1.2 copy-done.4
  69.0 3.0 fusion.4
  72.0 10.4 %convolution_convert_fusion = bf16[512,3584]{1,0:T(8,128)(2,1)} fusion(bf16[1,1,512,3584]{3,2,1,0:T(8,128)(2,1)} %param.11, f32[512,512]{1,0:T(8,128)} %fusion.4, bf16[512,3584]{1,0:T(8,128)(2,1)} %bitcast.79, bf16[1,1,3584,512]{3,2,1,0:T(8,128)(2,1)} %param.9), kind=kOutput, calls=%fused_computation | convolution fusion | flops 3761504256 | bytes 15728640 | tf_op jit(solution)/shard_map/dot_general | solution.py:27
  82.5 3.5 %broadcast_select_fusion = bf16[8,32,3584]{2,1,0:T(8,128)(2,1)} fusion(pred[]{:T(512)S(6)} %eq.74, bf16[8,64,3584]{2,1,0:T(8,128)(2,1)} %bitcast.73), kind=kLoop, calls=%fused_computation.22 | loop fusion | flops 917504 | bytes 5505025 | tf_op jit(solution)/shard_map/jit(_where)/select_n | solution.py:47
  86.4 20.3 %all-to-all-done = bf16[8,32,3584]{2,1,0:T(8,128)(2,1)S(1)} async-done(((bf16[8,32,3584]{2,1,0:T(8,128)(2,1)}), bf16[8,32,3584]{2,1,0:T(8,128)(2,1)S(1)}, u32[]{:S(2)}, u32[]{:S(2)}) %all-to-all-start) | async-done | bytes 1835040 | tf_op jit(solution)/shard_map/all_to_all | solution.py:34
  106.7 5.1 %convert_add_fusion = f32[8,32,3584]{2,1,0:T(8,128)} fusion(bf16[8,32,3584]{2,1,0:T(8,128)(2,1)} %collective-permute-done.4, pred[]{:T(512)S(6)} %eq.74, bf16[8,64,3584]{2,1,0:T(8,128)(2,1)} %bitcast.74), kind=kLoop, calls=%fused_computation.20 | loop fusion | flops 3670016 | bytes 9175041 | tf_op jit(solution)/shard_map/add | solution.py:49
  111.8 4.7 %all-to-all-start.3 = ((f32[8,32,3584]{2,1,0:T(8,128)}), f32[8,32,3584]{2,1,0:T(8,128)}, u32[]{:S(2)}, u32[]{:S(2)}) async-start(f32[8,32,3584]{2,1,0:T(8,128)} %convert_add_fusion), calls=%async_computation.3 | async-start | bytes 7340032 | tf_op jit(solution)/shard_map/all_to_all | solution.py:50
  116.5 1.7 broadcast_select_fusion.5
  118.5 1.9 copy-done.3
  120.4 1.2 copy-done.5
  121.6 2.0 fusion.6
  123.6 10.2 %convolution_convert_fusion.1 = bf16[512,3584]{1,0:T(8,128)(2,1)} fusion(bf16[1,1,512,3584]{3,2,1,0:T(8,128)(2,1)} %param.11, f32[512,512]{1,0:T(8,128)S(1)} %fusion.6, bf16[512,3584]{1,0:T(8,128)(2,1)} %bitcast.81, bf16[1,1,3584,512]{3,2,1,0:T(8,128)(2,1)} %param.9), kind=kOutput, calls=%fused_computation.1 | convolution fusion | flops 3761504256 | bytes 15728640 | tf_op jit(solution)/shard_map/dot_general | solution.py:27
  133.9 2.4 broadcast_select_fusion.3
  136.8 3.4 %collective-permute-done.1 = bf16[8,32,3584]{2,1,0:T(8,128)(2,1)S(1)} collective-permute-done((bf16[8,32,3584]{2,1,0:T(8,128)(2,1)S(1)}, bf16[8,32,3584]{2,1,0:T(8,128)(2,1)S(1)}, u32[]{:S(2)}, u32[]{:S(2)}) %collective-permute-start.1) | collective-permute-done | bytes 1835040 | tf_op jit(solution)/shard_map/ppermute | solution.py:14
  140.2 2.6 convert_add_fusion.1
  142.8 56.3 %all-to-all-done.3 = f32[8,32,3584]{2,1,0:T(8,128)} async-done(((f32[8,32,3584]{2,1,0:T(8,128)}), f32[8,32,3584]{2,1,0:T(8,128)}, u32[]{:S(2)}, u32[]{:S(2)}) %all-to-all-start.3) | async-done | bytes 3670048 | tf_op jit(solution)/shard_map/all_to_all | solution.py:50
  199.1 4.5 %all-to-all-start.1 = ((f32[8,32,3584]{2,1,0:T(8,128)}), f32[8,32,3584]{2,1,0:T(8,128)}, u32[]{:S(2)}, u32[]{:S(2)}) async-start(f32[8,32,3584]{2,1,0:T(8,128)} %convert_add_fusion.1), calls=%async_computation.1 | async-start | bytes 7340032 | tf_op jit(solution)/shard_map/all_to_all | solution.py:50
  203.6 4.3 %fusion.1 = bf16[64,3584]{1,0:T(8,128)(2,1)S(1)} fusion(f32[256,64]{0,1:T(8,128)S(1)} %get-tuple-element.10, f32[256,3584]{1,0:T(8,128)} %bitcast.19, bf16[1,2,64,3584]{3,2,1,0:T(8,128)(2,1)S(1)} %copy-done.1), kind=kOutput, calls=%fused_computation.7 | convolution fusion | flops 705331200 | bytes 4653056 | tf_op jit(solution)/shard_map/dot_general | solution.py:96
  207.9 2.5 collective-permute-start.5
  210.4 75.9 %all-to-all-done.1 = f32[8,32,3584]{2,1,0:T(8,128)} async-done(((f32[8,32,3584]{2,1,0:T(8,128)}), f32[8,32,3584]{2,1,0:T(8,128)}, u32[]{:S(2)}, u32[]{:S(2)}) %all-to-all-start.1) | async-done | bytes 3670048 | tf_op jit(solution)/shard_map/all_to_all | solution.py:50
  286.3 4.3 %fusion = bf16[64,3584]{1,0:T(8,128)(2,1)S(1)} fusion(f32[256,64]{0,1:T(8,128)S(1)} %get-tuple-element.21, f32[256,3584]{1,0:T(8,128)} %bitcast.10, bf16[1,2,64,3584]{3,2,1,0:T(8,128)(2,1)S(1)} %copy-done.1), kind=kOutput, calls=%fused_computation.6 | convolution fusion | flops 705331200 | bytes 4653056 | tf_op jit(solution)/shard_map/dot_general | solution.py:96
  290.7 1.5 collective-permute-start.2
  292.2 11.5 %collective-permute-done.2 = bf16[64,3584]{1,0:T(8,128)(2,1)S(1)} collective-permute-done((bf16[64,3584]{1,0:T(8,128)(2,1)S(1)}, bf16[64,3584]{1,0:T(8,128)(2,1)S(1)}, u32[]{:S(2)}, u32[]{:S(2)}) %collective-permute-start.2) | collective-permute-done | bytes 458784 | tf_op jit(solution)/shard_map/ppermute | solution.py:20
  303.7 1.0 maximum_bitcast_fusion
  (37 shorter events, 5.5 us)
Async XLA Ops:
  2.1 55.6 %copy-start.1 = (bf16[1,2,64,3584]{3,2,1,0:T(8,128)(2,1)S(1)}, bf16[1,2,64,3584]{3,2,1,0:T(8,128)(2,1)}, u32[]{:S(2)}) copy-start(bf16[1,2,64,3584]{3,2,1,0:T(8,128)(2,1)} %param.7) | copy-start | bytes 2752516
  57.7 5.6 %collective-permute-start.3 = (bf16[8,32,3584]{2,1,0:T(8,128)(2,1)}, bf16[8,32,3584]{2,1,0:T(8,128)(2,1)}, u32[]{:S(2)}, u32[]{:S(2)}) collective-permute-start(bf16[8,32,3584]{2,1,0:T(8,128)(2,1)} %all_to_all.20), channel_id=1, source_target_pairs={{0,1},{1,0},{2,3},{3,2},{4,5},{5,4},{6,7},{7,6},{8,9},{9,8},{10,11... | collective-permute-start | bytes 5505032 | tf_op jit(solution)/shard_map/ppermute | solution.py:14
  59.7 47.0 %all-to-all-start = ((bf16[8,32,3584]{2,1,0:T(8,128)(2,1)}), bf16[8,32,3584]{2,1,0:T(8,128)(2,1)S(1)}, u32[]{:S(2)}, u32[]{:S(2)}) async-start(bf16[8,32,3584]{2,1,0:T(8,128)(2,1)} %bitcast.4), calls=%async_computation | async-start | bytes 3670016 | tf_op jit(solution)/shard_map/all_to_all | solution.py:34
  65.6 3.4 %copy-start.4 = (bf16[1,1,3584,512]{3,2,1,0:T(8,128)(2,1)S(1)}, bf16[1,1,3584,512]{3,2,1,0:T(8,128)(2,1)}, u32[]{:S(2)}) copy-start(bf16[1,1,3584,512]{3,2,1,0:T(8,128)(2,1)} %param.10) | copy-start | bytes 11010052
  65.9 1.9 copy-start.2
  86.0 20.7 %collective-permute-start.4 = (bf16[8,32,3584]{2,1,0:T(8,128)(2,1)}, bf16[8,32,3584]{2,1,0:T(8,128)(2,1)}, u32[]{:S(2)}, u32[]{:S(2)}) collective-permute-start(bf16[8,32,3584]{2,1,0:T(8,128)(2,1)} %broadcast_select_fusion), channel_id=1, source_target_pairs={{0,1},{1,0},{2,3},{3,2},{4,5},{5,4},{6,7},{7,6},{8,9},{9,8},{10,11... | collective-permute-start | bytes 5505032 | tf_op jit(solution)/shard_map/ppermute | solution.py:14
  106.7 9.8 %collective-permute-start = (bf16[8,32,3584]{2,1,0:T(8,128)(2,1)S(1)}, bf16[8,32,3584]{2,1,0:T(8,128)(2,1)}, u32[]{:S(2)}, u32[]{:S(2)}) collective-permute-start(bf16[8,32,3584]{2,1,0:T(8,128)(2,1)S(1)} %all-to-all-done), channel_id=1, source_target_pairs={{0,1},{1,0},{2,3},{3,2},{4,5},{5,4},{6,7},{7,6},{8,9},{9,8},{10,11... | collective-permute-start | bytes 5505032 | tf_op jit(solution)/shard_map/ppermute | solution.py:14
  111.8 87.3 %all-to-all-start.3 = ((f32[8,32,3584]{2,1,0:T(8,128)}), f32[8,32,3584]{2,1,0:T(8,128)}, u32[]{:S(2)}, u32[]{:S(2)}) async-start(f32[8,32,3584]{2,1,0:T(8,128)} %convert_add_fusion), calls=%async_computation.3 | async-start | bytes 7340032 | tf_op jit(solution)/shard_map/all_to_all | solution.py:50
  118.2 3.4 %copy-start.5 = (bf16[1,1,3584,512]{3,2,1,0:T(8,128)(2,1)S(1)}, bf16[1,1,3584,512]{3,2,1,0:T(8,128)(2,1)}, u32[]{:S(2)}) copy-start(bf16[1,1,3584,512]{3,2,1,0:T(8,128)(2,1)} %param.10) | copy-start | bytes 11010052
  118.5 1.9 copy-start.3
  133.9 6.3 %copy-start = (bf16[512,3584]{1,0:T(8,128)(2,1)S(1)}, bf16[512,3584]{1,0:T(8,128)(2,1)}, u32[]{:S(2)}) copy-start(bf16[512,3584]{1,0:T(8,128)(2,1)} %convolution_convert_fusion.1) | copy-start | bytes 11010052
  136.3 3.9 %collective-permute-start.1 = (bf16[8,32,3584]{2,1,0:T(8,128)(2,1)S(1)}, bf16[8,32,3584]{2,1,0:T(8,128)(2,1)S(1)}, u32[]{:S(2)}, u32[]{:S(2)}) collective-permute-start(bf16[8,32,3584]{2,1,0:T(8,128)(2,1)S(1)} %broadcast_select_fusion.3), channel_id=1, source_target_pairs={{0,1},{1,0},{2,3},{3,2},{4,5},{5,4},{6,7},{7,6},{8,9},{9,8},{10,11... | collective-permute-start | bytes 5505032 | tf_op jit(solution)/shard_map/ppermute | solution.py:14
  199.1 87.3 %all-to-all-start.1 = ((f32[8,32,3584]{2,1,0:T(8,128)}), f32[8,32,3584]{2,1,0:T(8,128)}, u32[]{:S(2)}, u32[]{:S(2)}) async-start(f32[8,32,3584]{2,1,0:T(8,128)} %convert_add_fusion.1), calls=%async_computation.1 | async-start | bytes 7340032 | tf_op jit(solution)/shard_map/all_to_all | solution.py:50
  207.9 84.3 %collective-permute-start.5 = (bf16[64,3584]{1,0:T(8,128)(2,1)S(1)}, bf16[64,3584]{1,0:T(8,128)(2,1)S(1)}, u32[]{:S(2)}, u32[]{:S(2)}) collective-permute-start(bf16[64,3584]{1,0:T(8,128)(2,1)S(1)} %fusion.1), channel_id=1, source_target_pairs={{0,24},{8,0},{16,8},{24,16},{1,25},{9,1},{17,9},{25,17},{2,26},{10... | collective-permute-start | bytes 1376264 | tf_op jit(solution)/shard_map/ppermute | solution.py:20
  290.7 13.0 %collective-permute-start.2 = (bf16[64,3584]{1,0:T(8,128)(2,1)S(1)}, bf16[64,3584]{1,0:T(8,128)(2,1)S(1)}, u32[]{:S(2)}, u32[]{:S(2)}) collective-permute-start(bf16[64,3584]{1,0:T(8,128)(2,1)S(1)} %fusion), channel_id=1, source_target_pairs={{0,8},{8,16},{16,24},{24,0},{1,9},{9,17},{17,25},{25,1},{2,10},{10... | collective-permute-start | bytes 1376264 | tf_op jit(solution)/shard_map/ppermute | solution.py:20
where the time goes:
time: 305 us
  waiting for transfers between devices  167 us (55%)
  blocking collectives  49.7 us (16%)
  matrix products  38.2 us (13%)
  other arithmetic  23 us (8%)
  starting transfers between devices  17.8 us (6%)
  local copies, waits for them, and re-layouts  8.53 us (3%)
    all_to_all x2, waiting for transfers between devices, expert_pass(): lax.all_to_all(summed, 'expert', split_axis=0, concat_axis=0, tiled=True)  132 us
    all_to_all x1, blocking collectives, expert_pass(): lax.all_to_all(outbound, 'expert', split_axis=0, concat_axis=0, tiled=True)  49.7 us
    dot_general x2, matrix products, shard_ffn(): jnp.dot(hidden, down_local, preferred_element_type=jnp.float32)  20.7 us
    all_to_all x1, waiting for transfers between devices, expert_pass(): lax.all_to_all(outbound, 'expert', split_axis=0, concat_axis=0, tiled=True)  20.3 us
    ppermute x2, waiting for transfers between devices, from_behind(): return lax.ppermute(value, axis, pairs)  11.5 us
    all_to_all x2, starting transfers between devices, expert_pass(): lax.all_to_all(summed, 'expert', split_axis=0, concat_axis=0, tiled=True)  9.18 us
    dot_general x2, matrix products, body(): jnp.dot(combine, expert_rows.reshape(lane_count, width), precision=lax.Pr...  8.69 us
    add x2, other arithmetic, expert_pass(): summed = kept_part.astype(jnp.float32) + received.astype(jnp.float32)  7.7 us
  transfers between devices with their start and end apart: 9, of which 5 were waited for; matrix products, arithmetic and copies ran while one was open for 18% of the time, Pallas kernels for 0%

commit v1 on v0

v1 whole, which is shorter than its diff:
```python
import jax
import jax.numpy as jnp
from jax import lax
from jax.sharding import PartitionSpec as P

CHUNKS = 2


def swap_cores(value):
    count = lax.axis_size("expert")
    return lax.ppermute(value, "expert", [(i, i ^ 1) for i in range(count)])


def hop(value, up_from, down_from):
    pairs = [(2 * z, 2 * z + 2) for z in up_from] + [(2 * z + 1, 2 * z - 1) for z in down_from]
    return lax.ppermute(value, "expert", pairs)


def gather_hop(value, step):
    chips = lax.axis_size("expert") // 2
    return hop(value, range(step, chips - 1), range(1, chips - step))


def reduce_hop(value, step):
    chips = lax.axis_size("expert") // 2
    return hop(value, range(0, chips - 1 - step), range(1 + step, chips))


def ffn(rows, scale, gate_local, up_local, down_local):
    gate_val = jnp.dot(rows, gate_local, preferred_element_type=jnp.float32)
    up_val = jnp.dot(rows, up_local, preferred_element_type=jnp.float32)
    hidden = (jax.nn.silu(gate_val) * up_val * scale).astype(jnp.bfloat16)
    return jnp.dot(hidden, down_local, preferred_element_type=jnp.float32).astype(jnp.bfloat16)


def add(a, b):
    return (a.astype(jnp.float32) + b.astype(jnp.float32)).astype(jnp.bfloat16)


def chunk_pass(state, scale_of, weights):
    chips = lax.axis_size("expert") // 2
    rank = lax.axis_index("expert")
    chip, core = rank // 2, rank % 2
    rows = state.shape[0]
    normed = state
    own = jnp.concatenate([normed, swap_cores(normed)], axis=0)
    travelling = own
    partials = []
    for step in range(chips - 1):
        travelling = gather_hop(travelling, step)
        other = swap_cores(travelling)
        below, above = chip - 1 - step, chip + 1 + step
        if 2 * step <= chips - 3:
            first = jnp.where(core == 0, below, above)
            second = jnp.where(core == 0, above, below)
            given = ffn(travelling, scale_of(first, core), *weights)
            kept = ffn(other, scale_of(second, 1 - core), *weights)
            partials.append(add(kept, swap_cores(given)))
        else:
            from_below = below >= 0
            source_core = jnp.where(from_below, 0, 1)
            block = jnp.where(core == source_core, travelling, other)
            half = ffn(block, scale_of(jnp.where(from_below, below, above), source_core), *weights)
            partials.append(add(half, swap_cores(half)))
    local = ffn(own, scale_of(chip, core), *weights)
    total = None
    for step in reversed(range(chips - 1)):
        payload = partials[step] if total is None else add(partials[step], total)
        total = reduce_hop(payload, step)
    given = add(total[:rows], local[rows:])
    return total[rows:].astype(jnp.float32) + local[:rows].astype(jnp.float32) + swap_cores(given).astype(jnp.float32)


def body(streams, norm_gain, w_gate, w_up, w_down, routes, gate_weights):
    chips = lax.axis_size("expert") // 2
    sections = lax.axis_size("pipe")
    weights = (w_gate[0, 0], w_up[0, 0], w_down[0, 0])
    tokens = streams.shape[2]
    per_stream = CHUNKS // 2
    rows = tokens // per_stream
    named = routes[0][..., None] == jnp.arange(chips, dtype=jnp.int32)
    dense = jnp.sum(jnp.where(named, gate_weights[0][..., None], 0.0), axis=2)
    dense_all = lax.all_gather(dense, "expert").reshape(chips, 2, 2, tokens, chips)
    mine = jnp.sum(jnp.where(jnp.arange(chips) == lax.axis_index("expert") // 2, dense_all, 0.0), axis=-1)
    outs = []
    for stream in range(2):
        state = streams[0, stream].astype(jnp.float32)
        normed = (
            state * lax.rsqrt(jnp.mean(state * state, axis=-1, keepdims=True) + 1e-06) * norm_gain[0]
        ).astype(jnp.bfloat16)
        pieces = []
        for part in range(per_stream):
            cut = slice(part * rows, (part + 1) * rows)

            def scale_of(chip, first_core, stream=stream, cut=cut):
                block = lax.dynamic_index_in_dim(mine[:, :, stream, cut], jnp.clip(chip, 0, chips - 1), 0, keepdims=False)
                block = jnp.where(first_core == 0, block, block[::-1])
                return block.reshape(-1, 1)

            mixed = state[cut] + chunk_pass(normed[cut], scale_of, weights)
            shift = 1 if stream == 0 else sections - 1
            pairs = [(source, (source + shift) % sections) for source in range(sections)]
            pieces.append(lax.ppermute(mixed.astype(jnp.bfloat16), "pipe", pairs))
        outs.append(jnp.concatenate(pieces, axis=0))
    return jnp.stack(outs)[None]


def solution(mesh):
    return jax.shard_map(
        body,
        mesh=mesh,
        in_specs=(
            P("pipe", None, "expert", None),
            P("pipe", None),
            P("pipe", "expert", None, None),
            P("pipe", "expert", None, None),
            P("pipe", "expert", None, None),
            P("pipe", None, "expert", None),
            P("pipe", None, "expert", None),
        ),
        out_specs=P("pipe", None, "expert", None),
        check_vma=False,
    )
```

time: 305 us -> 222 us (0.73)
  the two profiles are of different devices: /device:TPU:0 before, /device:TPU:22 now
where the time goes in v1:
time: 222 us; the launch traced here: 218 us
  matrix products  82.8 us (37%)
  waiting for transfers between devices  65.9 us (30%)
  starting transfers between devices  38.3 us (17%)
  other arithmetic  17.7 us (8%)
  blocking collectives  12.2 us (5%)
    dot_general x10, matrix products, ffn(): jnp.dot(hidden, down_local, preferred_element_type=jnp.float32)  56.2 us
    ppermute x12, waiting for transfers between devices, hop(): return lax.ppermute(value, 'expert', pairs)  44.1 us
    ppermute x12, starting transfers between devices, hop(): return lax.ppermute(value, 'expert', pairs)  26.9 us
    dot_general x10, matrix products, ffn(): up_val = jnp.dot(rows, up_local, preferred_element_type=jnp.float32)  26.6 us
    ppermute x2, waiting for transfers between devices, body(): pieces.append(lax.ppermute(mixed.astype(jnp.bfloat16), 'pipe', pairs))  19.6 us
    all_gather x1, blocking collectives, body(): lax.all_gather(dense, 'expert').reshape(chips, 2, 2, tokens, chips)  12.2 us
    ppermute x16, starting transfers between devices, swap_cores(): return lax.ppermute(value, 'expert', [(i, i ^ 1) for i in range(count)])  8.45 us
    convert_element_type x6, other arithmetic, add(): return (a.astype(jnp.float32) + b.astype(jnp.float32)).astype(jnp.bfloat16)  8.25 us
  transfers between devices with their start and end apart: 30, of which 10 were waited for; matrix products, arithmetic and copies ran while one was open for 44% of the time, Pallas kernels for 0%

profile of v1, /device:TPU:22, one launch (start us, length us, event | category | flops | bytes accessed | tf_op | source)
XLA Modules:
  0.0 218.4 jit_solution(2203484296674924893)
XLA Ops:
  4.9 12.2 %all-gather = f32[16,64,4]{1,2,0:T(4,128)S(1)} all-gather(f32[2,64,4]{1,2,0:T(4,128)S(1)} %select_reduce_fusion.1), channel_id=2, replica_groups=mesh['pipe'=4,'expert'=8] {'expert'}, dimensions={0}, use_global_device_ids=true | all-gather | bytes 18432 | tf_op jit(solution)/shard_map/all_gather | solution.py:83
  19.6 5.5 %collective-permute-start.1 = (bf16[128,3584]{1,0:T(8,128)(2,1)}, bf16[128,3584]{1,0:T(8,128)(2,1)S(1)}, u32[]{:S(2)}, u32[]{:S(2)}) collective-permute-start(bf16[128,3584]{1,0:T(8,128)(2,1)} %pad_maximum_fusion), channel_id=1, source_target_pairs={{0,2},{2,4},{4,6},{3,1},{5,3},{7,5},{8,10},{10,12},{12,14},{11,9},... | collective-permute-start | bytes 2752520 | tf_op jit(solution)/shard_map/ppermute | solution.py:16
  28.1 3.6 %fusion.22 = f32[128,512]{1,0:T(8,128)} fusion(bf16[1,1,3584,512]{3,2,1,0:T(8,128)(2,1)} %param.10, bf16[64,3584]{1,0:T(8,128)(2,1)} %copy-done.5, bf16[64,3584]{1,0:T(8,128)(2,1)S(1)} %get-tuple-element.7), kind=kOutput, calls=%fused_computation.32 | convolution fusion | flops 471597056 | bytes 4849664 | tf_op jit(solution)/shard_map/dot_general | solution.py:31
  33.0 5.6 %convolution_convert_fusion.5 = bf16[128,3584]{1,0:T(8,128)(2,1)} fusion(bf16[1,1,512,3584]{3,2,1,0:T(8,128)(2,1)} %param.11, f32[128,512]{1,0:T(8,128)} %fusion.22, bf16[1,1,3584,512]{3,2,1,0:T(8,128)(2,1)} %param.9, f32[128]{0:T(128)S(1)} %mul.227, bf16[64,3584]{1,0:T(8,128)(2,1)} %copy-done.5, bf16[64,3584]{1,0:T(8,128)(2,1)S(1)} %get-tuple-element.7), kind=kOutput, calls=%fused_computation.6 | convolution fusion | flops 942276608 | bytes 9437696 | tf_op jit(solution)/shard_map/dot_general | solution.py:33
  38.5 2.1 collective-permute-start.4
  40.6 5.5 %convolution_convert_fusion = bf16[128,3584]{1,0:T(8,128)(2,1)} fusion(bf16[1,1,512,3584]{3,2,1,0:T(8,128)(2,1)} %param.11, f32[128,512]{1,0:T(8,128)} %fusion.12, bf16[1,1,3584,512]{3,2,1,0:T(8,128)(2,1)} %param.9, f32[128]{0:T(128)S(1)} %mul.256, bf16[64,3584]{1,0:T(8,128)(2,1)S(1)} %collective-permute-done.15, bf16[64,3584]{1,0:T(8,128)(2,1)S(1)} %get-tuple-element.8), kind=kOutput, calls=%fused_computation | convolution fusion | flops 942276608 | bytes 9437696 | tf_op jit(solution)/shard_map/dot_general | solution.py:33
  46.2 2.7 %fusion.28 = f32[128,512]{1,0:T(8,128)S(1)} fusion(bf16[128,3584]{1,0:T(8,128)(2,1)S(1)} %collective-permute-done.1, bf16[1,1,3584,512]{3,2,1,0:T(8,128)(2,1)} %param.10), kind=kOutput, calls=%fused_computation.38 | convolution fusion | flops 469762048 | bytes 4849664 | tf_op jit(solution)/shard_map/dot_general | solution.py:31
  48.8 5.4 %convolution_convert_fusion.8 = bf16[128,3584]{1,0:T(8,128)(2,1)} fusion(bf16[1,1,512,3584]{3,2,1,0:T(8,128)(2,1)} %param.11, f32[128,512]{1,0:T(8,128)S(1)} %fusion.28, bf16[128,3584]{1,0:T(8,128)(2,1)S(1)} %collective-permute-done.1, bf16[1,1,3584,512]{3,2,1,0:T(8,128)(2,1)} %param.9, f32[128]{0:T(128)S(1)} %mul.212), kind=kOutput, calls=%fused_computation.9 | convolution fusion | flops 940441600 | bytes 9437696 | tf_op jit(solution)/shard_map/dot_general | solution.py:33
  56.6 3.4 %collective-permute-start.5 = (bf16[128,3584]{1,0:T(8,128)(2,1)}, bf16[128,3584]{1,0:T(8,128)(2,1)}, u32[]{:S(2)}, u32[]{:S(2)}) collective-permute-start(bf16[128,3584]{1,0:T(8,128)(2,1)} %collective-permute-done.4), channel_id=1, source_target_pairs={{0,1},{1,0},{2,3},{3,2},{4,5},{5,4},{6,7},{7,6},{8,9},{9,8},{10,11... | collective-permute-start | bytes 2752520 | tf_op jit(solution)/shard_map/ppermute | solution.py:11
  60.0 2.7 %fusion.18 = f32[128,512]{1,0:T(8,128)S(1)} fusion(bf16[128,3584]{1,0:T(8,128)(2,1)S(1)} %collective-permute-done.16, bf16[1,1,3584,512]{3,2,1,0:T(8,128)(2,1)} %param.10), kind=kOutput, calls=%fused_computation.28 | convolution fusion | flops 469762048 | bytes 4849664 | tf_op jit(solution)/shard_map/dot_general | solution.py:31
  62.7 5.4 %convolution_convert_fusion.3 = bf16[128,3584]{1,0:T(8,128)(2,1)} fusion(bf16[1,1,512,3584]{3,2,1,0:T(8,128)(2,1)} %param.11, f32[128,512]{1,0:T(8,128)S(1)} %fusion.18, bf16[128,3584]{1,0:T(8,128)(2,1)S(1)} %collective-permute-done.16, bf16[1,1,3584,512]{3,2,1,0:T(8,128)(2,1)} %param.9, f32[128]{0:T(128)S(1)} %mul.241), kind=kOutput, calls=%fused_computation.3 | convolution fusion | flops 940441600 | bytes 9437696 | tf_op jit(solution)/shard_map/dot_general | solution.py:33
  68.6 2.9 %fusion.30 = f32[128,512]{1,0:T(8,128)S(1)} fusion(bf16[128,3584]{1,0:T(8,128)(2,1)S(1)} %collective-permute-done.2, bf16[1,1,3584,512]{3,2,1,0:T(8,128)(2,1)} %param.10), kind=kOutput, calls=%fused_computation.40 | convolution fusion | flops 469762048 | bytes 4849664 | tf_op jit(solution)/shard_map/dot_general | solution.py:31
  71.5 2.3 %collective-permute-start.7 = (bf16[128,3584]{1,0:T(8,128)(2,1)}, bf16[128,3584]{1,0:T(8,128)(2,1)}, u32[]{:S(2)}, u32[]{:S(2)}) collective-permute-start(bf16[128,3584]{1,0:T(8,128)(2,1)} %collective-permute-done.4), channel_id=1, source_target_pairs={{4,6},{3,1},{12,14},{11,9},{20,22},{19,17},{28,30},{27,25}} | collective-permute-start | bytes 2752520 | tf_op jit(solution)/shard_map/ppermute | solution.py:16
  75.7 5.7 %convolution_convert_fusion.7 = bf16[128,3584]{1,0:T(8,128)(2,1)} fusion(bf16[1,1,512,3584]{3,2,1,0:T(8,128)(2,1)} %param.11, f32[128,512]{1,0:T(8,128)S(1)} %fusion.26, bf16[1,1,3584,512]{3,2,1,0:T(8,128)(2,1)} %param.9, bf16[128,3584]{1,0:T(8,128)(2,1)} %collective-permute-done.4, bf16[128,3584]{1,0:T(8,128)(2,1)} %collective-permute-done.5, pred[]{:T(512)S(6)} %eq.62, ...), kind=kOutput, calls=%fused_computation.8 | convolution fusion | flops 940900352 | bytes 10355201 | tf_op jit(solution)/shard_map/dot_general | solution.py:33
  81.4 2.6 %collective-permute-done.7 = bf16[128,3584]{1,0:T(8,128)(2,1)} collective-permute-done((bf16[128,3584]{1,0:T(8,128)(2,1)}, bf16[128,3584]{1,0:T(8,128)(2,1)}, u32[]{:S(2)}, u32[]{:S(2)}) %collective-permute-start.7) | collective-permute-done | bytes 917536 | tf_op jit(solution)/shard_map/ppermute | solution.py:16
  84.0 5.4 %collective-permute-start.22 = (bf16[128,3584]{1,0:T(8,128)(2,1)}, bf16[128,3584]{1,0:T(8,128)(2,1)}, u32[]{:S(2)}, u32[]{:S(2)}) collective-permute-start(bf16[128,3584]{1,0:T(8,128)(2,1)} %collective-permute-done.19), channel_id=1, source_target_pairs={{4,6},{3,1},{12,14},{11,9},{20,22},{19,17},{28,30},{27,25}} | collective-permute-start | bytes 2752520 | tf_op jit(solution)/shard_map/ppermute | solution.py:16
  89.4 3.0 %fusion.16 = f32[128,512]{1,0:T(8,128)S(1)} fusion(bf16[1,1,3584,512]{3,2,1,0:T(8,128)(2,1)} %param.10, bf16[128,3584]{1,0:T(8,128)(2,1)} %collective-permute-done.19, bf16[128,3584]{1,0:T(8,128)(2,1)} %collective-permute-done.20, pred[]{:T(512)S(6)} %eq.62), kind=kOutput, calls=%fused_computation.26 | convolution fusion | flops 470220800 | bytes 5767169 | tf_op jit(solution)/shard_map/dot_general | solution.py:31
  92.4 5.7 %convolution_convert_fusion.2 = bf16[128,3584]{1,0:T(8,128)(2,1)} fusion(bf16[1,1,512,3584]{3,2,1,0:T(8,128)(2,1)} %param.11, f32[128,512]{1,0:T(8,128)S(1)} %fusion.16, bf16[1,1,3584,512]{3,2,1,0:T(8,128)(2,1)} %param.9, bf16[128,3584]{1,0:T(8,128)(2,1)} %collective-permute-done.19, bf16[128,3584]{1,0:T(8,128)(2,1)} %collective-permute-done.20, ...), kind=kOutput, calls=%fused_computation.2 | convolution fusion | flops 940900352 | bytes 10355201 | tf_op jit(solution)/shard_map/dot_general | solution.py:33
  100.1 3.0 %fusion.24 = f32[128,512]{1,0:T(8,128)S(1)} fusion(bf16[1,1,3584,512]{3,2,1,0:T(8,128)(2,1)} %param.10, bf16[128,3584]{1,0:T(8,128)(2,1)} %collective-permute-done.7, bf16[128,3584]{1,0:T(8,128)(2,1)} %collective-permute-done.8, pred[]{:T(512)S(6)} %eq.64), kind=kOutput, calls=%fused_computation.34 | convolution fusion | flops 470220800 | bytes 5767169 | tf_op jit(solution)/shard_map/dot_general | solution.py:31
  103.1 5.7 %convolution_convert_fusion.6 = bf16[128,3584]{1,0:T(8,128)(2,1)} fusion(bf16[1,1,512,3584]{3,2,1,0:T(8,128)(2,1)} %param.11, f32[128,512]{1,0:T(8,128)S(1)} %fusion.24, bf16[1,1,3584,512]{3,2,1,0:T(8,128)(2,1)} %param.9, bf16[128,3584]{1,0:T(8,128)(2,1)} %collective-permute-done.7, bf16[128,3584]{1,0:T(8,128)(2,1)} %collective-permute-done.8, pred[]{:T(512)S(6)} %eq.64, ...), kind=kOutput, calls=%fused_computation.7 | convolution fusion | flops 940900352 | bytes 10355201 | tf_op jit(solution)/shard_map/dot_general | solution.py:33
  108.8 3.0 %fusion.14 = f32[128,512]{1,0:T(8,128)S(1)} fusion(bf16[1,1,3584,512]{3,2,1,0:T(8,128)(2,1)} %param.10, bf16[128,3584]{1,0:T(8,128)(2,1)} %collective-permute-done.22, bf16[128,3584]{1,0:T(8,128)(2,1)} %collective-permute-done.23, pred[]{:T(512)S(6)} %eq.64), kind=kOutput, calls=%fused_computation.24 | convolution fusion | flops 470220800 | bytes 5767169 | tf_op jit(solution)/shard_map/dot_general | solution.py:31
  111.8 5.7 %convolution_convert_fusion.1 = bf16[128,3584]{1,0:T(8,128)(2,1)} fusion(bf16[1,1,512,3584]{3,2,1,0:T(8,128)(2,1)} %param.11, f32[128,512]{1,0:T(8,128)S(1)} %fusion.14, bf16[1,1,3584,512]{3,2,1,0:T(8,128)(2,1)} %param.9, bf16[128,3584]{1,0:T(8,128)(2,1)} %collective-permute-done.22, bf16[128,3584]{1,0:T(8,128)(2,1)} %collective-permute-done.23, ...), kind=kOutput, calls=%fused_computation.1 | convolution fusion | flops 940900352 | bytes 10355201 | tf_op jit(solution)/shard_map/dot_general | solution.py:33
  129.6 21.1 %collective-permute-done.11 = bf16[128,3584]{1,0:T(8,128)(2,1)} collective-permute-done((bf16[128,3584]{1,0:T(8,128)(2,1)S(1)}, bf16[128,3584]{1,0:T(8,128)(2,1)}, u32[]{:S(2)}, u32[]{:S(2)}) %collective-permute-start.11) | collective-permute-done | bytes 917536 | tf_op jit(solution)/shard_map/ppermute | solution.py:16
  150.7 5.8 %add_convert_fusion.5 = bf16[128,3584]{1,0:T(8,128)(2,1)} fusion(bf16[128,3584]{1,0:T(8,128)(2,1)} %collective-permute-done.11, bf16[128,3584]{1,0:T(8,128)(2,1)} %collective-permute-done.3, bf16[1,1,512,3584]{3,2,1,0:T(8,128)(2,1)} %param.11, f32[128,512]{1,0:T(8,128)S(1)} %fusion.30, bf16[128,3584]{1,0:T(8,128)(2,1)S(1)} %collective-permute-done.2, ...), kind=kOutput, calls=%fused_computation.67 | convolution fusion | flops 944111616 | bytes 11272704 | tf_op jit(solution)/shard_map/dot_general | solution.py:33
  158.5 2.7 %fusion.20 = f32[128,512]{1,0:T(8,128)S(1)} fusion(bf16[128,3584]{1,0:T(8,128)(2,1)S(1)} %collective-permute-done.17, bf16[1,1,3584,512]{3,2,1,0:T(8,128)(2,1)} %param.10), kind=kOutput, calls=%fused_computation.30 | convolution fusion | flops 469762048 | bytes 4849664 | tf_op jit(solution)/shard_map/dot_general | solution.py:31
  161.2 3.5 %collective-permute-done.26 = bf16[128,3584]{1,0:T(8,128)(2,1)} collective-permute-done((bf16[128,3584]{1,0:T(8,128)(2,1)}, bf16[128,3584]{1,0:T(8,128)(2,1)}, u32[]{:S(2)}, u32[]{:S(2)}) %collective-permute-start.26) | collective-permute-done | bytes 917536 | tf_op jit(solution)/shard_map/ppermute | solution.py:16
  164.7 5.8 %add_convert_fusion = bf16[128,3584]{1,0:T(8,128)(2,1)} fusion(bf16[128,3584]{1,0:T(8,128)(2,1)} %collective-permute-done.26, bf16[128,3584]{1,0:T(8,128)(2,1)} %collective-permute-done.18, bf16[1,1,512,3584]{3,2,1,0:T(8,128)(2,1)} %param.11, f32[128,512]{1,0:T(8,128)S(1)} %fusion.20, bf16[128,3584]{1,0:T(8,128)(2,1)S(1)} %collective-permute-done.17, ...), kind=kOutput, calls=%fused_computation.62 | convolution fusion | flops 944111616 | bytes 11272704 | tf_op jit(solution)/shard_map/dot_general | solution.py:33
  172.4 6.7 %collective-permute-done.12 = bf16[128,3584]{1,0:T(8,128)(2,1)} collective-permute-done((bf16[128,3584]{1,0:T(8,128)(2,1)}, bf16[128,3584]{1,0:T(8,128)(2,1)}, u32[]{:S(2)}, u32[]{:S(2)}) %collective-permute-start.12) | collective-permute-done | bytes 917536 | tf_op jit(solution)/shard_map/ppermute | solution.py:16
  180.9 8.6 %collective-permute-done.27 = bf16[128,3584]{1,0:T(8,128)(2,1)S(1)} collective-permute-done((bf16[128,3584]{1,0:T(8,128)(2,1)}, bf16[128,3584]{1,0:T(8,128)(2,1)S(1)}, u32[]{:S(2)}, u32[]{:S(2)}) %collective-permute-start.27) | collective-permute-done | bytes 917536 | tf_op jit(solution)/shard_map/ppermute | solution.py:16
  195.4 2.4 %collective-permute-start.14 = (bf16[64,3584]{1,0:T(8,128)(2,1)S(1)}, bf16[64,3584]{1,0:T(8,128)(2,1)S(1)}, u32[]{:S(2)}, u32[]{:S(2)}) collective-permute-start(bf16[64,3584]{1,0:T(8,128)(2,1)S(1)} %get-tuple-element.9), channel_id=1, source_target_pairs={{0,8},{8,16},{16,24},{24,0},{1,9},{9,17},{17,25},{25,1},{2,10},{10... | collective-permute-start | bytes 1376264 | tf_op jit(solution)/shard_map/ppermute | solution.py:103
  197.8 11.3 %collective-permute-done.29 = bf16[64,3584]{1,0:T(8,128)(2,1)S(1)} collective-permute-done((bf16[64,3584]{1,0:T(8,128)(2,1)S(1)}, bf16[64,3584]{1,0:T(8,128)(2,1)S(1)}, u32[]{:S(2)}, u32[]{:S(2)}) %collective-permute-start.29) | collective-permute-done | bytes 458784 | tf_op jit(solution)/shard_map/ppermute | solution.py:103
  209.1 8.3 %collective-permute-done.14 = bf16[64,3584]{1,0:T(8,128)(2,1)S(1)} collective-permute-done((bf16[64,3584]{1,0:T(8,128)(2,1)S(1)}, bf16[64,3584]{1,0:T(8,128)(2,1)S(1)}, u32[]{:S(2)}, u32[]{:S(2)}) %collective-permute-start.14) | collective-permute-done | bytes 458784 | tf_op jit(solution)/shard_map/ppermute | solution.py:103
  (111 shorter events, 42.9 us)
Async XLA Ops:
  3.7 14.9 %collective-permute-start = (bf16[64,3584]{1,0:T(8,128)(2,1)S(1)}, bf16[64,3584]{1,0:T(8,128)(2,1)S(1)}, u32[]{:S(2)}, u32[]{:S(2)}) collective-permute-start(bf16[64,3584]{1,0:T(8,128)(2,1)S(1)} %get-tuple-element.7), channel_id=1, source_target_pairs={{0,1},{1,0},{2,3},{3,2},{4,5},{5,4},{6,7},{7,6},{8,9},{9,8},{10,11... | collective-permute-start | bytes 1376264 | tf_op jit(solution)/shard_map/ppermute | solution.py:11
  3.7 21.4 %collective-permute-start.15 = (bf16[64,3584]{1,0:T(8,128)(2,1)S(1)}, bf16[64,3584]{1,0:T(8,128)(2,1)S(1)}, u32[]{:S(2)}, u32[]{:S(2)}) collective-permute-start(bf16[64,3584]{1,0:T(8,128)(2,1)S(1)} %get-tuple-element.8), channel_id=1, source_target_pairs={{0,1},{1,0},{2,3},{3,2},{4,5},{5,4},{6,7},{7,6},{8,9},{9,8},{10,11... | collective-permute-start | bytes 1376264 | tf_op jit(solution)/shard_map/ppermute | solution.py:11
  19.6 12.0 %copy-start = (bf16[1,1,3584,512]{3,2,1,0:T(8,128)(2,1)S(1)}, bf16[1,1,3584,512]{3,2,1,0:T(8,128)(2,1)}, u32[]{:S(2)}) copy-start(bf16[1,1,3584,512]{3,2,1,0:T(8,128)(2,1)} %param.10) | copy-start | bytes 11010052
  19.6 18.9 %collective-permute-start.1 = (bf16[128,3584]{1,0:T(8,128)(2,1)}, bf16[128,3584]{1,0:T(8,128)(2,1)S(1)}, u32[]{:S(2)}, u32[]{:S(2)}) collective-permute-start(bf16[128,3584]{1,0:T(8,128)(2,1)} %pad_maximum_fusion), channel_id=1, source_target_pairs={{0,2},{2,4},{4,6},{3,1},{5,3},{7,5},{8,10},{10,12},{12,14},{11,9},... | collective-permute-start | bytes 2752520 | tf_op jit(solution)/shard_map/ppermute | solution.py:16
  26.1 28.5 %collective-permute-start.16 = (bf16[128,3584]{1,0:T(8,128)(2,1)}, bf16[128,3584]{1,0:T(8,128)(2,1)S(1)}, u32[]{:S(2)}, u32[]{:S(2)}) collective-permute-start(bf16[128,3584]{1,0:T(8,128)(2,1)} %pad_maximum_fusion.1), channel_id=1, source_target_pairs={{0,2},{2,4},{4,6},{3,1},{5,3},{7,5},{8,10},{10,12},{12,14},{11,9},... | collective-permute-start | bytes 2752520 | tf_op jit(solution)/shard_map/ppermute | solution.py:16
  38.5 18.0 %collective-permute-start.4 = (bf16[128,3584]{1,0:T(8,128)(2,1)S(1)}, bf16[128,3584]{1,0:T(8,128)(2,1)}, u32[]{:S(2)}, u32[]{:S(2)}) collective-permute-start(bf16[128,3584]{1,0:T(8,128)(2,1)S(1)} %collective-permute-done.1), channel_id=1, source_target_pairs={{2,4},{4,6},{3,1},{5,3},{10,12},{12,14},{11,9},{13,11},{18,20},{20... | collective-permute-start | bytes 2752520 | tf_op jit(solution)/shard_map/ppermute | solution.py:16
  46.1 22.0 %collective-permute-start.2 = (bf16[128,3584]{1,0:T(8,128)(2,1)S(1)}, bf16[128,3584]{1,0:T(8,128)(2,1)S(1)}, u32[]{:S(2)}, u32[]{:S(2)}) collective-permute-start(bf16[128,3584]{1,0:T(8,128)(2,1)S(1)} %collective-permute-done.1), channel_id=1, source_target_pairs={{0,1},{1,0},{2,3},{3,2},{4,5},{5,4},{6,7},{7,6},{8,9},{9,8},{10,11... | collective-permute-start | bytes 2752520 | tf_op jit(solution)/shard_map/ppermute | solution.py:11
  54.2 75.4 %collective-permute-start.3 = (bf16[128,3584]{1,0:T(8,128)(2,1)}, bf16[128,3584]{1,0:T(8,128)(2,1)}, u32[]{:S(2)}, u32[]{:S(2)}) collective-permute-start(bf16[128,3584]{1,0:T(8,128)(2,1)} %convolution_convert_fusion.8), channel_id=1, source_target_pairs={{0,1},{1,0},{2,3},{3,2},{4,5},{5,4},{6,7},{7,6},{8,9},{9,8},{10,11... | collective-permute-start | bytes 2752520 | tf_op jit(solution)/shard_map/ppermute | solution.py:11
  54.6 16.9 %collective-permute-start.19 = (bf16[128,3584]{1,0:T(8,128)(2,1)S(1)}, bf16[128,3584]{1,0:T(8,128)(2,1)}, u32[]{:S(2)}, u32[]{:S(2)}) collective-permute-start(bf16[128,3584]{1,0:T(8,128)(2,1)S(1)} %collective-permute-done.16), channel_id=1, source_target_pairs={{2,4},{4,6},{3,1},{5,3},{10,12},{12,14},{11,9},{13,11},{18,20},{20... | collective-permute-start | bytes 2752520 | tf_op jit(solution)/shard_map/ppermute | solution.py:16
  56.6 17.3 %collective-permute-start.5 = (bf16[128,3584]{1,0:T(8,128)(2,1)}, bf16[128,3584]{1,0:T(8,128)(2,1)}, u32[]{:S(2)}, u32[]{:S(2)}) collective-permute-start(bf16[128,3584]{1,0:T(8,128)(2,1)} %collective-permute-done.4), channel_id=1, source_target_pairs={{0,1},{1,0},{2,3},{3,2},{4,5},{5,4},{6,7},{7,6},{8,9},{9,8},{10,11... | collective-permute-start | bytes 2752520 | tf_op jit(solution)/shard_map/ppermute | solution.py:11
  68.1 93.1 %collective-permute-start.18 = (bf16[128,3584]{1,0:T(8,128)(2,1)}, bf16[128,3584]{1,0:T(8,128)(2,1)}, u32[]{:S(2)}, u32[]{:S(2)}) collective-permute-start(bf16[128,3584]{1,0:T(8,128)(2,1)} %convolution_convert_fusion.3), channel_id=1, source_target_pairs={{0,1},{1,0},{2,3},{3,2},{4,5},{5,4},{6,7},{7,6},{8,9},{9,8},{10,11... | collective-permute-start | bytes 2752520 | tf_op jit(solution)/shard_map/ppermute | solution.py:11
  68.1 90.4 %collective-permute-start.17 = (bf16[128,3584]{1,0:T(8,128)(2,1)S(1)}, bf16[128,3584]{1,0:T(8,128)(2,1)S(1)}, u32[]{:S(2)}, u32[]{:S(2)}) collective-permute-start(bf16[128,3584]{1,0:T(8,128)(2,1)S(1)} %collective-permute-done.16), channel_id=1, source_target_pairs={{0,1},{1,0},{2,3},{3,2},{4,5},{5,4},{6,7},{7,6},{8,9},{9,8},{10,11... | collective-permute-start | bytes 2752520 | tf_op jit(solution)/shard_map/ppermute | solution.py:11
  71.5 12.5 %collective-permute-start.7 = (bf16[128,3584]{1,0:T(8,128)(2,1)}, bf16[128,3584]{1,0:T(8,128)(2,1)}, u32[]{:S(2)}, u32[]{:S(2)}) collective-permute-start(bf16[128,3584]{1,0:T(8,128)(2,1)} %collective-permute-done.4), channel_id=1, source_target_pairs={{4,6},{3,1},{12,14},{11,9},{20,22},{19,17},{28,30},{27,25}} | collective-permute-start | bytes 2752520 | tf_op jit(solution)/shard_map/ppermute | solution.py:16
  73.8 15.6 %collective-permute-start.20 = (bf16[128,3584]{1,0:T(8,128)(2,1)}, bf16[128,3584]{1,0:T(8,128)(2,1)}, u32[]{:S(2)}, u32[]{:S(2)}) collective-permute-start(bf16[128,3584]{1,0:T(8,128)(2,1)} %collective-permute-done.19), channel_id=1, source_target_pairs={{0,1},{1,0},{2,3},{3,2},{4,5},{5,4},{6,7},{7,6},{8,9},{9,8},{10,11... | collective-permute-start | bytes 2752520 | tf_op jit(solution)/shard_map/ppermute | solution.py:11
  84.0 15.6 %collective-permute-start.22 = (bf16[128,3584]{1,0:T(8,128)(2,1)}, bf16[128,3584]{1,0:T(8,128)(2,1)}, u32[]{:S(2)}, u32[]{:S(2)}) collective-permute-start(bf16[128,3584]{1,0:T(8,128)(2,1)} %collective-permute-done.19), channel_id=1, source_target_pairs={{4,6},{3,1},{12,14},{11,9},{20,22},{19,17},{28,30},{27,25}} | collective-permute-start | bytes 2752520 | tf_op jit(solution)/shard_map/ppermute | solution.py:16
  89.4 10.2 %collective-permute-start.8 = (bf16[128,3584]{1,0:T(8,128)(2,1)}, bf16[128,3584]{1,0:T(8,128)(2,1)}, u32[]{:S(2)}, u32[]{:S(2)}) collective-permute-start(bf16[128,3584]{1,0:T(8,128)(2,1)} %collective-permute-done.7), channel_id=1, source_target_pairs={{0,1},{1,0},{2,3},{3,2},{4,5},{5,4},{6,7},{7,6},{8,9},{9,8},{10,11... | collective-permute-start | bytes 2752520 | tf_op jit(solution)/shard_map/ppermute | solution.py:11
  99.6 22.8 %collective-permute-start.6 = (bf16[128,3584]{1,0:T(8,128)(2,1)}, bf16[128,3584]{1,0:T(8,128)(2,1)}, u32[]{:S(2)}, u32[]{:S(2)}) collective-permute-start(bf16[128,3584]{1,0:T(8,128)(2,1)} %convolution_convert_fusion.7), channel_id=1, source_target_pairs={{0,1},{1,0},{2,3},{3,2},{4,5},{5,4},{6,7},{7,6},{8,9},{9,8},{10,11... | collective-permute-start | bytes 2752520 | tf_op jit(solution)/shard_map/ppermute | solution.py:11
  99.6 9.2 %collective-permute-start.23 = (bf16[128,3584]{1,0:T(8,128)(2,1)}, bf16[128,3584]{1,0:T(8,128)(2,1)}, u32[]{:S(2)}, u32[]{:S(2)}) collective-permute-start(bf16[128,3584]{1,0:T(8,128)(2,1)} %collective-permute-done.22), channel_id=1, source_target_pairs={{0,1},{1,0},{2,3},{3,2},{4,5},{5,4},{6,7},{7,6},{8,9},{9,8},{10,11... | collective-permute-start | bytes 2752520 | tf_op jit(solution)/shard_map/ppermute | solution.py:11
  108.8 8.7 %collective-permute-start.9 = (bf16[128,3584]{1,0:T(8,128)(2,1)}, bf16[128,3584]{1,0:T(8,128)(2,1)}, u32[]{:S(2)}, u32[]{:S(2)}) collective-permute-start(bf16[128,3584]{1,0:T(8,128)(2,1)} %convolution_convert_fusion.6), channel_id=1, source_target_pairs={{0,1},{1,0},{2,3},{3,2},{4,5},{5,4},{6,7},{7,6},{8,9},{9,8},{10,11... | collective-permute-start | bytes 2752520 | tf_op jit(solution)/shard_map/ppermute | solution.py:11
  117.5 2.9 %collective-permute-start.24 = (bf16[128,3584]{1,0:T(8,128)(2,1)}, bf16[128,3584]{1,0:T(8,128)(2,1)S(1)}, u32[]{:S(2)}, u32[]{:S(2)}) collective-permute-start(bf16[128,3584]{1,0:T(8,128)(2,1)} %convolution_convert_fusion.1), channel_id=1, source_target_pairs={{0,1},{1,0},{2,3},{3,2},{4,5},{5,4},{6,7},{7,6},{8,9},{9,8},{10,11... | collective-permute-start | bytes 2752520 | tf_op jit(solution)/shard_map/ppermute | solution.py:11
  120.3 3.1 %collective-permute-start.10 = (bf16[128,3584]{1,0:T(8,128)(2,1)S(1)}, bf16[128,3584]{1,0:T(8,128)(2,1)S(1)}, u32[]{:S(2)}, u32[]{:S(2)}) collective-permute-start(bf16[128,3584]{1,0:T(8,128)(2,1)S(1)} %add_convert_fusion.7), channel_id=1, source_target_pairs={{0,2},{7,5},{8,10},{15,13},{16,18},{23,21},{24,26},{31,29}} | collective-permute-start | bytes 2752520 | tf_op jit(solution)/shard_map/ppermute | solution.py:16
  122.5 3.3 %collective-permute-start.21 = (bf16[128,3584]{1,0:T(8,128)(2,1)S(1)}, bf16[128,3584]{1,0:T(8,128)(2,1)S(1)}, u32[]{:S(2)}, u32[]{:S(2)}) collective-permute-start(bf16[128,3584]{1,0:T(8,128)(2,1)S(1)} %copy-done.4), channel_id=1, source_target_pairs={{0,1},{1,0},{2,3},{3,2},{4,5},{5,4},{6,7},{7,6},{8,9},{9,8},{10,11... | collective-permute-start | bytes 2752520 | tf_op jit(solution)/shard_map/ppermute | solution.py:11
  123.5 3.6 %collective-permute-start.25 = (bf16[128,3584]{1,0:T(8,128)(2,1)S(1)}, bf16[128,3584]{1,0:T(8,128)(2,1)S(1)}, u32[]{:S(2)}, u32[]{:S(2)}) collective-permute-start(bf16[128,3584]{1,0:T(8,128)(2,1)S(1)} %add_convert_fusion.2), channel_id=1, source_target_pairs={{0,2},{7,5},{8,10},{15,13},{16,18},{23,21},{24,26},{31,29}} | collective-permute-start | bytes 2752520 | tf_op jit(solution)/shard_map/ppermute | solution.py:16
  125.7 25.0 %collective-permute-start.11 = (bf16[128,3584]{1,0:T(8,128)(2,1)S(1)}, bf16[128,3584]{1,0:T(8,128)(2,1)}, u32[]{:S(2)}, u32[]{:S(2)}) collective-permute-start(bf16[128,3584]{1,0:T(8,128)(2,1)S(1)} %add_convert_fusion.6), channel_id=1, source_target_pairs={{0,2},{2,4},{5,3},{7,5},{8,10},{10,12},{13,11},{15,13},{16,18},{18... | collective-permute-start | bytes 2752520 | tf_op jit(solution)/shard_map/ppermute | solution.py:16
  128.3 36.3 %collective-permute-start.26 = (bf16[128,3584]{1,0:T(8,128)(2,1)}, bf16[128,3584]{1,0:T(8,128)(2,1)}, u32[]{:S(2)}, u32[]{:S(2)}) collective-permute-start(bf16[128,3584]{1,0:T(8,128)(2,1)} %add_convert_fusion.1), channel_id=1, source_target_pairs={{0,2},{2,4},{5,3},{7,5},{8,10},{10,12},{13,11},{15,13},{16,18},{18... | collective-permute-start | bytes 2752520 | tf_op jit(solution)/shard_map/ppermute | solution.py:16
  156.6 22.6 %collective-permute-start.12 = (bf16[128,3584]{1,0:T(8,128)(2,1)}, bf16[128,3584]{1,0:T(8,128)(2,1)}, u32[]{:S(2)}, u32[]{:S(2)}) collective-permute-start(bf16[128,3584]{1,0:T(8,128)(2,1)} %add_convert_fusion.5), channel_id=1, source_target_pairs={{0,2},{2,4},{4,6},{3,1},{5,3},{7,5},{8,10},{10,12},{12,14},{11,9},... | collective-permute-start | bytes 2752520 | tf_op jit(solution)/shard_map/ppermute | solution.py:16
  161.2 31.8 %copy-start.2 = (bf16[1,2,64,3584]{3,2,1,0:T(8,128)(2,1)S(1)}, bf16[1,2,64,3584]{3,2,1,0:T(8,128)(2,1)}, u32[]{:S(2)}) copy-start(bf16[1,2,64,3584]{3,2,1,0:T(8,128)(2,1)} %param.7) | copy-start | bytes 2752516
  170.5 19.1 %collective-permute-start.27 = (bf16[128,3584]{1,0:T(8,128)(2,1)}, bf16[128,3584]{1,0:T(8,128)(2,1)S(1)}, u32[]{:S(2)}, u32[]{:S(2)}) collective-permute-start(bf16[128,3584]{1,0:T(8,128)(2,1)} %add_convert_fusion), channel_id=1, source_target_pairs={{0,2},{2,4},{4,6},{3,1},{5,3},{7,5},{8,10},{10,12},{12,14},{11,9},... | collective-permute-start | bytes 2752520 | tf_op jit(solution)/shard_map/ppermute | solution.py:16
  180.4 11.1 %collective-permute-start.13 = (bf16[64,3584]{1,0:T(8,128)(2,1)S(1)}, bf16[64,3584]{1,0:T(8,128)(2,1)S(1)}, u32[]{:S(2)}, u32[]{:S(2)}) collective-permute-start(bf16[64,3584]{1,0:T(8,128)(2,1)S(1)} %add_convert_fusion.11), channel_id=1, source_target_pairs={{0,1},{1,0},{2,3},{3,2},{4,5},{5,4},{6,7},{7,6},{8,9},{9,8},{10,11... | collective-permute-start | bytes 1376264 | tf_op jit(solution)/shard_map/ppermute | solution.py:11
  190.7 2.3 %collective-permute-start.28 = (bf16[64,3584]{1,0:T(8,128)(2,1)S(1)}, bf16[64,3584]{1,0:T(8,128)(2,1)S(1)}, u32[]{:S(2)}, u32[]{:S(2)}) collective-permute-start(bf16[64,3584]{1,0:T(8,128)(2,1)S(1)} %add_convert_fusion.10), channel_id=1, source_target_pairs={{0,1},{1,0},{2,3},{3,2},{4,5},{5,4},{6,7},{7,6},{8,9},{9,8},{10,11... | collective-permute-start | bytes 1376264 | tf_op jit(solution)/shard_map/ppermute | solution.py:11
  194.8 14.3 %collective-permute-start.29 = (bf16[64,3584]{1,0:T(8,128)(2,1)S(1)}, bf16[64,3584]{1,0:T(8,128)(2,1)S(1)}, u32[]{:S(2)}, u32[]{:S(2)}) collective-permute-start(bf16[64,3584]{1,0:T(8,128)(2,1)S(1)} %get-tuple-element.10), channel_id=1, source_target_pairs={{0,24},{8,0},{16,8},{24,16},{1,25},{9,1},{17,9},{25,17},{2,26},{10... | collective-permute-start | bytes 1376264 | tf_op jit(solution)/shard_map/ppermute | solution.py:103
  195.4 22.0 %collective-permute-start.14 = (bf16[64,3584]{1,0:T(8,128)(2,1)S(1)}, bf16[64,3584]{1,0:T(8,128)(2,1)S(1)}, u32[]{:S(2)}, u32[]{:S(2)}) collective-permute-start(bf16[64,3584]{1,0:T(8,128)(2,1)S(1)} %get-tuple-element.9), channel_id=1, source_target_pairs={{0,8},{8,16},{16,24},{24,0},{1,9},{9,17},{17,25},{25,1},{2,10},{10... | collective-permute-start | bytes 1376264 | tf_op jit(solution)/shard_map/ppermute | solution.py:103
  (4 other events, 24.1 us)

commit v2 on v1

v2 whole, which is shorter than its diff:
```python
import functools

import jax
import jax.numpy as jnp
from jax import lax
from jax.experimental import pallas as pl
from jax.experimental.pallas import tpu as pltpu
from jax.sharding import PartitionSpec as P

PARTS = 2
TAIL = 128
NO_COST = pl.CostEstimate(flops=1024, bytes_accessed=1024, transcendentals=0)
NEAR = pl.BlockSpec(memory_space=pltpu.VMEM)
ANYWHERE = pl.BlockSpec(memory_space=pl.ANY)
LIMIT = pltpu.CompilerParams(vmem_limit_bytes=16 << 20)


def swap_cores(value):
    count = lax.axis_size("expert")
    return lax.ppermute(value, "expert", [(i, i ^ 1) for i in range(count)])


def hop_pairs(step):
    chips = lax.axis_size("expert") // 2
    up = [(2 * z, 2 * z + 2) for z in range(step, chips - 1)]
    down = [(2 * z + 1, 2 * z - 1) for z in range(1, chips - step)]
    return up + down


def gather_hop(value, step):
    return lax.ppermute(value, "expert", hop_pairs(step))


def reduce_hop(value, step):
    return lax.ppermute(value, "expert", [(target, source) for source, target in hop_pairs(step)])


def near(*values):
    return [pltpu.with_memory_space_constraint(x, pltpu.VMEM) for x in values]


class Order:
    def __init__(self):
        self.before = []

    def call(self, kernel, out_shape, in_specs, operands, out_specs=NEAR, **options):
        before, count = self.before, len(operands)
        result = pl.pallas_call(
            lambda *refs: kernel(*refs[:count], *refs[count + len(before):]),
            out_shape=out_shape,
            in_specs=in_specs + [ANYWHERE] * len(before),
            out_specs=jax.tree.map(lambda _: out_specs, out_shape),
            compiler_params=LIMIT,
            cost_estimate=NO_COST,
            **options,
        )(*operands, *before)
        self.before = [jax.tree.leaves(result)[0]]
        return result

    def wait(self, value):
        return self.call(
            lambda here, out: None,
            jax.ShapeDtypeStruct(value.shape, value.dtype),
            [ANYWHERE],
            [value],
            out_specs=ANYWHERE,
            input_output_aliases={0: 0},
            name="arrived",
        )


def load_kernel(*refs):
    *pairs, sems = refs
    half = len(pairs) // 2
    copies = [pltpu.make_async_copy(pairs[k], pairs[half + k], sems.at[k]) for k in range(half)]
    for copy in copies:
        copy.start()
    for copy in copies:
        copy.wait()


def ffn_kernel(count, *refs):
    blocks, (mask, gate_a, up_a, down_a, gate_b, up_b, down_b), outs = refs[:count], refs[count:count + 7], refs[count + 7:]
    width = gate_a.shape[0]
    half = width // 2
    block = jnp.concatenate([b[...] for b in blocks], axis=0)
    rows = block[:, :width]
    scale = jnp.sum(block[:, width:].astype(jnp.float32) * mask[...], axis=-1, keepdims=True)

    def hidden(gate_w, up_w):
        gate_val = jnp.dot(rows, gate_w[...], preferred_element_type=jnp.float32)
        up_val = jnp.dot(rows, up_w[...], preferred_element_type=jnp.float32)
        return (gate_val / (1.0 + jnp.exp(-gate_val)) * up_val * scale).astype(jnp.bfloat16)

    first, second = hidden(gate_a, up_a), hidden(gate_b, up_b)
    for k in range(2):
        part = pl.ds(k * half, half)
        result = jnp.dot(first, down_a[:, part], preferred_element_type=jnp.float32)
        result += jnp.dot(second, down_b[:, part], preferred_element_type=jnp.float32)
        result = result.astype(jnp.bfloat16)
        start = 0
        for out in outs:
            out[:, part] = result[start:start + out.shape[0]]
            start += out.shape[0]


def sum_kernel(starts, *refs):
    *terms, out = refs
    rows = out.shape[0]
    total = terms[0][pl.ds(starts[0], rows)].astype(jnp.float32)
    for term, start in zip(terms[1:], starts[1:]):
        total += term[pl.ds(start, rows)].astype(jnp.float32)
    out[...] = total.astype(jnp.bfloat16)


def stack_kernel(*refs):
    *parts, out = refs
    start = 0
    for part in parts:
        out[pl.ds(start, part.shape[0])] = part[...]
        start += part.shape[0]


class Device:
    def __init__(self, order, weights, mask):
        self.order, self.weights, self.mask = order, weights, mask

    def load(self):
        own = self.order.call(
            load_kernel,
            [pltpu.VMEM(w.shape, w.dtype) for w in self.weights],
            [ANYWHERE] * len(self.weights),
            [pltpu.with_memory_space_constraint(w, pltpu.HBM) for w in self.weights],
            scratch_shapes=[pltpu.SemaphoreType.DMA((len(self.weights),))],
            name="weights_to_vmem",
        )
        self.weights = (*own, *(swap_cores(w) for w in own))

    def ffn(self, blocks, parts):
        rows = sum(block.shape[0] for block in blocks) // parts
        return self.order.call(
            functools.partial(ffn_kernel, len(blocks)),
            [jax.ShapeDtypeStruct((rows, self.weights[0].shape[0]), jnp.bfloat16)] * parts,
            [NEAR] * (len(blocks) + 7),
            near(*blocks, self.mask, *self.weights),
            name="expert",
        )

    def add(self, *terms, rows=None):
        terms = [term if isinstance(term, tuple) else (term, 0) for term in terms]
        rows = rows or terms[0][0].shape[0]
        return self.order.call(
            functools.partial(sum_kernel, [start for _, start in terms]),
            jax.ShapeDtypeStruct((rows, terms[0][0].shape[1]), jnp.bfloat16),
            [NEAR] * len(terms),
            near(*[term for term, _ in terms]),
            name="sum",
        )

    def stack(self, *parts):
        rows = sum(part.shape[0] for part in parts)
        return self.order.call(
            stack_kernel,
            jax.ShapeDtypeStruct((rows, parts[0].shape[1]), jnp.bfloat16),
            [NEAR] * len(parts),
            near(*parts),
            name="stack",
        )


class Chunk:
    def __init__(self, device, own, state, local, pairs, together):
        self.device, self.own, self.state, self.local, self.pairs = device, own, state, local, pairs
        self.last = lax.axis_size("expert") // 2 - 2
        self.rows = own[0].shape[0] // 2
        self.together = together
        self.moving, self.held, self.partials, self.shifted = {}, [], [], []

    def depart(self, after=True):
        for part, own in enumerate(self.own):
            self.moving[part] = gather_hop(self.device.order.wait(own) if after else own, 0)

    def gather(self, step):
        blocks = []
        for part in range(len(self.own)):
            blocks.append(self.device.order.wait(self.moving[part]))
            if step < self.last:
                self.moving[part] = gather_hop(blocks[part], step + 1)
        self.held.append(blocks)

    def work(self):
        for blocks in self.held:
            self.partials.append(self.device.ffn(blocks, 1 if self.together else len(blocks)))
        self.held = []

    def send_back(self):
        self.sums = [reduce_hop(partial, self.last) for partial in self.partials[self.last]]

    def go_on(self, step):
        for part, value in enumerate(self.sums):
            total = self.device.add(self.partials[step][part], self.device.order.wait(value))
            self.sums[part] = reduce_hop(total, step)

    def finish(self):
        rows = self.rows
        start = 0
        for value in self.sums:
            total = self.device.order.wait(value)
            cuts = range(0, total.shape[0], 2 * rows)
            theirs = swap_cores(jnp.concatenate([total[c + rows:c + 2 * rows] for c in cuts], axis=0))
            mine = jnp.concatenate([total[c:c + rows] for c in cuts], axis=0)
            state = self.state[start:start + mine.shape[0]]
            mixed = self.device.add(state, (self.local[0], self.local[1] + start), mine, theirs)
            self.shifted.append(lax.ppermute(mixed, "pipe", self.pairs))
            start += mine.shape[0]

    def settle(self):
        self.shifted = [self.device.order.wait(value) for value in self.shifted]

    def result(self):
        return jnp.concatenate(self.shifted, axis=0)


def in_parts(value):
    parts = []
    for _ in range(3):
        parts.append(value.astype(jnp.bfloat16))
        value = value - parts[-1].astype(jnp.float32)
    return parts


def body(streams, norm_gain, w_gate, w_up, w_down, routes, gate_weights):
    chips = lax.axis_size("expert") // 2
    sections = lax.axis_size("pipe")
    weights = (w_gate[0, 0], w_up[0, 0], w_down[0, 0])
    tokens = streams.shape[2]
    rows = tokens // PARTS
    named = routes[0][..., None] == jnp.arange(chips, dtype=jnp.int32)
    dense = jnp.sum(jnp.where(named, gate_weights[0][..., None], 0.0), axis=2)
    tail = jnp.concatenate(in_parts(dense), axis=-1)
    tail = jnp.pad(tail, ((0, 0), (0, 0), (0, TAIL - tail.shape[-1])))
    lane = jnp.arange(TAIL)
    mask = ((lane % chips == lax.axis_index("expert") // 2) & (lane < 3 * chips)).astype(jnp.float32)[None]
    wide = streams[0].astype(jnp.float32)
    normed = (
        wide * lax.rsqrt(jnp.mean(wide * wide, axis=-1, keepdims=True) + 1e-06) * norm_gain[0]
    ).astype(jnp.bfloat16)
    sent, mask = lax.optimization_barrier((jnp.concatenate([normed, tail], axis=-1), mask))
    swapped = swap_cores(sent)
    device = Device(Order(), weights, mask)
    own = [
        [device.stack(sent[stream, cut:cut + rows], swapped[stream, cut:cut + rows]) for cut in range(0, tokens, rows)]
        for stream in range(2)
    ]
    chunks = []
    local = []
    for stream in range(2):
        step = 1 if stream == 0 else sections - 1
        pairs = [(source, (source + step) % sections) for source in range(sections)]
        chunks.append(Chunk(device, own[stream], streams[0, stream], None, pairs, together=stream == 0))
    one, two = chunks
    last = one.last
    one.depart(after=False)
    device.load()
    for step in range(last):
        one.gather(step)
    two.depart()
    one.work()
    one.gather(last)
    one.work()
    one.send_back()
    for step in range(last):
        two.gather(step)
        two.work()
        if step == 0:
            (local,) = device.ffn([sent.reshape(-1, sent.shape[-1])], 1)
            one.local, two.local = (local, 0), (local, tokens)
        if step < last - 1 or last == 1:
            one.go_on(last - 1 - step)
    two.gather(last)
    two.work()
    two.send_back()
    one.go_on(0)
    for step in reversed(range(1, last)):
        two.go_on(step)
    one.finish()
    two.go_on(0)
    one.settle()
    two.finish()
    return jnp.stack([one.result(), two.result()])[None]


def solution(mesh):
    return jax.shard_map(
        body,
        mesh=mesh,
        in_specs=(
            P("pipe", None, "expert", None),
            P("pipe", None),
            P("pipe", "expert", None, None),
            P("pipe", "expert", None, None),
            P("pipe", "expert", None, None),
            P("pipe", None, "expert", None),
            P("pipe", None, "expert", None),
        ),
        out_specs=P("pipe", None, "expert", None),
        check_vma=False,
    )
```

time: 222 us -> 148 us (0.67); the launches traced: 218 us -> 147 us
  matrix products: 82.8 us -> 0 us
  Pallas kernels: 0 us -> 28.1 us
  starting transfers between devices: 38.3 us -> 53.9 us
  other arithmetic: 17.7 us -> 4.57 us
  blocking collectives: 12.2 us -> 0 us
  waiting for transfers between devices: 65.9 us -> 59.5 us
    dot_general x20 -> x0, matrix products: 82.8 us -> none  [the longest x10 56.2 us: ffn(): jnp.dot(hidden, down_local, preferred_element_type=jnp.float32)]
    pallas_call x0 -> x45, Pallas kernels: none -> 28.1 us  [call(): pl.pallas_call(lambda *refs: kernel(*refs[:count], *refs[count + len(befo...]
    ppermute x14 -> x24, starting transfers between devices: 29.9 us -> 52.9 us  [the longest x12 35.8 us: gather_hop(): return lax.ppermute(value, 'expert', hop_pairs(step))]
    all_gather x1 -> x0, blocking collectives: 12.2 us -> none  [body(): lax.all_gather(dense, 'expert').reshape(chips, 2, 2, tokens, chips)]
    convert_element_type x8 -> x4, other arithmetic: 11.5 us -> 0.31 us  [the longest x1 0.28 us: body(): normed = (wide * lax.rsqrt(jnp.mean(wide * wide, axis=-1, keepdims=True)...]
    ppermute x14 -> x24, waiting for transfers between devices: 63.8 us -> 52.9 us  [the longest x9 26.4 us: reduce_hop(): lax.ppermute(value, 'expert', [(target, source) for source, target in hop...]
    ppermute x16 -> x7, starting transfers between devices: 8.45 us -> 1 us  [swap_cores(): return lax.ppermute(value, 'expert', [(i, i ^ 1) for i in range(count)])]
    ppermute x16 -> x7, waiting for transfers between devices: 2.12 us -> 6.52 us  [swap_cores(): return lax.ppermute(value, 'expert', [(i, i ^ 1) for i in range(count)])]
  transfers between devices with their start and end apart: 30 -> 31, of which waited for: 10 -> 22; matrix products, arithmetic and copies ran while one was open for 44% -> 0% of each run, Pallas kernels for 0% -> 16%
where the time goes in v2:
time: 148 us; the launch traced here: 147 us
  waiting for transfers between devices  59.5 us (40%)
  starting transfers between devices  53.9 us (36%)
  Pallas kernels  28.1 us (19%)
  other arithmetic  4.57 us (3%)
    ppermute x12, starting transfers between devices, gather_hop(): return lax.ppermute(value, 'expert', hop_pairs(step))  35.8 us
    pallas_call x45, Pallas kernels, call(): pl.pallas_call(lambda *refs: kernel(*refs[:count], *refs[count + len(befo...  28.1 us
    ppermute x9, waiting for transfers between devices, reduce_hop(): lax.ppermute(value, 'expert', [(target, source) for source, target in hop...  26.4 us
    ppermute x9, starting transfers between devices, reduce_hop(): lax.ppermute(value, 'expert', [(target, source) for source, target in hop...  15.4 us
    ppermute x3, waiting for transfers between devices, finish(): self.shifted.append(lax.ppermute(mixed, 'pipe', self.pairs))  14.6 us
    ppermute x12, waiting for transfers between devices, gather_hop(): return lax.ppermute(value, 'expert', hop_pairs(step))  11.9 us
    ppermute x7, waiting for transfers between devices, swap_cores(): return lax.ppermute(value, 'expert', [(i, i ^ 1) for i in range(count)])  6.52 us
  transfers between devices with their start and end apart: 31, of which 22 were waited for; matrix products, arithmetic and copies ran while one was open for 0% of the time, Pallas kernels for 16%

profile of v2, /device:TPU:22, one launch (start us, length us, event | category | flops | bytes accessed | tf_op | source)
XLA Modules:
  0.0 147.3 jit_solution(3014564265314987389)
XLA Ops:
  4.0 2.4 %collective-permute-done = bf16[2,64,3712]{2,1,0:T(8,128)(2,1)S(1)} collective-permute-done((bf16[2,64,3712]{2,1,0:T(8,128)(2,1)S(1)}, bf16[2,64,3712]{2,1,0:T(8,128)(2,1)S(1)}, u32[]{:S(2)}, u32[]{:S(2)}) %collective-permute-start) | collective-permute-done | bytes 950304 | tf_op jit(solution)/shard_map/ppermute | solution.py:20
  6.7 4.2 %weights_to_vmem.1 = (bf16[3584,512]{1,0:T(8,128)(2,1)S(1)}, bf16[3584,512]{1,0:T(8,128)(2,1)S(1)}, bf16[512,3584]{1,0:T(8,128)(2,1)S(1)}) custom-call(bf16[3584,512]{1,0:T(8,128)(2,1)} %bitcast.39, bf16[3584,512]{1,0:T(8,128)(2,1)} %bitcast.40, bf16[512,3584]{1,0:T(8,128)(2,1)} %bitcast.41, bf16[64,3712]{1,0:T(8,128)(2,1)S(1)} %stack.19.refs_3_.refs_0_), custom_call_target="tpu_custom_call" | custom-call | flops 1024 | bytes 1024 | tf_op jit(solution)/shard_map/weights_to_vmem/pallas_call | solution.py:48
  11.7 3.5 %collective-permute-start.5 = (bf16[64,3712]{1,0:T(8,128)(2,1)S(1)}, bf16[64,3712]{1,0:T(8,128)(2,1)S(1)}, u32[]{:S(2)}, u32[]{:S(2)}) collective-permute-start(bf16[64,3712]{1,0:T(8,128)(2,1)S(1)} %stack.16.refs_2_), channel_id=1, source_target_pairs={{0,2},{2,4},{4,6},{3,1},{5,3},{7,5},{8,10},{10,12},{12,14},{11,9},... | collective-permute-start | bytes 1425416 | tf_op jit(solution)/shard_map/ppermute | solution.py:31
  15.1 1.9 %collective-permute-start.4 = (bf16[64,3712]{1,0:T(8,128)(2,1)S(1)}, bf16[64,3712]{1,0:T(8,128)(2,1)S(1)}, u32[]{:S(2)}, u32[]{:S(2)}) collective-permute-start(bf16[64,3712]{1,0:T(8,128)(2,1)S(1)} %stack.17.refs_2_), channel_id=1, source_target_pairs={{0,2},{2,4},{4,6},{3,1},{5,3},{7,5},{8,10},{10,12},{12,14},{11,9},... | collective-permute-start | bytes 1425416 | tf_op jit(solution)/shard_map/ppermute | solution.py:31
  17.1 5.1 %collective-permute-done.5.refs_0_ = bf16[64,3712]{1,0:T(8,128)(2,1)S(1)} collective-permute-done((bf16[64,3712]{1,0:T(8,128)(2,1)S(1)}, bf16[64,3712]{1,0:T(8,128)(2,1)S(1)}, u32[]{:S(2)}, u32[]{:S(2)}) %collective-permute-start.5) | collective-permute-done | bytes 475168 | tf_op jit(solution)/shard_map/ppermute | solution.py:31
  22.2 3.5 %collective-permute-start.7 = (bf16[64,3712]{1,0:T(8,128)(2,1)S(1)}, bf16[64,3712]{1,0:T(8,128)(2,1)S(1)}, u32[]{:S(2)}, u32[]{:S(2)}) collective-permute-start(bf16[64,3712]{1,0:T(8,128)(2,1)S(1)} %arrived.24.refs_1_.refs_0_), channel_id=1, source_target_pairs={{2,4},{4,6},{3,1},{5,3},{10,12},{12,14},{11,9},{13,11},{18,20},{20... | collective-permute-start | bytes 1425416 | tf_op jit(solution)/shard_map/ppermute | solution.py:31
  27.3 3.5 %collective-permute-start.6 = (bf16[64,3712]{1,0:T(8,128)(2,1)S(1)}, bf16[64,3712]{1,0:T(8,128)(2,1)S(1)}, u32[]{:S(2)}, u32[]{:S(2)}) collective-permute-start(bf16[64,3712]{1,0:T(8,128)(2,1)S(1)} %arrived.25.refs_1_), channel_id=1, source_target_pairs={{2,4},{4,6},{3,1},{5,3},{10,12},{12,14},{11,9},{13,11},{18,20},{20... | collective-permute-start | bytes 1425416 | tf_op jit(solution)/shard_map/ppermute | solution.py:31
  30.8 2.0 %collective-permute-done.7.refs_0_ = bf16[64,3712]{1,0:T(8,128)(2,1)S(1)} collective-permute-done((bf16[64,3712]{1,0:T(8,128)(2,1)S(1)}, bf16[64,3712]{1,0:T(8,128)(2,1)S(1)}, u32[]{:S(2)}, u32[]{:S(2)}) %collective-permute-start.7) | collective-permute-done | bytes 475168 | tf_op jit(solution)/shard_map/ppermute | solution.py:31
  32.7 3.5 %collective-permute-start.9 = (bf16[64,3712]{1,0:T(8,128)(2,1)S(1)}, bf16[64,3712]{1,0:T(8,128)(2,1)S(1)}, u32[]{:S(2)}, u32[]{:S(2)}) collective-permute-start(bf16[64,3712]{1,0:T(8,128)(2,1)S(1)} %arrived.26.refs_1_.refs_0_), channel_id=1, source_target_pairs={{4,6},{3,1},{12,14},{11,9},{20,22},{19,17},{28,30},{27,25}} | collective-permute-start | bytes 1425416 | tf_op jit(solution)/shard_map/ppermute | solution.py:31
  37.8 3.5 %collective-permute-start.10 = (bf16[64,3712]{1,0:T(8,128)(2,1)S(1)}, bf16[64,3712]{1,0:T(8,128)(2,1)S(1)}, u32[]{:S(2)}, u32[]{:S(2)}) collective-permute-start(bf16[64,3712]{1,0:T(8,128)(2,1)S(1)} %arrived.27.refs_1_), channel_id=1, source_target_pairs={{4,6},{3,1},{12,14},{11,9},{20,22},{19,17},{28,30},{27,25}} | collective-permute-start | bytes 1425416 | tf_op jit(solution)/shard_map/ppermute | solution.py:31
  41.4 1.9 %collective-permute-start.8 = (bf16[64,3712]{1,0:T(8,128)(2,1)S(1)}, bf16[64,3712]{1,0:T(8,128)(2,1)S(1)}, u32[]{:S(2)}, u32[]{:S(2)}) collective-permute-start(bf16[64,3712]{1,0:T(8,128)(2,1)S(1)} %arrived.28.refs_1_), channel_id=1, source_target_pairs={{0,2},{2,4},{4,6},{3,1},{5,3},{7,5},{8,10},{10,12},{12,14},{11,9},... | collective-permute-start | bytes 1425416 | tf_op jit(solution)/shard_map/ppermute | solution.py:31
  43.3 1.9 %collective-permute-start.11 = (bf16[64,3712]{1,0:T(8,128)(2,1)S(1)}, bf16[64,3712]{1,0:T(8,128)(2,1)S(1)}, u32[]{:S(2)}, u32[]{:S(2)}) collective-permute-start(bf16[64,3712]{1,0:T(8,128)(2,1)S(1)} %arrived.29.refs_9_), channel_id=1, source_target_pairs={{0,2},{2,4},{4,6},{3,1},{5,3},{7,5},{8,10},{10,12},{12,14},{11,9},... | collective-permute-start | bytes 1425416 | tf_op jit(solution)/shard_map/ppermute | solution.py:31
  45.2 3.2 %expert.7.refs_9_.refs_0_ = bf16[128,3584]{1,0:T(8,128)(2,1)S(1)} custom-call(bf16[64,3712]{1,0:T(8,128)(2,1)S(1)} %arrived.24.refs_1_.refs_0_, bf16[64,3712]{1,0:T(8,128)(2,1)S(1)} %arrived.25.refs_1_, f32[1,128]{1,0:T(1,128)S(1)} %and_convert_fusion.refs_2_.refs_1_, bf16[3584,512]{1,0:T(8,128)(2,1)S(1)} %get-tuple-element.18.refs_1_.refs_3_.refs_2_, ...), custom_call_target="tpu_custom_call" | custom-call | flops 1024 | bytes 1024 | tf_op jit(solution)/shard_map/expert/pallas_call | solution.py:48
  48.4 3.2 %expert.8.refs_1_.refs_0_ = bf16[128,3584]{1,0:T(8,128)(2,1)S(1)} custom-call(bf16[64,3712]{1,0:T(8,128)(2,1)S(1)} %arrived.26.refs_1_.refs_0_, bf16[64,3712]{1,0:T(8,128)(2,1)S(1)} %arrived.27.refs_1_, f32[1,128]{1,0:T(1,128)S(1)} %and_convert_fusion.refs_2_.refs_1_, bf16[3584,512]{1,0:T(8,128)(2,1)S(1)} %get-tuple-element.18.refs_1_.refs_3_.refs_2_, ...), custom_call_target="tpu_custom_call" | custom-call | flops 1024 | bytes 1024 | tf_op jit(solution)/shard_map/expert/pallas_call | solution.py:48
  51.7 3.2 %expert.9.refs_1_ = bf16[128,3584]{1,0:T(8,128)(2,1)S(1)} custom-call(bf16[64,3712]{1,0:T(8,128)(2,1)S(1)} %arrived.30.refs_1_.refs_0_, bf16[64,3712]{1,0:T(8,128)(2,1)S(1)} %arrived.31.refs_1_.refs_9_, f32[1,128]{1,0:T(1,128)S(1)} %and_convert_fusion.refs_2_.refs_1_, bf16[3584,512]{1,0:T(8,128)(2,1)S(1)} %get-tuple-element.18.refs_1_.refs_3_.refs_2_, ...), custom_call_target="tpu_custom_call" | custom-call | flops 1024 | bytes 1024 | tf_op jit(solution)/shard_map/expert/pallas_call | solution.py:48
  56.2 4.6 %collective-permute-start.14 = (bf16[64,3712]{1,0:T(8,128)(2,1)S(1)}, bf16[64,3712]{1,0:T(8,128)(2,1)S(1)}, u32[]{:S(2)}, u32[]{:S(2)}) collective-permute-start(bf16[64,3712]{1,0:T(8,128)(2,1)S(1)} %arrived.32.refs_1_.refs_0_), channel_id=1, source_target_pairs={{2,4},{4,6},{3,1},{5,3},{10,12},{12,14},{11,9},{13,11},{18,20},{20... | collective-permute-start | bytes 1425416 | tf_op jit(solution)/shard_map/ppermute | solution.py:31
  60.9 2.1 %collective-permute-start.16 = (bf16[64,3712]{1,0:T(8,128)(2,1)S(1)}, bf16[64,3712]{1,0:T(8,128)(2,1)S(1)}, u32[]{:S(2)}, u32[]{:S(2)}) collective-permute-start(bf16[64,3712]{1,0:T(8,128)(2,1)S(1)} %arrived.33.refs_1_.refs_9_), channel_id=1, source_target_pairs={{2,4},{4,6},{3,1},{5,3},{10,12},{12,14},{11,9},{13,11},{18,20},{20... | collective-permute-start | bytes 1425416 | tf_op jit(solution)/shard_map/ppermute | solution.py:31
  63.0 3.2 %expert.10 = (bf16[64,3584]{1,0:T(8,128)(2,1)S(1)}, bf16[64,3584]{1,0:T(8,128)(2,1)S(1)}) custom-call(bf16[64,3712]{1,0:T(8,128)(2,1)S(1)} %arrived.32.refs_1_.refs_0_, bf16[64,3712]{1,0:T(8,128)(2,1)S(1)} %arrived.33.refs_1_.refs_9_, f32[1,128]{1,0:T(1,128)S(1)} %and_convert_fusion.refs_2_.refs_1_, ...), custom_call_target="tpu_custom_call" | custom-call | flops 1024 | bytes 1024 | tf_op jit(solution)/shard_map/expert/pallas_call | solution.py:48
  66.2 3.2 %expert.11.refs_1_ = bf16[128,3584]{1,0:T(8,128)(2,1)S(1)} custom-call(bf16[128,3712]{1,0:T(8,128)(2,1)S(1)} %bitcast.37, f32[1,128]{1,0:T(1,128)S(1)} %and_convert_fusion.refs_2_.refs_1_, bf16[3584,512]{1,0:T(8,128)(2,1)S(1)} %get-tuple-element.18.refs_1_.refs_3_.refs_2_, bf16[3584,512]{1,0:T(8,128)(2,1)S(1)} %get-tuple-element.19.refs_4_.refs_3_, ...), custom_call_target="tpu_custom_call" | custom-call | flops 1024 | bytes 1024 | tf_op jit(solution)/shard_map/expert/pallas_call | solution.py:48
  72.1 4.4 %collective-permute-start.17 = (bf16[64,3712]{1,0:T(8,128)(2,1)S(1)}, bf16[64,3712]{1,0:T(8,128)(2,1)S(1)}, u32[]{:S(2)}, u32[]{:S(2)}) collective-permute-start(bf16[64,3712]{1,0:T(8,128)(2,1)S(1)} %arrived.36.refs_1_.refs_9_), channel_id=1, source_target_pairs={{4,6},{3,1},{12,14},{11,9},{20,22},{19,17},{28,30},{27,25}} | collective-permute-start | bytes 1425416 | tf_op jit(solution)/shard_map/ppermute | solution.py:31
  78.4 3.2 %expert.12 = (bf16[64,3584]{1,0:T(8,128)(2,1)S(1)}, bf16[64,3584]{1,0:T(8,128)(2,1)S(1)}) custom-call(bf16[64,3712]{1,0:T(8,128)(2,1)S(1)} %arrived.35.refs_1_.refs_0_, bf16[64,3712]{1,0:T(8,128)(2,1)S(1)} %arrived.36.refs_1_.refs_9_, f32[1,128]{1,0:T(1,128)S(1)} %and_convert_fusion.refs_2_.refs_1_, ...), custom_call_target="tpu_custom_call" | custom-call | flops 1024 | bytes 1024 | tf_op jit(solution)/shard_map/expert/pallas_call | solution.py:48
  83.2 3.2 %expert.13 = (bf16[64,3584]{1,0:T(8,128)(2,1)S(1)}, bf16[64,3584]{1,0:T(8,128)(2,1)S(1)}) custom-call(bf16[64,3712]{1,0:T(8,128)(2,1)S(1)} %arrived.37.refs_1_.refs_0_, bf16[64,3712]{1,0:T(8,128)(2,1)S(1)} %arrived.38.refs_1_.refs_9_, f32[1,128]{1,0:T(1,128)S(1)} %and_convert_fusion.refs_2_.refs_1_, ...), custom_call_target="tpu_custom_call" | custom-call | flops 1024 | bytes 1024 | tf_op jit(solution)/shard_map/expert/pallas_call | solution.py:48
  87.7 4.1 %collective-permute-done.13.refs_0_ = bf16[128,3584]{1,0:T(8,128)(2,1)S(1)} collective-permute-done((bf16[128,3584]{1,0:T(8,128)(2,1)S(1)}, bf16[128,3584]{1,0:T(8,128)(2,1)S(1)}, u32[]{:S(2)}, u32[]{:S(2)}) %collective-permute-start.13) | collective-permute-done | bytes 917536 | tf_op jit(solution)/shard_map/ppermute | solution.py:35
  98.8 3.4 %collective-permute-done.19.refs_0_ = bf16[64,3584]{1,0:T(8,128)(2,1)S(1)} collective-permute-done((bf16[64,3584]{1,0:T(8,128)(2,1)S(1)}, bf16[64,3584]{1,0:T(8,128)(2,1)S(1)}, u32[]{:S(2)}, u32[]{:S(2)}) %collective-permute-start.19) | collective-permute-done | bytes 458784 | tf_op jit(solution)/shard_map/ppermute | solution.py:35
  102.3 1.9 %collective-permute-start.23 = (bf16[64,3584]{1,0:T(8,128)(2,1)S(1)}, bf16[64,3584]{1,0:T(8,128)(2,1)S(1)}, u32[]{:S(2)}, u32[]{:S(2)}) collective-permute-start(bf16[64,3584]{1,0:T(8,128)(2,1)S(1)} %sum.12.refs_1_), channel_id=1, source_target_pairs={{4,2},{6,4},{1,3},{3,5},{12,10},{14,12},{9,11},{11,13},{20,18},{22... | collective-permute-start | bytes 1376264 | tf_op jit(solution)/shard_map/ppermute | solution.py:35
  104.2 7.8 %collective-permute-done.18.refs_0_ = bf16[128,3584]{1,0:T(8,128)(2,1)S(1)} collective-permute-done((bf16[128,3584]{1,0:T(8,128)(2,1)S(1)}, bf16[128,3584]{1,0:T(8,128)(2,1)S(1)}, u32[]{:S(2)}, u32[]{:S(2)}) %collective-permute-start.18) | collective-permute-done | bytes 917536 | tf_op jit(solution)/shard_map/ppermute | solution.py:35
  114.7 2.2 %collective-permute-done.24.refs_0_ = bf16[64,3584]{1,0:T(8,128)(2,1)S(1)} collective-permute-done((bf16[64,3584]{1,0:T(8,128)(2,1)S(1)}, bf16[64,3584]{1,0:T(8,128)(2,1)S(1)}, u32[]{:S(2)}, u32[]{:S(2)}) %collective-permute-start.24) | collective-permute-done | bytes 458784 | tf_op jit(solution)/shard_map/ppermute | solution.py:35
  119.0 2.9 %collective-permute-done.23.refs_0_ = bf16[64,3584]{1,0:T(8,128)(2,1)S(1)} collective-permute-done((bf16[64,3584]{1,0:T(8,128)(2,1)S(1)}, bf16[64,3584]{1,0:T(8,128)(2,1)S(1)}, u32[]{:S(2)}, u32[]{:S(2)}) %collective-permute-start.23) | collective-permute-done | bytes 458784 | tf_op jit(solution)/shard_map/ppermute | solution.py:35
  123.9 3.0 %collective-permute-done.22.refs_0_ = bf16[64,3584]{1,0:T(8,128)(2,1)S(1)} collective-permute-done((bf16[64,3584]{1,0:T(8,128)(2,1)S(1)}, bf16[64,3584]{1,0:T(8,128)(2,1)S(1)}, u32[]{:S(2)}, u32[]{:S(2)}) %collective-permute-start.22) | collective-permute-done | bytes 458784 | tf_op jit(solution)/shard_map/ppermute | solution.py:214
  129.1 3.2 %collective-permute-done.28.refs_0_ = bf16[64,3584]{1,0:T(8,128)(2,1)S(1)} collective-permute-done((bf16[64,3584]{1,0:T(8,128)(2,1)S(1)}, bf16[64,3584]{1,0:T(8,128)(2,1)S(1)}, u32[]{:S(2)}, u32[]{:S(2)}) %collective-permute-start.28) | collective-permute-done | bytes 458784 | tf_op jit(solution)/shard_map/ppermute | solution.py:35
  134.6 7.2 %collective-permute-done.27 = bf16[32,3584]{1,0:T(8,128)(2,1)S(1)} collective-permute-done((bf16[32,3584]{1,0:T(8,128)(2,1)S(1)}, bf16[32,3584]{1,0:T(8,128)(2,1)S(1)}, u32[]{:S(2)}, u32[]{:S(2)}) %collective-permute-start.27) | collective-permute-done | bytes 229408 | tf_op jit(solution)/shard_map/ppermute | solution.py:214
  141.8 4.5 %collective-permute-done.30 = bf16[32,3584]{1,0:T(8,128)(2,1)S(1)} collective-permute-done((bf16[32,3584]{1,0:T(8,128)(2,1)S(1)}, bf16[32,3584]{1,0:T(8,128)(2,1)S(1)}, u32[]{:S(2)}, u32[]{:S(2)}) %collective-permute-start.30) | collective-permute-done | bytes 229408 | tf_op jit(solution)/shard_map/ppermute | solution.py:214
  (101 shorter events, 36.2 us)
Async XLA Ops:
  0.0 3.4 %copy-start = (bf16[1,2,64,3584]{3,2,1,0:T(8,128)(2,1)S(1)}, bf16[1,2,64,3584]{3,2,1,0:T(8,128)(2,1)}, u32[]{:S(2)}) copy-start(bf16[1,2,64,3584]{3,2,1,0:T(8,128)(2,1)} %param.7) | copy-start | bytes 2752516
  3.9 2.6 %collective-permute-start = (bf16[2,64,3712]{2,1,0:T(8,128)(2,1)S(1)}, bf16[2,64,3712]{2,1,0:T(8,128)(2,1)S(1)}, u32[]{:S(2)}, u32[]{:S(2)}) collective-permute-start(bf16[2,64,3712]{2,1,0:T(8,128)(2,1)S(1)} %pad_maximum_fusion), channel_id=1, source_target_pairs={{0,1},{1,0},{2,3},{3,2},{4,5},{5,4},{6,7},{7,6},{8,9},{9,8},{10,11... | collective-permute-start | bytes 2850824 | tf_op jit(solution)/shard_map/ppermute | solution.py:20
  10.9 30.4 %collective-permute-start.1 = (bf16[3584,512]{1,0:T(8,128)(2,1)S(1)}, bf16[3584,512]{1,0:T(8,128)(2,1)S(1)}, u32[]{:S(2)}, u32[]{:S(2)}) collective-permute-start(bf16[3584,512]{1,0:T(8,128)(2,1)S(1)} %get-tuple-element.18.refs_1_.refs_3_.refs_2_), channel_id=1, source_target_pairs={{0,1},{1,0},{2,3},{3,2},{4,5},{5,4},{6,7},{7,6},{8,9},{9,8},{10,11... | collective-permute-start | bytes 11010056 | tf_op jit(solution)/shard_map/ppermute | solution.py:20
  11.1 32.1 %collective-permute-start.2 = (bf16[3584,512]{1,0:T(8,128)(2,1)S(1)}, bf16[3584,512]{1,0:T(8,128)(2,1)S(1)}, u32[]{:S(2)}, u32[]{:S(2)}) collective-permute-start(bf16[3584,512]{1,0:T(8,128)(2,1)S(1)} %get-tuple-element.19.refs_4_.refs_3_), channel_id=1, source_target_pairs={{0,1},{1,0},{2,3},{3,2},{4,5},{5,4},{6,7},{7,6},{8,9},{9,8},{10,11... | collective-permute-start | bytes 11010056 | tf_op jit(solution)/shard_map/ppermute | solution.py:20
  11.5 33.7 %collective-permute-start.3 = (bf16[512,3584]{1,0:T(8,128)(2,1)S(1)}, bf16[512,3584]{1,0:T(8,128)(2,1)S(1)}, u32[]{:S(2)}, u32[]{:S(2)}) collective-permute-start(bf16[512,3584]{1,0:T(8,128)(2,1)S(1)} %get-tuple-element.20.refs_5_.refs_4_), channel_id=1, source_target_pairs={{0,1},{1,0},{2,3},{3,2},{4,5},{5,4},{6,7},{7,6},{8,9},{9,8},{10,11... | collective-permute-start | bytes 11010056 | tf_op jit(solution)/shard_map/ppermute | solution.py:20
  11.7 10.5 %collective-permute-start.5 = (bf16[64,3712]{1,0:T(8,128)(2,1)S(1)}, bf16[64,3712]{1,0:T(8,128)(2,1)S(1)}, u32[]{:S(2)}, u32[]{:S(2)}) collective-permute-start(bf16[64,3712]{1,0:T(8,128)(2,1)S(1)} %stack.16.refs_2_), channel_id=1, source_target_pairs={{0,2},{2,4},{4,6},{3,1},{5,3},{7,5},{8,10},{10,12},{12,14},{11,9},... | collective-permute-start | bytes 1425416 | tf_op jit(solution)/shard_map/ppermute | solution.py:31
  15.1 12.1 %collective-permute-start.4 = (bf16[64,3712]{1,0:T(8,128)(2,1)S(1)}, bf16[64,3712]{1,0:T(8,128)(2,1)S(1)}, u32[]{:S(2)}, u32[]{:S(2)}) collective-permute-start(bf16[64,3712]{1,0:T(8,128)(2,1)S(1)} %stack.17.refs_2_), channel_id=1, source_target_pairs={{0,2},{2,4},{4,6},{3,1},{5,3},{7,5},{8,10},{10,12},{12,14},{11,9},... | collective-permute-start | bytes 1425416 | tf_op jit(solution)/shard_map/ppermute | solution.py:31
  22.2 10.5 %collective-permute-start.7 = (bf16[64,3712]{1,0:T(8,128)(2,1)S(1)}, bf16[64,3712]{1,0:T(8,128)(2,1)S(1)}, u32[]{:S(2)}, u32[]{:S(2)}) collective-permute-start(bf16[64,3712]{1,0:T(8,128)(2,1)S(1)} %arrived.24.refs_1_.refs_0_), channel_id=1, source_target_pairs={{2,4},{4,6},{3,1},{5,3},{10,12},{12,14},{11,9},{13,11},{18,20},{20... | collective-permute-start | bytes 1425416 | tf_op jit(solution)/shard_map/ppermute | solution.py:31
  27.3 10.5 %collective-permute-start.6 = (bf16[64,3712]{1,0:T(8,128)(2,1)S(1)}, bf16[64,3712]{1,0:T(8,128)(2,1)S(1)}, u32[]{:S(2)}, u32[]{:S(2)}) collective-permute-start(bf16[64,3712]{1,0:T(8,128)(2,1)S(1)} %arrived.25.refs_1_), channel_id=1, source_target_pairs={{2,4},{4,6},{3,1},{5,3},{10,12},{12,14},{11,9},{13,11},{18,20},{20... | collective-permute-start | bytes 1425416 | tf_op jit(solution)/shard_map/ppermute | solution.py:31
  32.7 18.9 %collective-permute-start.9 = (bf16[64,3712]{1,0:T(8,128)(2,1)S(1)}, bf16[64,3712]{1,0:T(8,128)(2,1)S(1)}, u32[]{:S(2)}, u32[]{:S(2)}) collective-permute-start(bf16[64,3712]{1,0:T(8,128)(2,1)S(1)} %arrived.26.refs_1_.refs_0_), channel_id=1, source_target_pairs={{4,6},{3,1},{12,14},{11,9},{20,22},{19,17},{28,30},{27,25}} | collective-permute-start | bytes 1425416 | tf_op jit(solution)/shard_map/ppermute | solution.py:31
  37.8 13.9 %collective-permute-start.10 = (bf16[64,3712]{1,0:T(8,128)(2,1)S(1)}, bf16[64,3712]{1,0:T(8,128)(2,1)S(1)}, u32[]{:S(2)}, u32[]{:S(2)}) collective-permute-start(bf16[64,3712]{1,0:T(8,128)(2,1)S(1)} %arrived.27.refs_1_), channel_id=1, source_target_pairs={{4,6},{3,1},{12,14},{11,9},{20,22},{19,17},{28,30},{27,25}} | collective-permute-start | bytes 1425416 | tf_op jit(solution)/shard_map/ppermute | solution.py:31
  41.4 14.9 %collective-permute-start.8 = (bf16[64,3712]{1,0:T(8,128)(2,1)S(1)}, bf16[64,3712]{1,0:T(8,128)(2,1)S(1)}, u32[]{:S(2)}, u32[]{:S(2)}) collective-permute-start(bf16[64,3712]{1,0:T(8,128)(2,1)S(1)} %arrived.28.refs_1_), channel_id=1, source_target_pairs={{0,2},{2,4},{4,6},{3,1},{5,3},{7,5},{8,10},{10,12},{12,14},{11,9},... | collective-permute-start | bytes 1425416 | tf_op jit(solution)/shard_map/ppermute | solution.py:31
  43.3 17.6 %collective-permute-start.11 = (bf16[64,3712]{1,0:T(8,128)(2,1)S(1)}, bf16[64,3712]{1,0:T(8,128)(2,1)S(1)}, u32[]{:S(2)}, u32[]{:S(2)}) collective-permute-start(bf16[64,3712]{1,0:T(8,128)(2,1)S(1)} %arrived.29.refs_9_), channel_id=1, source_target_pairs={{0,2},{2,4},{4,6},{3,1},{5,3},{7,5},{8,10},{10,12},{12,14},{11,9},... | collective-permute-start | bytes 1425416 | tf_op jit(solution)/shard_map/ppermute | solution.py:31
  54.9 15.3 %collective-permute-start.12 = (bf16[128,3584]{1,0:T(8,128)(2,1)S(1)}, bf16[128,3584]{1,0:T(8,128)(2,1)S(1)}, u32[]{:S(2)}, u32[]{:S(2)}) collective-permute-start(bf16[128,3584]{1,0:T(8,128)(2,1)S(1)} %expert.9.refs_1_), channel_id=1, source_target_pairs={{6,4},{1,3},{14,12},{9,11},{22,20},{17,19},{30,28},{25,27}} | collective-permute-start | bytes 2752520 | tf_op jit(solution)/shard_map/ppermute | solution.py:35
  56.2 14.2 %collective-permute-start.14 = (bf16[64,3712]{1,0:T(8,128)(2,1)S(1)}, bf16[64,3712]{1,0:T(8,128)(2,1)S(1)}, u32[]{:S(2)}, u32[]{:S(2)}) collective-permute-start(bf16[64,3712]{1,0:T(8,128)(2,1)S(1)} %arrived.32.refs_1_.refs_0_), channel_id=1, source_target_pairs={{2,4},{4,6},{3,1},{5,3},{10,12},{12,14},{11,9},{13,11},{18,20},{20... | collective-permute-start | bytes 1425416 | tf_op jit(solution)/shard_map/ppermute | solution.py:31
  60.9 11.2 %collective-permute-start.16 = (bf16[64,3712]{1,0:T(8,128)(2,1)S(1)}, bf16[64,3712]{1,0:T(8,128)(2,1)S(1)}, u32[]{:S(2)}, u32[]{:S(2)}) collective-permute-start(bf16[64,3712]{1,0:T(8,128)(2,1)S(1)} %arrived.33.refs_1_.refs_9_), channel_id=1, source_target_pairs={{2,4},{4,6},{3,1},{5,3},{10,12},{12,14},{11,9},{13,11},{18,20},{20... | collective-permute-start | bytes 1425416 | tf_op jit(solution)/shard_map/ppermute | solution.py:31
  70.4 11.2 %collective-permute-start.15 = (bf16[64,3712]{1,0:T(8,128)(2,1)S(1)}, bf16[64,3712]{1,0:T(8,128)(2,1)S(1)}, u32[]{:S(2)}, u32[]{:S(2)}) collective-permute-start(bf16[64,3712]{1,0:T(8,128)(2,1)S(1)} %arrived.35.refs_1_.refs_0_), channel_id=1, source_target_pairs={{4,6},{3,1},{12,14},{11,9},{20,22},{19,17},{28,30},{27,25}} | collective-permute-start | bytes 1425416 | tf_op jit(solution)/shard_map/ppermute | solution.py:31
  72.1 11.0 %collective-permute-start.17 = (bf16[64,3712]{1,0:T(8,128)(2,1)S(1)}, bf16[64,3712]{1,0:T(8,128)(2,1)S(1)}, u32[]{:S(2)}, u32[]{:S(2)}) collective-permute-start(bf16[64,3712]{1,0:T(8,128)(2,1)S(1)} %arrived.36.refs_1_.refs_9_), channel_id=1, source_target_pairs={{4,6},{3,1},{12,14},{11,9},{20,22},{19,17},{28,30},{27,25}} | collective-permute-start | bytes 1425416 | tf_op jit(solution)/shard_map/ppermute | solution.py:31
  76.5 15.3 %collective-permute-start.13 = (bf16[128,3584]{1,0:T(8,128)(2,1)S(1)}, bf16[128,3584]{1,0:T(8,128)(2,1)S(1)}, u32[]{:S(2)}, u32[]{:S(2)}) collective-permute-start(bf16[128,3584]{1,0:T(8,128)(2,1)S(1)} %sum.9.refs_1_), channel_id=1, source_target_pairs={{4,2},{6,4},{1,3},{3,5},{12,10},{14,12},{9,11},{11,13},{20,18},{22... | collective-permute-start | bytes 2752520 | tf_op jit(solution)/shard_map/ppermute | solution.py:35
  86.4 10.4 %collective-permute-start.20 = (bf16[64,3584]{1,0:T(8,128)(2,1)S(1)}, bf16[64,3584]{1,0:T(8,128)(2,1)S(1)}, u32[]{:S(2)}, u32[]{:S(2)}) collective-permute-start(bf16[64,3584]{1,0:T(8,128)(2,1)S(1)} %get-tuple-element.23.refs_1_), channel_id=1, source_target_pairs={{6,4},{1,3},{14,12},{9,11},{22,20},{17,19},{30,28},{25,27}} | collective-permute-start | bytes 1376264 | tf_op jit(solution)/shard_map/ppermute | solution.py:35
  91.8 10.4 %collective-permute-start.19 = (bf16[64,3584]{1,0:T(8,128)(2,1)S(1)}, bf16[64,3584]{1,0:T(8,128)(2,1)S(1)}, u32[]{:S(2)}, u32[]{:S(2)}) collective-permute-start(bf16[64,3584]{1,0:T(8,128)(2,1)S(1)} %get-tuple-element.25), channel_id=1, source_target_pairs={{6,4},{1,3},{14,12},{9,11},{22,20},{17,19},{30,28},{25,27}} | collective-permute-start | bytes 1376264 | tf_op jit(solution)/shard_map/ppermute | solution.py:35
  93.3 18.7 %collective-permute-start.18 = (bf16[128,3584]{1,0:T(8,128)(2,1)S(1)}, bf16[128,3584]{1,0:T(8,128)(2,1)S(1)}, u32[]{:S(2)}, u32[]{:S(2)}) collective-permute-start(bf16[128,3584]{1,0:T(8,128)(2,1)S(1)} %sum.10.refs_1_), channel_id=1, source_target_pairs={{2,0},{4,2},{6,4},{1,3},{3,5},{5,7},{10,8},{12,10},{14,12},{9,11},... | collective-permute-start | bytes 2752520 | tf_op jit(solution)/shard_map/ppermute | solution.py:35
  96.9 20.0 %collective-permute-start.24 = (bf16[64,3584]{1,0:T(8,128)(2,1)S(1)}, bf16[64,3584]{1,0:T(8,128)(2,1)S(1)}, u32[]{:S(2)}, u32[]{:S(2)}) collective-permute-start(bf16[64,3584]{1,0:T(8,128)(2,1)S(1)} %sum.11.refs_1_), channel_id=1, source_target_pairs={{4,2},{6,4},{1,3},{3,5},{12,10},{14,12},{9,11},{11,13},{20,18},{22... | collective-permute-start | bytes 1376264 | tf_op jit(solution)/shard_map/ppermute | solution.py:35
  102.3 19.6 %collective-permute-start.23 = (bf16[64,3584]{1,0:T(8,128)(2,1)S(1)}, bf16[64,3584]{1,0:T(8,128)(2,1)S(1)}, u32[]{:S(2)}, u32[]{:S(2)}) collective-permute-start(bf16[64,3584]{1,0:T(8,128)(2,1)S(1)} %sum.12.refs_1_), channel_id=1, source_target_pairs={{4,2},{6,4},{1,3},{3,5},{12,10},{14,12},{9,11},{11,13},{20,18},{22... | collective-permute-start | bytes 1376264 | tf_op jit(solution)/shard_map/ppermute | solution.py:35
  112.1 1.9 %collective-permute-start.21 = (bf16[64,3584]{1,0:T(8,128)(2,1)S(1)}, bf16[64,3584]{1,0:T(8,128)(2,1)S(1)}, u32[]{:S(2)}, u32[]{:S(2)}) collective-permute-start(bf16[64,3584]{1,0:T(8,128)(2,1)S(1)} %pad_maximum_fusion.2), channel_id=1, source_target_pairs={{0,1},{1,0},{2,3},{3,2},{4,5},{5,4},{6,7},{7,6},{8,9},{9,8},{10,11... | collective-permute-start | bytes 1376264 | tf_op jit(solution)/shard_map/ppermute | solution.py:20
  114.2 12.6 %collective-permute-start.22 = (bf16[64,3584]{1,0:T(8,128)(2,1)S(1)}, bf16[64,3584]{1,0:T(8,128)(2,1)S(1)}, u32[]{:S(2)}, u32[]{:S(2)}) collective-permute-start(bf16[64,3584]{1,0:T(8,128)(2,1)S(1)} %sum.13.refs_1_), channel_id=1, source_target_pairs={{0,8},{8,16},{16,24},{24,0},{1,9},{9,17},{17,25},{25,1},{2,10},{10... | collective-permute-start | bytes 1376264 | tf_op jit(solution)/shard_map/ppermute | solution.py:214
  117.0 10.4 %collective-permute-start.25 = (bf16[64,3584]{1,0:T(8,128)(2,1)S(1)}, bf16[64,3584]{1,0:T(8,128)(2,1)S(1)}, u32[]{:S(2)}, u32[]{:S(2)}) collective-permute-start(bf16[64,3584]{1,0:T(8,128)(2,1)S(1)} %sum.14.refs_1_), channel_id=1, source_target_pairs={{2,0},{4,2},{6,4},{1,3},{3,5},{5,7},{10,8},{12,10},{14,12},{9,11},... | collective-permute-start | bytes 1376264 | tf_op jit(solution)/shard_map/ppermute | solution.py:35
  121.9 10.4 %collective-permute-start.28 = (bf16[64,3584]{1,0:T(8,128)(2,1)S(1)}, bf16[64,3584]{1,0:T(8,128)(2,1)S(1)}, u32[]{:S(2)}, u32[]{:S(2)}) collective-permute-start(bf16[64,3584]{1,0:T(8,128)(2,1)S(1)} %sum.15.refs_1_), channel_id=1, source_target_pairs={{2,0},{4,2},{6,4},{1,3},{3,5},{5,7},{10,8},{12,10},{14,12},{9,11},... | collective-permute-start | bytes 1376264 | tf_op jit(solution)/shard_map/ppermute | solution.py:35
  127.4 1.6 %collective-permute-start.26 = (bf16[32,3584]{1,0:T(8,128)(2,1)S(1)}, bf16[32,3584]{1,0:T(8,128)(2,1)S(1)}, u32[]{:S(2)}, u32[]{:S(2)}) collective-permute-start(bf16[32,3584]{1,0:T(8,128)(2,1)S(1)} %get-tuple-element.43), channel_id=1, source_target_pairs={{0,1},{1,0},{2,3},{3,2},{4,5},{5,4},{6,7},{7,6},{8,9},{9,8},{10,11... | collective-permute-start | bytes 688136 | tf_op jit(solution)/shard_map/ppermute | solution.py:20
  132.3 1.6 %collective-permute-start.29 = (bf16[32,3584]{1,0:T(8,128)(2,1)S(1)}, bf16[32,3584]{1,0:T(8,128)(2,1)S(1)}, u32[]{:S(2)}, u32[]{:S(2)}) collective-permute-start(bf16[32,3584]{1,0:T(8,128)(2,1)S(1)} %get-tuple-element.41), channel_id=1, source_target_pairs={{0,1},{1,0},{2,3},{3,2},{4,5},{5,4},{6,7},{7,6},{8,9},{9,8},{10,11... | collective-permute-start | bytes 688136 | tf_op jit(solution)/shard_map/ppermute | solution.py:20
  132.4 9.4 %collective-permute-start.27 = (bf16[32,3584]{1,0:T(8,128)(2,1)S(1)}, bf16[32,3584]{1,0:T(8,128)(2,1)S(1)}, u32[]{:S(2)}, u32[]{:S(2)}) collective-permute-start(bf16[32,3584]{1,0:T(8,128)(2,1)S(1)} %sum.16.refs_1_), channel_id=1, source_target_pairs={{0,24},{8,0},{16,8},{24,16},{1,25},{9,1},{17,9},{25,17},{2,26},{10... | collective-permute-start | bytes 688136 | tf_op jit(solution)/shard_map/ppermute | solution.py:214
  134.0 12.2 %collective-permute-start.30 = (bf16[32,3584]{1,0:T(8,128)(2,1)S(1)}, bf16[32,3584]{1,0:T(8,128)(2,1)S(1)}, u32[]{:S(2)}, u32[]{:S(2)}) collective-permute-start(bf16[32,3584]{1,0:T(8,128)(2,1)S(1)} %sum.17), channel_id=1, source_target_pairs={{0,24},{8,0},{16,8},{24,16},{1,25},{9,1},{17,9},{25,17},{2,26},{10... | collective-permute-start | bytes 688136 | tf_op jit(solution)/shard_map/ppermute | solution.py:214

commit v3 on v2

--- a/solution.py
+++ b/solution.py
@@ -40,8 +40,8 @@
 
 
 class Order:
-    def __init__(self):
-        self.before = []
+    def __init__(self, first):
+        self.before = [first]
 
     def call(self, kernel, out_shape, in_specs, operands, out_specs=NEAR, **options):
         before, count = self.before, len(operands)
@@ -50,9 +50,7 @@
             out_shape=out_shape,
             in_specs=in_specs + [ANYWHERE] * len(before),
             out_specs=jax.tree.map(lambda _: out_specs, out_shape),
-            compiler_params=LIMIT,
-            cost_estimate=NO_COST,
-            **options,
+            **{"compiler_params": LIMIT, "cost_estimate": NO_COST, **options},
         )(*operands, *before)
         self.before = [jax.tree.leaves(result)[0]]
         return result
@@ -67,6 +65,86 @@
             input_output_aliases={0: 0},
             name="arrived",
         )
+
+
+def begin_kernel(chips, *refs):
+    sources, out, weights, copied, sems = refs[:7], refs[7], refs[8:11], refs[11:15], refs[15]
+    copies = [pltpu.make_async_copy(a, b, sems.at[k]) for k, (a, b) in enumerate(zip(sources, (*copied, *weights)))]
+    for copy in copies:
+        copy.start()
+    for copy in copies[:4]:
+        copy.wait()
+    streams, gain, routes, gates = copied
+    _, tokens, width = streams.shape
+    square = (tokens, tokens)
+    diagonal = lax.broadcasted_iota(jnp.int32, square, 0) == lax.broadcasted_iota(jnp.int32, square, 1)
+    lane = lax.broadcasted_iota(jnp.int32, (tokens, TAIL), 1)
+    expert, addend = jnp.full((tokens, TAIL), -1, jnp.int32), jnp.zeros((tokens, TAIL), jnp.int32)
+    for which in range(3):
+        for e in range(chips):
+            here = lane == which * chips + e
+            expert, addend = jnp.where(here, e, expert), jnp.where(here, which, addend)
+
+    def column(row):
+        return jnp.sum(jnp.where(diagonal, row, 0), axis=1, keepdims=True)
+
+    for stream in range(streams.shape[0]):
+        place = pl.ds(stream * tokens, tokens)
+        state = streams[stream].astype(jnp.float32)
+        scale = lax.rsqrt(jnp.mean(state * state, axis=-1, keepdims=True) + 1e-06)
+        out[place, pl.ds(0, width)] = (state * scale * gain[...]).astype(jnp.bfloat16)
+        left = jnp.zeros((tokens, TAIL), jnp.float32)
+        for k in range(routes.shape[1]):
+            named = column(routes[stream, pl.ds(k, 1)]) == expert
+            left += jnp.where(named, column(gates[stream, pl.ds(k, 1)]), 0.0)
+        tail = jnp.zeros((tokens, TAIL), jnp.float32)
+        for which in range(3):
+            rounded = left.astype(jnp.bfloat16).astype(jnp.float32)
+            tail = jnp.where(addend == which, rounded, tail)
+            left = left - rounded
+        out[place, pl.ds(width, TAIL)] = tail.astype(jnp.bfloat16)
+    for copy in copies[4:]:
+        copy.wait()
+
+
+def norm_kernel(chips, *refs):
+    sources, outs, copied, sems = refs[:4], refs[4:-5], refs[-5:-1], refs[-1]
+    copies = [pltpu.make_async_copy(a, b, sems.at[k]) for k, (a, b) in enumerate(zip(sources, copied))]
+    for copy in copies:
+        copy.start()
+    for copy in copies:
+        copy.wait()
+    streams, gain, routes, gates = copied
+    _, tokens, width = streams.shape
+    square = (tokens, tokens)
+    diagonal = lax.broadcasted_iota(jnp.int32, square, 0) == lax.broadcasted_iota(jnp.int32, square, 1)
+    lane = lax.broadcasted_iota(jnp.int32, (tokens, TAIL), 1)
+    expert, addend = jnp.full((tokens, TAIL), -1, jnp.int32), jnp.zeros((tokens, TAIL), jnp.int32)
+    for which in range(3):
+        for e in range(chips):
+            here = lane == which * chips + e
+            expert, addend = jnp.where(here, e, expert), jnp.where(here, which, addend)
+
+    def column(row):
+        return jnp.sum(jnp.where(diagonal, row, 0), axis=1, keepdims=True)
+
+    for stream in range(streams.shape[0]):
+        place = pl.ds(stream * tokens, tokens)
+        state = streams[stream].astype(jnp.float32)
+        scale = lax.rsqrt(jnp.mean(state * state, axis=-1, keepdims=True) + 1e-06)
+        out[place, pl.ds(0, width)] = (state * scale * gain[...]).astype(jnp.bfloat16)
+        left = jnp.zeros((tokens, TAIL), jnp.float32)
+        for k in range(routes.shape[1]):
+            named = column(routes[stream, pl.ds(k, 1)]) == expert
+            left += jnp.where(named, column(gates[stream, pl.ds(k, 1)]), 0.0)
+        tail = jnp.zeros((tokens, TAIL), jnp.float32)
+        for which in range(3):
+            rounded = left.astype(jnp.bfloat16).astype(jnp.float32)
+            tail = jnp.where(addend == which, rounded, tail)
+            left = left - rounded
+        out[place, pl.ds(width, TAIL)] = tail.astype(jnp.bfloat16)
+    for copy in copies[4:]:
+        copy.wait()
 
 
 def load_kernel(*refs):
@@ -113,27 +191,32 @@
     out[...] = total.astype(jnp.bfloat16)
 
 
-def stack_kernel(*refs):
+def stack_kernel(start, rows, *refs):
     *parts, out = refs
-    start = 0
-    for part in parts:
-        out[pl.ds(start, part.shape[0])] = part[...]
-        start += part.shape[0]
+    for which, part in enumerate(parts):
+        out[pl.ds(which * rows, rows)] = part[pl.ds(start, rows)]
 
 
 class Device:
     def __init__(self, order, weights, mask):
         self.order, self.weights, self.mask = order, weights, mask
 
-    def load(self):
-        own = self.order.call(
-            load_kernel,
-            [pltpu.VMEM(w.shape, w.dtype) for w in self.weights],
-            [ANYWHERE] * len(self.weights),
-            [pltpu.with_memory_space_constraint(w, pltpu.HBM) for w in self.weights],
-            scratch_shapes=[pltpu.SemaphoreType.DMA((len(self.weights),))],
-            name="weights_to_vmem",
-        )
+    def begin(self, chips, *sources):
+        streams = sources[0]
+        sent = jax.ShapeDtypeStruct((streams.shape[0] * streams.shape[1], streams.shape[2] + TAIL), jnp.bfloat16)
+        sent, gate_w, up_w, down_w = self.order.call(
+            functools.partial(begin_kernel, chips),
+            [sent] + [pltpu.VMEM(w.shape, w.dtype) for w in self.weights],
+            [ANYWHERE] * 7,
+            [pltpu.with_memory_space_constraint(x, pltpu.HBM) for x in (*sources, *self.weights)],
+            scratch_shapes=[pltpu.VMEM(x.shape, x.dtype) for x in sources] + [pltpu.SemaphoreType.DMA((7,))],
+            name="begin",
+        )
+        self.weights = gate_w, up_w, down_w
+        return sent
+
+    def share(self):
+        own = [self.order.wait(w) for w in self.weights]
         self.weights = (*own, *(swap_cores(w) for w in own))
 
     def ffn(self, blocks, parts):
@@ -144,6 +227,7 @@
             [NEAR] * (len(blocks) + 7),
             near(*blocks, self.mask, *self.weights),
             name="expert",
+            compiler_params=pltpu.CompilerParams(vmem_limit_bytes=28 << 20),
         )
 
     def add(self, *terms, rows=None):
@@ -157,11 +241,10 @@
             name="sum",
         )
 
-    def stack(self, *parts):
-        rows = sum(part.shape[0] for part in parts)
+    def stack(self, *parts, start, rows):
         return self.order.call(
-            stack_kernel,
-            jax.ShapeDtypeStruct((rows, parts[0].shape[1]), jnp.bfloat16),
+            functools.partial(stack_kernel, start, rows),
+            jax.ShapeDtypeStruct((len(parts) * rows, parts[0].shape[1]), jnp.bfloat16),
             [NEAR] * len(parts),
             near(*parts),
             name="stack",
@@ -174,7 +257,7 @@
         self.last = lax.axis_size("expert") // 2 - 2
         self.rows = own[0].shape[0] // 2
         self.together = together
-        self.moving, self.held, self.partials, self.shifted = {}, [], [], []
+        self.moving, self.held, self.partials, self.shifted = {}, {}, {}, []
 
     def depart(self, after=True):
         for part, own in enumerate(self.own):
@@ -186,12 +269,11 @@
             blocks.append(self.device.order.wait(self.moving[part]))
             if step < self.last:
                 self.moving[part] = gather_hop(blocks[part], step + 1)
-        self.held.append(blocks)
-
-    def work(self):
-        for blocks in self.held:
-            self.partials.append(self.device.ffn(blocks, 1 if self.together else len(blocks)))
-        self.held = []
+        self.held[step] = blocks
+
+    def work(self, step):
+        blocks = self.held.pop(step)
+        self.partials[step] = self.device.ffn(blocks, 1 if self.together else len(blocks))
 
     def send_back(self):
         self.sums = [reduce_hop(partial, self.last) for partial in self.partials[self.last]]
@@ -221,39 +303,24 @@
         return jnp.concatenate(self.shifted, axis=0)
 
 
-def in_parts(value):
-    parts = []
-    for _ in range(3):
-        parts.append(value.astype(jnp.bfloat16))
-        value = value - parts[-1].astype(jnp.float32)
-    return parts
-
-
 def body(streams, norm_gain, w_gate, w_up, w_down, routes, gate_weights):
     chips = lax.axis_size("expert") // 2
     sections = lax.axis_size("pipe")
     weights = (w_gate[0, 0], w_up[0, 0], w_down[0, 0])
     tokens = streams.shape[2]
     rows = tokens // PARTS
-    named = routes[0][..., None] == jnp.arange(chips, dtype=jnp.int32)
-    dense = jnp.sum(jnp.where(named, gate_weights[0][..., None], 0.0), axis=2)
-    tail = jnp.concatenate(in_parts(dense), axis=-1)
-    tail = jnp.pad(tail, ((0, 0), (0, 0), (0, TAIL - tail.shape[-1])))
     lane = jnp.arange(TAIL)
     mask = ((lane % chips == lax.axis_index("expert") // 2) & (lane < 3 * chips)).astype(jnp.float32)[None]
-    wide = streams[0].astype(jnp.float32)
-    normed = (
-        wide * lax.rsqrt(jnp.mean(wide * wide, axis=-1, keepdims=True) + 1e-06) * norm_gain[0]
-    ).astype(jnp.bfloat16)
-    sent, mask = lax.optimization_barrier((jnp.concatenate([normed, tail], axis=-1), mask))
+    device = Device(Order(mask), weights, mask)
+    sent = device.begin(
+        chips, streams[0], norm_gain, routes[0].transpose(0, 2, 1), gate_weights[0].transpose(0, 2, 1)
+    )
     swapped = swap_cores(sent)
-    device = Device(Order(), weights, mask)
     own = [
-        [device.stack(sent[stream, cut:cut + rows], swapped[stream, cut:cut + rows]) for cut in range(0, tokens, rows)]
-        for stream in range(2)
+        [device.stack(sent, swapped, start=start, rows=rows) for start in range(first, first + tokens, rows)]
+        for first in (0, tokens)
     ]
     chunks = []
-    local = []
     for stream in range(2):
         step = 1 if stream == 0 else sections - 1
         pairs = [(source, (source + step) % sections) for source in range(sections)]
@@ -261,30 +328,30 @@
     one, two = chunks
     last = one.last
     one.depart(after=False)
-    device.load()
+    device.share()
     for step in range(last):
         one.gather(step)
     two.depart()
-    one.work()
+    for step in range(last):
+        one.work(step)
     one.gather(last)
-    one.work()
+    one.work(last)
     one.send_back()
     for step in range(last):
         two.gather(step)
-        two.work()
-        if step == 0:
-            (local,) = device.ffn([sent.reshape(-1, sent.shape[-1])], 1)
-            one.local, two.local = (local, 0), (local, tokens)
-        if step < last - 1 or last == 1:
+        if step < last - 1:
             one.go_on(last - 1 - step)
     two.gather(last)
-    two.work()
+    two.work(last)
     two.send_back()
     one.go_on(0)
-    for step in reversed(range(1, last)):
+    for step in reversed(range(last)):
+        two.work(step)
+        if step == 0:
+            (local,) = device.ffn([sent], 1)
+            one.local, two.local = (local, 0), (local, tokens)
+            one.finish()
         two.go_on(step)
-    one.finish()
-    two.go_on(0)
     one.settle()
     two.finish()
     return jnp.stack([one.result(), two.result()])[None]

time: 148 us -> 144 us (0.973)
  other arithmetic: 4.57 us -> 1.1 us
    ppermute x9, waiting for transfers between devices: 26.4 us -> 23 us  [reduce_hop(): lax.ppermute(value, 'expert', [(target, source) for source, target in hop...]
    ppermute x12, waiting for transfers between devices: 11.9 us -> 15 us  [gather_hop(): return lax.ppermute(value, 'expert', hop_pairs(step))]
    reduce_sum x2 -> x0, other arithmetic: 2.24 us -> none  [the longest x1 1.45 us: body(): jnp.mean(wide * wide, axis=-1, keepdims=True) + 1e-06]
    pallas_call x45 -> x48, Pallas kernels: 28.1 us -> 28.3 us  [call(): pl.pallas_call(lambda *refs: kernel(*refs[:count], *refs[count + len(befo...]
  transfers between devices with their start and end apart: 31 -> 31, of which waited for: 22 -> 21; matrix products, arithmetic and copies ran while one was open for 0% -> 0% of each run, Pallas kernels for 16% -> 16%
where the time goes in v3:
time: 144 us
  waiting for transfers between devices  59.2 us (41%)
  starting transfers between devices  54.2 us (38%)
  Pallas kernels  28.3 us (20%)
    ppermute x12, starting transfers between devices, gather_hop(): return lax.ppermute(value, 'expert', hop_pairs(step))  35.6 us
    pallas_call x48, Pallas kernels, call(): pl.pallas_call(lambda *refs: kernel(*refs[:count], *refs[count + len(befo...  28.3 us
    ppermute x9, waiting for transfers between devices, reduce_hop(): lax.ppermute(value, 'expert', [(target, source) for source, target in hop...  23 us
    ppermute x9, starting transfers between devices, reduce_hop(): lax.ppermute(value, 'expert', [(target, source) for source, target in hop...  15.9 us
    ppermute x12, waiting for transfers between devices, gather_hop(): return lax.ppermute(value, 'expert', hop_pairs(step))  15 us
    ppermute x3, waiting for transfers between devices, finish(): self.shifted.append(lax.ppermute(mixed, 'pipe', self.pairs))  14.6 us
    ppermute x7, waiting for transfers between devices, swap_cores(): return lax.ppermute(value, 'expert', [(i, i ^ 1) for i in range(count)])  6.59 us
  transfers between devices with their start and end apart: 31, of which 21 were waited for; matrix products, arithmetic and copies ran while one was open for 0% of the time, Pallas kernels for 16%

profile of v3, /device:TPU:22, one launch (start us, length us, event | category | flops | bytes accessed | tf_op | source)
XLA Modules:
  0.0 143.6 jit_solution(4986477879329647306)
XLA Ops:
  0.0 4.6 %begin.1 = (bf16[128,3712]{1,0:T(8,128)(2,1)S(1)}, bf16[3584,512]{1,0:T(8,128)(2,1)S(1)}, bf16[3584,512]{1,0:T(8,128)(2,1)S(1)}, bf16[512,3584]{1,0:T(8,128)(2,1)S(1)}) custom-call(bf16[2,64,3584]{2,1,0:T(8,128)(2,1)} %bitcast.22, f32[1,3584]{1,0:T(1,128)} %refs_1_.1, s32[2,2,64]{2,1,0:T(2,128)} %bitcast.26, f32[2,2,64]{2,1,0:T(2,128)} %bitcast.27, ...), custom_call_target="tpu_custom_call" | custom-call | flops 1024 | bytes 1024 | tf_op jit(solution)/shard_map/begin/pallas_call | solution.py:48
  4.7 2.5 %collective-permute-done.refs_1_ = bf16[128,3712]{1,0:T(8,128)(2,1)S(1)} collective-permute-done((bf16[128,3712]{1,0:T(8,128)(2,1)S(1)}, bf16[128,3712]{1,0:T(8,128)(2,1)S(1)}, u32[]{:S(2)}, u32[]{:S(2)}) %collective-permute-start) | collective-permute-done | bytes 950304 | tf_op jit(solution)/shard_map/ppermute | solution.py:20
  8.1 3.5 %collective-permute-start.5 = (bf16[64,3712]{1,0:T(8,128)(2,1)S(1)}, bf16[64,3712]{1,0:T(8,128)(2,1)S(1)}, u32[]{:S(2)}, u32[]{:S(2)}) collective-permute-start(bf16[64,3712]{1,0:T(8,128)(2,1)S(1)} %stack.16.refs_2_), channel_id=1, source_target_pairs={{0,2},{2,4},{4,6},{3,1},{5,3},{7,5},{8,10},{10,12},{12,14},{11,9},... | collective-permute-start | bytes 1425416 | tf_op jit(solution)/shard_map/ppermute | solution.py:31
  13.5 5.1 %collective-permute-done.5.refs_0_ = bf16[64,3712]{1,0:T(8,128)(2,1)S(1)} collective-permute-done((bf16[64,3712]{1,0:T(8,128)(2,1)S(1)}, bf16[64,3712]{1,0:T(8,128)(2,1)S(1)}, u32[]{:S(2)}, u32[]{:S(2)}) %collective-permute-start.5) | collective-permute-done | bytes 475168 | tf_op jit(solution)/shard_map/ppermute | solution.py:31
  18.6 3.5 %collective-permute-start.7 = (bf16[64,3712]{1,0:T(8,128)(2,1)S(1)}, bf16[64,3712]{1,0:T(8,128)(2,1)S(1)}, u32[]{:S(2)}, u32[]{:S(2)}) collective-permute-start(bf16[64,3712]{1,0:T(8,128)(2,1)S(1)} %arrived.30.refs_1_.refs_0_), channel_id=1, source_target_pairs={{2,4},{4,6},{3,1},{5,3},{10,12},{12,14},{11,9},{13,11},{18,20},{20... | collective-permute-start | bytes 1425416 | tf_op jit(solution)/shard_map/ppermute | solution.py:31
  23.7 3.5 %collective-permute-start.6 = (bf16[64,3712]{1,0:T(8,128)(2,1)S(1)}, bf16[64,3712]{1,0:T(8,128)(2,1)S(1)}, u32[]{:S(2)}, u32[]{:S(2)}) collective-permute-start(bf16[64,3712]{1,0:T(8,128)(2,1)S(1)} %arrived.31.refs_1_), channel_id=1, source_target_pairs={{2,4},{4,6},{3,1},{5,3},{10,12},{12,14},{11,9},{13,11},{18,20},{20... | collective-permute-start | bytes 1425416 | tf_op jit(solution)/shard_map/ppermute | solution.py:31
  27.2 2.0 %collective-permute-done.7.refs_0_ = bf16[64,3712]{1,0:T(8,128)(2,1)S(1)} collective-permute-done((bf16[64,3712]{1,0:T(8,128)(2,1)S(1)}, bf16[64,3712]{1,0:T(8,128)(2,1)S(1)}, u32[]{:S(2)}, u32[]{:S(2)}) %collective-permute-start.7) | collective-permute-done | bytes 475168 | tf_op jit(solution)/shard_map/ppermute | solution.py:31
  29.2 3.5 %collective-permute-start.9 = (bf16[64,3712]{1,0:T(8,128)(2,1)S(1)}, bf16[64,3712]{1,0:T(8,128)(2,1)S(1)}, u32[]{:S(2)}, u32[]{:S(2)}) collective-permute-start(bf16[64,3712]{1,0:T(8,128)(2,1)S(1)} %arrived.32.refs_1_.refs_0_), channel_id=1, source_target_pairs={{4,6},{3,1},{12,14},{11,9},{20,22},{19,17},{28,30},{27,25}} | collective-permute-start | bytes 1425416 | tf_op jit(solution)/shard_map/ppermute | solution.py:31
  34.3 3.5 %collective-permute-start.10 = (bf16[64,3712]{1,0:T(8,128)(2,1)S(1)}, bf16[64,3712]{1,0:T(8,128)(2,1)S(1)}, u32[]{:S(2)}, u32[]{:S(2)}) collective-permute-start(bf16[64,3712]{1,0:T(8,128)(2,1)S(1)} %arrived.33.refs_1_), channel_id=1, source_target_pairs={{4,6},{3,1},{12,14},{11,9},{20,22},{19,17},{28,30},{27,25}} | collective-permute-start | bytes 1425416 | tf_op jit(solution)/shard_map/ppermute | solution.py:31
  37.8 1.9 %collective-permute-start.8 = (bf16[64,3712]{1,0:T(8,128)(2,1)S(1)}, bf16[64,3712]{1,0:T(8,128)(2,1)S(1)}, u32[]{:S(2)}, u32[]{:S(2)}) collective-permute-start(bf16[64,3712]{1,0:T(8,128)(2,1)S(1)} %arrived.34.refs_1_), channel_id=1, source_target_pairs={{0,2},{2,4},{4,6},{3,1},{5,3},{7,5},{8,10},{10,12},{12,14},{11,9},... | collective-permute-start | bytes 1425416 | tf_op jit(solution)/shard_map/ppermute | solution.py:31
  41.7 3.2 %expert.7.refs_9_.refs_0_ = bf16[128,3584]{1,0:T(8,128)(2,1)S(1)} custom-call(bf16[64,3712]{1,0:T(8,128)(2,1)S(1)} %arrived.30.refs_1_.refs_0_, bf16[64,3712]{1,0:T(8,128)(2,1)S(1)} %arrived.31.refs_1_, f32[1,128]{1,0:T(1,128)S(1)} %and_convert_fusion.refs_7_.refs_2_.refs_1_, bf16[3584,512]{1,0:T(8,128)(2,1)S(1)} %arrived.27.refs_1_.refs_3_.refs_2_, ...), custom_call_target="tpu_custom_call" | custom-call | flops 1024 | bytes 1024 | tf_op jit(solution)/shard_map/expert/pallas_call | solution.py:48
  44.9 3.2 %expert.8.refs_1_.refs_0_ = bf16[128,3584]{1,0:T(8,128)(2,1)S(1)} custom-call(bf16[64,3712]{1,0:T(8,128)(2,1)S(1)} %arrived.32.refs_1_.refs_0_, bf16[64,3712]{1,0:T(8,128)(2,1)S(1)} %arrived.33.refs_1_, f32[1,128]{1,0:T(1,128)S(1)} %and_convert_fusion.refs_7_.refs_2_.refs_1_, bf16[3584,512]{1,0:T(8,128)(2,1)S(1)} %arrived.27.refs_1_.refs_3_.refs_2_, ...), custom_call_target="tpu_custom_call" | custom-call | flops 1024 | bytes 1024 | tf_op jit(solution)/shard_map/expert/pallas_call | solution.py:48
  48.1 3.2 %expert.9.refs_1_ = bf16[128,3584]{1,0:T(8,128)(2,1)S(1)} custom-call(bf16[64,3712]{1,0:T(8,128)(2,1)S(1)} %arrived.36.refs_1_.refs_0_, bf16[64,3712]{1,0:T(8,128)(2,1)S(1)} %arrived.37.refs_1_.refs_9_, f32[1,128]{1,0:T(1,128)S(1)} %and_convert_fusion.refs_7_.refs_2_.refs_1_, bf16[3584,512]{1,0:T(8,128)(2,1)S(1)} %arrived.27.refs_1_.refs_3_.refs_2_, ...), custom_call_target="tpu_custom_call" | custom-call | flops 1024 | bytes 1024 | tf_op jit(solution)/shard_map/expert/pallas_call | solution.py:48
  52.6 4.6 %collective-permute-start.12 = (bf16[64,3712]{1,0:T(8,128)(2,1)S(1)}, bf16[64,3712]{1,0:T(8,128)(2,1)S(1)}, u32[]{:S(2)}, u32[]{:S(2)}) collective-permute-start(bf16[64,3712]{1,0:T(8,128)(2,1)S(1)} %arrived.38.refs_1_.refs_0_), channel_id=1, source_target_pairs={{2,4},{4,6},{3,1},{5,3},{10,12},{12,14},{11,9},{13,11},{18,20},{20... | collective-permute-start | bytes 1425416 | tf_op jit(solution)/shard_map/ppermute | solution.py:31
  59.2 7.4 %collective-permute-done.13.refs_0_ = bf16[128,3584]{1,0:T(8,128)(2,1)S(1)} collective-permute-done((bf16[128,3584]{1,0:T(8,128)(2,1)S(1)}, bf16[128,3584]{1,0:T(8,128)(2,1)S(1)}, u32[]{:S(2)}, u32[]{:S(2)}) %collective-permute-start.13) | collective-permute-done | bytes 917536 | tf_op jit(solution)/shard_map/ppermute | solution.py:35
  68.5 4.4 %collective-permute-start.17 = (bf16[64,3712]{1,0:T(8,128)(2,1)S(1)}, bf16[64,3712]{1,0:T(8,128)(2,1)S(1)}, u32[]{:S(2)}, u32[]{:S(2)}) collective-permute-start(bf16[64,3712]{1,0:T(8,128)(2,1)S(1)} %arrived.42.refs_1_), channel_id=1, source_target_pairs={{4,6},{3,1},{12,14},{11,9},{20,22},{19,17},{28,30},{27,25}} | collective-permute-start | bytes 1425416 | tf_op jit(solution)/shard_map/ppermute | solution.py:31
  72.9 2.1 %collective-permute-start.15 = (bf16[128,3584]{1,0:T(8,128)(2,1)S(1)}, bf16[128,3584]{1,0:T(8,128)(2,1)S(1)}, u32[]{:S(2)}, u32[]{:S(2)}) collective-permute-start(bf16[128,3584]{1,0:T(8,128)(2,1)S(1)} %sum.9.refs_1_), channel_id=1, source_target_pairs={{4,2},{6,4},{1,3},{3,5},{12,10},{14,12},{9,11},{11,13},{20,18},{22... | collective-permute-start | bytes 2752520 | tf_op jit(solution)/shard_map/ppermute | solution.py:35
  75.0 4.5 %collective-permute-done.17.refs_0_ = bf16[64,3712]{1,0:T(8,128)(2,1)S(1)} collective-permute-done((bf16[64,3712]{1,0:T(8,128)(2,1)S(1)}, bf16[64,3712]{1,0:T(8,128)(2,1)S(1)}, u32[]{:S(2)}, u32[]{:S(2)}) %collective-permute-start.17) | collective-permute-done | bytes 475168 | tf_op jit(solution)/shard_map/ppermute | solution.py:31
  79.5 3.2 %expert.10 = (bf16[64,3584]{1,0:T(8,128)(2,1)S(1)}, bf16[64,3584]{1,0:T(8,128)(2,1)S(1)}) custom-call(bf16[64,3712]{1,0:T(8,128)(2,1)S(1)} %arrived.43.refs_1_.refs_0_, bf16[64,3712]{1,0:T(8,128)(2,1)S(1)} %arrived.44.refs_1_.refs_9_, f32[1,128]{1,0:T(1,128)S(1)} %and_convert_fusion.refs_7_.refs_2_.refs_1_, ...), custom_call_target="tpu_custom_call" | custom-call | flops 1024 | bytes 1024 | tf_op jit(solution)/shard_map/expert/pallas_call | solution.py:48
  84.0 4.2 %collective-permute-done.15.refs_0_ = bf16[128,3584]{1,0:T(8,128)(2,1)S(1)} collective-permute-done((bf16[128,3584]{1,0:T(8,128)(2,1)S(1)}, bf16[128,3584]{1,0:T(8,128)(2,1)S(1)}, u32[]{:S(2)}, u32[]{:S(2)}) %collective-permute-start.15) | collective-permute-done | bytes 917536 | tf_op jit(solution)/shard_map/ppermute | solution.py:35
  89.7 2.1 %collective-permute-start.20 = (bf16[128,3584]{1,0:T(8,128)(2,1)S(1)}, bf16[128,3584]{1,0:T(8,128)(2,1)S(1)}, u32[]{:S(2)}, u32[]{:S(2)}) collective-permute-start(bf16[128,3584]{1,0:T(8,128)(2,1)S(1)} %sum.10.refs_9_), channel_id=1, source_target_pairs={{2,0},{4,2},{6,4},{1,3},{3,5},{5,7},{10,8},{12,10},{14,12},{9,11},... | collective-permute-start | bytes 2752520 | tf_op jit(solution)/shard_map/ppermute | solution.py:35
  91.7 3.2 %expert.11 = (bf16[64,3584]{1,0:T(8,128)(2,1)S(1)}, bf16[64,3584]{1,0:T(8,128)(2,1)S(1)}) custom-call(bf16[64,3712]{1,0:T(8,128)(2,1)S(1)} %arrived.41.refs_1_.refs_0_, bf16[64,3712]{1,0:T(8,128)(2,1)S(1)} %arrived.42.refs_1_, f32[1,128]{1,0:T(1,128)S(1)} %and_convert_fusion.refs_7_.refs_2_.refs_1_, bf16[3584,512]{1,0:T(8,128)(2,1)S(1)} %arrived.27.refs_1_.refs_3_.refs_2_, ...), custom_call_target="tpu_custom_call" | custom-call | flops 1024 | bytes 1024 | tf_op jit(solution)/shard_map/expert/pallas_call | solution.py:48
  98.6 2.1 %collective-permute-start.23 = (bf16[64,3584]{1,0:T(8,128)(2,1)S(1)}, bf16[64,3584]{1,0:T(8,128)(2,1)S(1)}, u32[]{:S(2)}, u32[]{:S(2)}) collective-permute-start(bf16[64,3584]{1,0:T(8,128)(2,1)S(1)} %sum.12.refs_9_), channel_id=1, source_target_pairs={{4,2},{6,4},{1,3},{3,5},{12,10},{14,12},{9,11},{11,13},{20,18},{22... | collective-permute-start | bytes 1376264 | tf_op jit(solution)/shard_map/ppermute | solution.py:35
  100.8 3.2 %expert.12 = (bf16[64,3584]{1,0:T(8,128)(2,1)S(1)}, bf16[64,3584]{1,0:T(8,128)(2,1)S(1)}) custom-call(bf16[64,3712]{1,0:T(8,128)(2,1)S(1)} %arrived.38.refs_1_.refs_0_, bf16[64,3712]{1,0:T(8,128)(2,1)S(1)} %arrived.39.refs_1_, f32[1,128]{1,0:T(1,128)S(1)} %and_convert_fusion.refs_7_.refs_2_.refs_1_, bf16[3584,512]{1,0:T(8,128)(2,1)S(1)} %arrived.27.refs_1_.refs_3_.refs_2_, ...), custom_call_target="tpu_custom_call" | custom-call | flops 1024 | bytes 1024 | tf_op jit(solution)/shard_map/expert/pallas_call | solution.py:48
  104.0 3.2 %expert.13.refs_1_ = bf16[128,3584]{1,0:T(8,128)(2,1)S(1)} custom-call(bf16[128,3712]{1,0:T(8,128)(2,1)S(1)} %get-tuple-element.15.refs_0_.refs_2_, f32[1,128]{1,0:T(1,128)S(1)} %and_convert_fusion.refs_7_.refs_2_.refs_1_, bf16[3584,512]{1,0:T(8,128)(2,1)S(1)} %arrived.27.refs_1_.refs_3_.refs_2_, bf16[3584,512]{1,0:T(8,128)(2,1)S(1)} %arrived.28.refs_1_.refs_4_.refs_3_, ...), custom_call_target="tpu_custom_call" | custom-call | flops 1024 | bytes 1024 | tf_op jit(solution)/shard_map/expert/pallas_call | solution.py:48
  111.1 2.1 %collective-permute-done.24.refs_0_ = bf16[64,3584]{1,0:T(8,128)(2,1)S(1)} collective-permute-done((bf16[64,3584]{1,0:T(8,128)(2,1)S(1)}, bf16[64,3584]{1,0:T(8,128)(2,1)S(1)}, u32[]{:S(2)}, u32[]{:S(2)}) %collective-permute-start.24) | collective-permute-done | bytes 458784 | tf_op jit(solution)/shard_map/ppermute | solution.py:35
  115.3 2.9 %collective-permute-done.23.refs_0_ = bf16[64,3584]{1,0:T(8,128)(2,1)S(1)} collective-permute-done((bf16[64,3584]{1,0:T(8,128)(2,1)S(1)}, bf16[64,3584]{1,0:T(8,128)(2,1)S(1)}, u32[]{:S(2)}, u32[]{:S(2)}) %collective-permute-start.23) | collective-permute-done | bytes 458784 | tf_op jit(solution)/shard_map/ppermute | solution.py:35
  118.3 1.9 %collective-permute-start.28 = (bf16[64,3584]{1,0:T(8,128)(2,1)S(1)}, bf16[64,3584]{1,0:T(8,128)(2,1)S(1)}, u32[]{:S(2)}, u32[]{:S(2)}) collective-permute-start(bf16[64,3584]{1,0:T(8,128)(2,1)S(1)} %sum.15.refs_1_), channel_id=1, source_target_pairs={{2,0},{4,2},{6,4},{1,3},{3,5},{5,7},{10,8},{12,10},{14,12},{9,11},... | collective-permute-start | bytes 1376264 | tf_op jit(solution)/shard_map/ppermute | solution.py:35
  120.2 3.0 %collective-permute-done.22.refs_0_ = bf16[64,3584]{1,0:T(8,128)(2,1)S(1)} collective-permute-done((bf16[64,3584]{1,0:T(8,128)(2,1)S(1)}, bf16[64,3584]{1,0:T(8,128)(2,1)S(1)}, u32[]{:S(2)}, u32[]{:S(2)}) %collective-permute-start.22) | collective-permute-done | bytes 458784 | tf_op jit(solution)/shard_map/ppermute | solution.py:296
  125.5 3.2 %collective-permute-done.28.refs_0_ = bf16[64,3584]{1,0:T(8,128)(2,1)S(1)} collective-permute-done((bf16[64,3584]{1,0:T(8,128)(2,1)S(1)}, bf16[64,3584]{1,0:T(8,128)(2,1)S(1)}, u32[]{:S(2)}, u32[]{:S(2)}) %collective-permute-start.28) | collective-permute-done | bytes 458784 | tf_op jit(solution)/shard_map/ppermute | solution.py:35
  131.0 7.2 %collective-permute-done.27 = bf16[32,3584]{1,0:T(8,128)(2,1)S(1)} collective-permute-done((bf16[32,3584]{1,0:T(8,128)(2,1)S(1)}, bf16[32,3584]{1,0:T(8,128)(2,1)S(1)}, u32[]{:S(2)}, u32[]{:S(2)}) %collective-permute-start.27) | collective-permute-done | bytes 229408 | tf_op jit(solution)/shard_map/ppermute | solution.py:296
  138.1 4.5 %collective-permute-done.30 = bf16[32,3584]{1,0:T(8,128)(2,1)S(1)} collective-permute-done((bf16[32,3584]{1,0:T(8,128)(2,1)S(1)}, bf16[32,3584]{1,0:T(8,128)(2,1)S(1)}, u32[]{:S(2)}, u32[]{:S(2)}) %collective-permute-start.30) | collective-permute-done | bytes 229408 | tf_op jit(solution)/shard_map/ppermute | solution.py:296
  (90 shorter events, 31.2 us)
Async XLA Ops:
  4.6 2.6 %collective-permute-start = (bf16[128,3712]{1,0:T(8,128)(2,1)S(1)}, bf16[128,3712]{1,0:T(8,128)(2,1)S(1)}, u32[]{:S(2)}, u32[]{:S(2)}) collective-permute-start(bf16[128,3712]{1,0:T(8,128)(2,1)S(1)} %get-tuple-element.15.refs_0_.refs_2_), channel_id=1, source_target_pairs={{0,1},{1,0},{2,3},{3,2},{4,5},{5,4},{6,7},{7,6},{8,9},{9,8},{10,11... | collective-permute-start | bytes 2850824 | tf_op jit(solution)/shard_map/ppermute | solution.py:20
  7.4 30.4 %collective-permute-start.3 = (bf16[512,3584]{1,0:T(8,128)(2,1)S(1)}, bf16[512,3584]{1,0:T(8,128)(2,1)S(1)}, u32[]{:S(2)}, u32[]{:S(2)}) collective-permute-start(bf16[512,3584]{1,0:T(8,128)(2,1)S(1)} %arrived.29.refs_1_.refs_5_.refs_4_), channel_id=1, source_target_pairs={{0,1},{1,0},{2,3},{3,2},{4,5},{5,4},{6,7},{7,6},{8,9},{9,8},{10,11... | collective-permute-start | bytes 11010056 | tf_op jit(solution)/shard_map/ppermute | solution.py:20
  7.6 32.1 %collective-permute-start.2 = (bf16[3584,512]{1,0:T(8,128)(2,1)S(1)}, bf16[3584,512]{1,0:T(8,128)(2,1)S(1)}, u32[]{:S(2)}, u32[]{:S(2)}) collective-permute-start(bf16[3584,512]{1,0:T(8,128)(2,1)S(1)} %arrived.28.refs_1_.refs_4_.refs_3_), channel_id=1, source_target_pairs={{0,1},{1,0},{2,3},{3,2},{4,5},{5,4},{6,7},{7,6},{8,9},{9,8},{10,11... | collective-permute-start | bytes 11010056 | tf_op jit(solution)/shard_map/ppermute | solution.py:20
  8.0 33.7 %collective-permute-start.1 = (bf16[3584,512]{1,0:T(8,128)(2,1)S(1)}, bf16[3584,512]{1,0:T(8,128)(2,1)S(1)}, u32[]{:S(2)}, u32[]{:S(2)}) collective-permute-start(bf16[3584,512]{1,0:T(8,128)(2,1)S(1)} %arrived.27.refs_1_.refs_3_.refs_2_), channel_id=1, source_target_pairs={{0,1},{1,0},{2,3},{3,2},{4,5},{5,4},{6,7},{7,6},{8,9},{9,8},{10,11... | collective-permute-start | bytes 11010056 | tf_op jit(solution)/shard_map/ppermute | solution.py:20
  8.1 10.5 %collective-permute-start.5 = (bf16[64,3712]{1,0:T(8,128)(2,1)S(1)}, bf16[64,3712]{1,0:T(8,128)(2,1)S(1)}, u32[]{:S(2)}, u32[]{:S(2)}) collective-permute-start(bf16[64,3712]{1,0:T(8,128)(2,1)S(1)} %stack.16.refs_2_), channel_id=1, source_target_pairs={{0,2},{2,4},{4,6},{3,1},{5,3},{7,5},{8,10},{10,12},{12,14},{11,9},... | collective-permute-start | bytes 1425416 | tf_op jit(solution)/shard_map/ppermute | solution.py:31
  11.6 12.1 %collective-permute-start.4 = (bf16[64,3712]{1,0:T(8,128)(2,1)S(1)}, bf16[64,3712]{1,0:T(8,128)(2,1)S(1)}, u32[]{:S(2)}, u32[]{:S(2)}) collective-permute-start(bf16[64,3712]{1,0:T(8,128)(2,1)S(1)} %stack.17.refs_2_), channel_id=1, source_target_pairs={{0,2},{2,4},{4,6},{3,1},{5,3},{7,5},{8,10},{10,12},{12,14},{11,9},... | collective-permute-start | bytes 1425416 | tf_op jit(solution)/shard_map/ppermute | solution.py:31
  18.6 10.5 %collective-permute-start.7 = (bf16[64,3712]{1,0:T(8,128)(2,1)S(1)}, bf16[64,3712]{1,0:T(8,128)(2,1)S(1)}, u32[]{:S(2)}, u32[]{:S(2)}) collective-permute-start(bf16[64,3712]{1,0:T(8,128)(2,1)S(1)} %arrived.30.refs_1_.refs_0_), channel_id=1, source_target_pairs={{2,4},{4,6},{3,1},{5,3},{10,12},{12,14},{11,9},{13,11},{18,20},{20... | collective-permute-start | bytes 1425416 | tf_op jit(solution)/shard_map/ppermute | solution.py:31
  23.7 10.5 %collective-permute-start.6 = (bf16[64,3712]{1,0:T(8,128)(2,1)S(1)}, bf16[64,3712]{1,0:T(8,128)(2,1)S(1)}, u32[]{:S(2)}, u32[]{:S(2)}) collective-permute-start(bf16[64,3712]{1,0:T(8,128)(2,1)S(1)} %arrived.31.refs_1_), channel_id=1, source_target_pairs={{2,4},{4,6},{3,1},{5,3},{10,12},{12,14},{11,9},{13,11},{18,20},{20... | collective-permute-start | bytes 1425416 | tf_op jit(solution)/shard_map/ppermute | solution.py:31
  29.2 18.9 %collective-permute-start.9 = (bf16[64,3712]{1,0:T(8,128)(2,1)S(1)}, bf16[64,3712]{1,0:T(8,128)(2,1)S(1)}, u32[]{:S(2)}, u32[]{:S(2)}) collective-permute-start(bf16[64,3712]{1,0:T(8,128)(2,1)S(1)} %arrived.32.refs_1_.refs_0_), channel_id=1, source_target_pairs={{4,6},{3,1},{12,14},{11,9},{20,22},{19,17},{28,30},{27,25}} | collective-permute-start | bytes 1425416 | tf_op jit(solution)/shard_map/ppermute | solution.py:31
  34.3 13.8 %collective-permute-start.10 = (bf16[64,3712]{1,0:T(8,128)(2,1)S(1)}, bf16[64,3712]{1,0:T(8,128)(2,1)S(1)}, u32[]{:S(2)}, u32[]{:S(2)}) collective-permute-start(bf16[64,3712]{1,0:T(8,128)(2,1)S(1)} %arrived.33.refs_1_), channel_id=1, source_target_pairs={{4,6},{3,1},{12,14},{11,9},{20,22},{19,17},{28,30},{27,25}} | collective-permute-start | bytes 1425416 | tf_op jit(solution)/shard_map/ppermute | solution.py:31
  37.8 14.8 %collective-permute-start.8 = (bf16[64,3712]{1,0:T(8,128)(2,1)S(1)}, bf16[64,3712]{1,0:T(8,128)(2,1)S(1)}, u32[]{:S(2)}, u32[]{:S(2)}) collective-permute-start(bf16[64,3712]{1,0:T(8,128)(2,1)S(1)} %arrived.34.refs_1_), channel_id=1, source_target_pairs={{0,2},{2,4},{4,6},{3,1},{5,3},{7,5},{8,10},{10,12},{12,14},{11,9},... | collective-permute-start | bytes 1425416 | tf_op jit(solution)/shard_map/ppermute | solution.py:31
  39.7 17.5 %collective-permute-start.11 = (bf16[64,3712]{1,0:T(8,128)(2,1)S(1)}, bf16[64,3712]{1,0:T(8,128)(2,1)S(1)}, u32[]{:S(2)}, u32[]{:S(2)}) collective-permute-start(bf16[64,3712]{1,0:T(8,128)(2,1)S(1)} %arrived.35.refs_9_), channel_id=1, source_target_pairs={{0,2},{2,4},{4,6},{3,1},{5,3},{7,5},{8,10},{10,12},{12,14},{11,9},... | collective-permute-start | bytes 1425416 | tf_op jit(solution)/shard_map/ppermute | solution.py:31
  51.3 15.3 %collective-permute-start.13 = (bf16[128,3584]{1,0:T(8,128)(2,1)S(1)}, bf16[128,3584]{1,0:T(8,128)(2,1)S(1)}, u32[]{:S(2)}, u32[]{:S(2)}) collective-permute-start(bf16[128,3584]{1,0:T(8,128)(2,1)S(1)} %expert.9.refs_1_), channel_id=1, source_target_pairs={{6,4},{1,3},{14,12},{9,11},{22,20},{17,19},{30,28},{25,27}} | collective-permute-start | bytes 2752520 | tf_op jit(solution)/shard_map/ppermute | solution.py:35
  52.6 14.2 %collective-permute-start.12 = (bf16[64,3712]{1,0:T(8,128)(2,1)S(1)}, bf16[64,3712]{1,0:T(8,128)(2,1)S(1)}, u32[]{:S(2)}, u32[]{:S(2)}) collective-permute-start(bf16[64,3712]{1,0:T(8,128)(2,1)S(1)} %arrived.38.refs_1_.refs_0_), channel_id=1, source_target_pairs={{2,4},{4,6},{3,1},{5,3},{10,12},{12,14},{11,9},{13,11},{18,20},{20... | collective-permute-start | bytes 1425416 | tf_op jit(solution)/shard_map/ppermute | solution.py:31
  57.2 11.2 %collective-permute-start.14 = (bf16[64,3712]{1,0:T(8,128)(2,1)S(1)}, bf16[64,3712]{1,0:T(8,128)(2,1)S(1)}, u32[]{:S(2)}, u32[]{:S(2)}) collective-permute-start(bf16[64,3712]{1,0:T(8,128)(2,1)S(1)} %arrived.39.refs_1_), channel_id=1, source_target_pairs={{2,4},{4,6},{3,1},{5,3},{10,12},{12,14},{11,9},{13,11},{18,20},{20... | collective-permute-start | bytes 1425416 | tf_op jit(solution)/shard_map/ppermute | solution.py:31
  66.8 8.2 %collective-permute-start.16 = (bf16[64,3712]{1,0:T(8,128)(2,1)S(1)}, bf16[64,3712]{1,0:T(8,128)(2,1)S(1)}, u32[]{:S(2)}, u32[]{:S(2)}) collective-permute-start(bf16[64,3712]{1,0:T(8,128)(2,1)S(1)} %arrived.41.refs_1_.refs_0_), channel_id=1, source_target_pairs={{4,6},{3,1},{12,14},{11,9},{20,22},{19,17},{28,30},{27,25}} | collective-permute-start | bytes 1425416 | tf_op jit(solution)/shard_map/ppermute | solution.py:31
  68.5 11.0 %collective-permute-start.17 = (bf16[64,3712]{1,0:T(8,128)(2,1)S(1)}, bf16[64,3712]{1,0:T(8,128)(2,1)S(1)}, u32[]{:S(2)}, u32[]{:S(2)}) collective-permute-start(bf16[64,3712]{1,0:T(8,128)(2,1)S(1)} %arrived.42.refs_1_), channel_id=1, source_target_pairs={{4,6},{3,1},{12,14},{11,9},{20,22},{19,17},{28,30},{27,25}} | collective-permute-start | bytes 1425416 | tf_op jit(solution)/shard_map/ppermute | solution.py:31
  72.9 15.3 %collective-permute-start.15 = (bf16[128,3584]{1,0:T(8,128)(2,1)S(1)}, bf16[128,3584]{1,0:T(8,128)(2,1)S(1)}, u32[]{:S(2)}, u32[]{:S(2)}) collective-permute-start(bf16[128,3584]{1,0:T(8,128)(2,1)S(1)} %sum.9.refs_1_), channel_id=1, source_target_pairs={{4,2},{6,4},{1,3},{3,5},{12,10},{14,12},{9,11},{11,13},{20,18},{22... | collective-permute-start | bytes 2752520 | tf_op jit(solution)/shard_map/ppermute | solution.py:35
  82.7 12.2 %collective-permute-start.19 = (bf16[64,3584]{1,0:T(8,128)(2,1)S(1)}, bf16[64,3584]{1,0:T(8,128)(2,1)S(1)}, u32[]{:S(2)}, u32[]{:S(2)}) collective-permute-start(bf16[64,3584]{1,0:T(8,128)(2,1)S(1)} %get-tuple-element.19.refs_1_), channel_id=1, source_target_pairs={{6,4},{1,3},{14,12},{9,11},{22,20},{17,19},{30,28},{25,27}} | collective-permute-start | bytes 1376264 | tf_op jit(solution)/shard_map/ppermute | solution.py:35
  88.2 10.4 %collective-permute-start.18 = (bf16[64,3584]{1,0:T(8,128)(2,1)S(1)}, bf16[64,3584]{1,0:T(8,128)(2,1)S(1)}, u32[]{:S(2)}, u32[]{:S(2)}) collective-permute-start(bf16[64,3584]{1,0:T(8,128)(2,1)S(1)} %get-tuple-element.21), channel_id=1, source_target_pairs={{6,4},{1,3},{14,12},{9,11},{22,20},{17,19},{30,28},{25,27}} | collective-permute-start | bytes 1376264 | tf_op jit(solution)/shard_map/ppermute | solution.py:35
  89.7 5.3 %copy-start = (bf16[1,2,64,3584]{3,2,1,0:T(8,128)(2,1)S(1)}, bf16[1,2,64,3584]{3,2,1,0:T(8,128)(2,1)}, u32[]{:S(2)}) copy-start(bf16[1,2,64,3584]{3,2,1,0:T(8,128)(2,1)} %param.7) | copy-start | bytes 2752516
  89.7 18.7 %collective-permute-start.20 = (bf16[128,3584]{1,0:T(8,128)(2,1)S(1)}, bf16[128,3584]{1,0:T(8,128)(2,1)S(1)}, u32[]{:S(2)}, u32[]{:S(2)}) collective-permute-start(bf16[128,3584]{1,0:T(8,128)(2,1)S(1)} %sum.10.refs_9_), channel_id=1, source_target_pairs={{2,0},{4,2},{6,4},{1,3},{3,5},{5,7},{10,8},{12,10},{14,12},{9,11},... | collective-permute-start | bytes 2752520 | tf_op jit(solution)/shard_map/ppermute | solution.py:35
  95.1 18.2 %collective-permute-start.24 = (bf16[64,3584]{1,0:T(8,128)(2,1)S(1)}, bf16[64,3584]{1,0:T(8,128)(2,1)S(1)}, u32[]{:S(2)}, u32[]{:S(2)}) collective-permute-start(bf16[64,3584]{1,0:T(8,128)(2,1)S(1)} %sum.11.refs_1_), channel_id=1, source_target_pairs={{4,2},{6,4},{1,3},{3,5},{12,10},{14,12},{9,11},{11,13},{20,18},{22... | collective-permute-start | bytes 1376264 | tf_op jit(solution)/shard_map/ppermute | solution.py:35
  98.6 19.6 %collective-permute-start.23 = (bf16[64,3584]{1,0:T(8,128)(2,1)S(1)}, bf16[64,3584]{1,0:T(8,128)(2,1)S(1)}, u32[]{:S(2)}, u32[]{:S(2)}) collective-permute-start(bf16[64,3584]{1,0:T(8,128)(2,1)S(1)} %sum.12.refs_9_), channel_id=1, source_target_pairs={{4,2},{6,4},{1,3},{3,5},{12,10},{14,12},{9,11},{11,13},{20,18},{22... | collective-permute-start | bytes 1376264 | tf_op jit(solution)/shard_map/ppermute | solution.py:35
  108.5 1.9 %collective-permute-start.21 = (bf16[64,3584]{1,0:T(8,128)(2,1)S(1)}, bf16[64,3584]{1,0:T(8,128)(2,1)S(1)}, u32[]{:S(2)}, u32[]{:S(2)}) collective-permute-start(bf16[64,3584]{1,0:T(8,128)(2,1)S(1)} %pad_maximum_fusion.1), channel_id=1, source_target_pairs={{0,1},{1,0},{2,3},{3,2},{4,5},{5,4},{6,7},{7,6},{8,9},{9,8},{10,11... | collective-permute-start | bytes 1376264 | tf_op jit(solution)/shard_map/ppermute | solution.py:20
  110.6 12.6 %collective-permute-start.22 = (bf16[64,3584]{1,0:T(8,128)(2,1)S(1)}, bf16[64,3584]{1,0:T(8,128)(2,1)S(1)}, u32[]{:S(2)}, u32[]{:S(2)}) collective-permute-start(bf16[64,3584]{1,0:T(8,128)(2,1)S(1)} %sum.13.refs_1_), channel_id=1, source_target_pairs={{0,8},{8,16},{16,24},{24,0},{1,9},{9,17},{17,25},{25,1},{2,10},{10... | collective-permute-start | bytes 1376264 | tf_op jit(solution)/shard_map/ppermute | solution.py:296
  113.4 10.4 %collective-permute-start.25 = (bf16[64,3584]{1,0:T(8,128)(2,1)S(1)}, bf16[64,3584]{1,0:T(8,128)(2,1)S(1)}, u32[]{:S(2)}, u32[]{:S(2)}) collective-permute-start(bf16[64,3584]{1,0:T(8,128)(2,1)S(1)} %sum.14.refs_1_), channel_id=1, source_target_pairs={{2,0},{4,2},{6,4},{1,3},{3,5},{5,7},{10,8},{12,10},{14,12},{9,11},... | collective-permute-start | bytes 1376264 | tf_op jit(solution)/shard_map/ppermute | solution.py:35
  118.3 10.4 %collective-permute-start.28 = (bf16[64,3584]{1,0:T(8,128)(2,1)S(1)}, bf16[64,3584]{1,0:T(8,128)(2,1)S(1)}, u32[]{:S(2)}, u32[]{:S(2)}) collective-permute-start(bf16[64,3584]{1,0:T(8,128)(2,1)S(1)} %sum.15.refs_1_), channel_id=1, source_target_pairs={{2,0},{4,2},{6,4},{1,3},{3,5},{5,7},{10,8},{12,10},{14,12},{9,11},... | collective-permute-start | bytes 1376264 | tf_op jit(solution)/shard_map/ppermute | solution.py:35
  123.8 1.6 %collective-permute-start.26 = (bf16[32,3584]{1,0:T(8,128)(2,1)S(1)}, bf16[32,3584]{1,0:T(8,128)(2,1)S(1)}, u32[]{:S(2)}, u32[]{:S(2)}) collective-permute-start(bf16[32,3584]{1,0:T(8,128)(2,1)S(1)} %get-tuple-element.33), channel_id=1, source_target_pairs={{0,1},{1,0},{2,3},{3,2},{4,5},{5,4},{6,7},{7,6},{8,9},{9,8},{10,11... | collective-permute-start | bytes 688136 | tf_op jit(solution)/shard_map/ppermute | solution.py:20
  128.7 1.6 %collective-permute-start.29 = (bf16[32,3584]{1,0:T(8,128)(2,1)S(1)}, bf16[32,3584]{1,0:T(8,128)(2,1)S(1)}, u32[]{:S(2)}, u32[]{:S(2)}) collective-permute-start(bf16[32,3584]{1,0:T(8,128)(2,1)S(1)} %get-tuple-element.31), channel_id=1, source_target_pairs={{0,1},{1,0},{2,3},{3,2},{4,5},{5,4},{6,7},{7,6},{8,9},{9,8},{10,11... | collective-permute-start | bytes 688136 | tf_op jit(solution)/shard_map/ppermute | solution.py:20
  128.8 9.4 %collective-permute-start.27 = (bf16[32,3584]{1,0:T(8,128)(2,1)S(1)}, bf16[32,3584]{1,0:T(8,128)(2,1)S(1)}, u32[]{:S(2)}, u32[]{:S(2)}) collective-permute-start(bf16[32,3584]{1,0:T(8,128)(2,1)S(1)} %sum.16.refs_1_), channel_id=1, source_target_pairs={{0,24},{8,0},{16,8},{24,16},{1,25},{9,1},{17,9},{25,17},{2,26},{10... | collective-permute-start | bytes 688136 | tf_op jit(solution)/shard_map/ppermute | solution.py:296
  130.4 12.2 %collective-permute-start.30 = (bf16[32,3584]{1,0:T(8,128)(2,1)S(1)}, bf16[32,3584]{1,0:T(8,128)(2,1)S(1)}, u32[]{:S(2)}, u32[]{:S(2)}) collective-permute-start(bf16[32,3584]{1,0:T(8,128)(2,1)S(1)} %sum.17), channel_id=1, source_target_pairs={{0,24},{8,0},{16,8},{24,16},{1,25},{9,1},{17,9},{25,17},{2,26},{10... | collective-permute-start | bytes 688136 | tf_op jit(solution)/shard_map/ppermute | solution.py:296

commit v4 on v3

--- a/solution.py
+++ b/solution.py
@@ -67,9 +67,17 @@
         )
 
 
+def load_kernel(up_in, down_in, up_out, down_out, sems):
+    copies = [pltpu.make_async_copy(up_in, up_out, sems.at[0]), pltpu.make_async_copy(down_in, down_out, sems.at[1])]
+    for copy in copies:
+        copy.start()
+    for copy in copies:
+        copy.wait()
+
+
 def begin_kernel(chips, *refs):
-    sources, out, weights, copied, sems = refs[:7], refs[7], refs[8:11], refs[11:15], refs[15]
-    copies = [pltpu.make_async_copy(a, b, sems.at[k]) for k, (a, b) in enumerate(zip(sources, (*copied, *weights)))]
+    sources, out, weight, copied, sems = refs[:5], refs[5], refs[6], refs[7:11], refs[11]
+    copies = [pltpu.make_async_copy(a, b, sems.at[k]) for k, (a, b) in enumerate(zip(sources, (*copied, weight)))]
     for copy in copies:
         copy.start()
     for copy in copies[:4]:
@@ -204,13 +212,22 @@
     def begin(self, chips, *sources):
         streams = sources[0]
         sent = jax.ShapeDtypeStruct((streams.shape[0] * streams.shape[1], streams.shape[2] + TAIL), jnp.bfloat16)
-        sent, gate_w, up_w, down_w = self.order.call(
+        sent, gate_w = self.order.call(
             functools.partial(begin_kernel, chips),
-            [sent] + [pltpu.VMEM(w.shape, w.dtype) for w in self.weights],
-            [ANYWHERE] * 7,
-            [pltpu.with_memory_space_constraint(x, pltpu.HBM) for x in (*sources, *self.weights)],
-            scratch_shapes=[pltpu.VMEM(x.shape, x.dtype) for x in sources] + [pltpu.SemaphoreType.DMA((7,))],
+            [sent] + [pltpu.VMEM(w.shape, w.dtype) for w in self.weights[:1]],
+            [ANYWHERE] * 5,
+            [pltpu.with_memory_space_constraint(x, pltpu.HBM) for x in (*sources, *self.weights[:1])],
+            scratch_shapes=[pltpu.VMEM(x.shape, x.dtype) for x in sources] + [pltpu.SemaphoreType.DMA((5,))],
             name="begin",
+        )
+        up_w, down_w = self.order.call(
+            load_kernel,
+            [pltpu.VMEM(w.shape, w.dtype) for w in self.weights[1:]],
+            [ANYWHERE] * 2,
+            [pltpu.with_memory_space_constraint(x, pltpu.HBM) for x in self.weights[1:]],
+            scratch_shapes=[pltpu.SemaphoreType.DMA((2,))],
+            cost_estimate=pl.CostEstimate(flops=10**11, bytes_accessed=1024, transcendentals=0),
+            name="load",
         )
         self.weights = gate_w, up_w, down_w
         return sent
@@ -332,13 +349,15 @@
     for step in range(last):
         one.gather(step)
     two.depart()
-    for step in range(last):
+    for step in range(1, last):
         one.work(step)
     one.gather(last)
     one.work(last)
     one.send_back()
     for step in range(last):
         two.gather(step)
+        if step == 0:
+            one.work(0)
         if step < last - 1:
             one.go_on(last - 1 - step)
     two.gather(last)

time: 144 us -> 140 us (0.972)
  waiting for transfers between devices: 59.2 us -> 51.1 us
  starting transfers between devices: 54.2 us -> 57 us
    ppermute x9, waiting for transfers between devices: 23 us -> 17.4 us  [reduce_hop(): lax.ppermute(value, 'expert', [(target, source) for source, target in hop...]
    ppermute x7, waiting for transfers between devices: 6.59 us -> 4.1 us  [swap_cores(): return lax.ppermute(value, 'expert', [(i, i ^ 1) for i in range(count)])]
    ppermute x12, starting transfers between devices: 35.6 us -> 38 us  [gather_hop(): return lax.ppermute(value, 'expert', hop_pairs(step))]
    pallas_call x48 -> x49, Pallas kernels: 28.3 us -> 29.3 us  [call(): pl.pallas_call(lambda *refs: kernel(*refs[:count], *refs[count + len(befo...]
  transfers between devices with their start and end apart: 31 -> 31, of which waited for: 21 -> 20; matrix products, arithmetic and copies ran while one was open for 0% -> 0% of each run, Pallas kernels for 16% -> 19%
where the time goes in v4:
time: 140 us; the launch traced here: 139 us
  starting transfers between devices  57 us (41%)
  waiting for transfers between devices  51.1 us (36%)
  Pallas kernels  29.3 us (21%)
    ppermute x12, starting transfers between devices, gather_hop(): return lax.ppermute(value, 'expert', hop_pairs(step))  38 us
    pallas_call x49, Pallas kernels, call(): pl.pallas_call(lambda *refs: kernel(*refs[:count], *refs[count + len(befo...  29.3 us
    ppermute x9, waiting for transfers between devices, reduce_hop(): lax.ppermute(value, 'expert', [(target, source) for source, target in hop...  17.4 us
    ppermute x9, starting transfers between devices, reduce_hop(): lax.ppermute(value, 'expert', [(target, source) for source, target in hop...  15.9 us
    ppermute x12, waiting for transfers between devices, gather_hop(): return lax.ppermute(value, 'expert', hop_pairs(step))  15 us
    ppermute x3, waiting for transfers between devices, finish(): self.shifted.append(lax.ppermute(mixed, 'pipe', self.pairs))  14.6 us
    ppermute x7, waiting for transfers between devices, swap_cores(): return lax.ppermute(value, 'expert', [(i, i ^ 1) for i in range(count)])  4.1 us
  transfers between devices with their start and end apart: 31, of which 20 were waited for; matrix products, arithmetic and copies ran while one was open for 0% of the time, Pallas kernels for 19%

profile of v4, /device:TPU:22, one launch (start us, length us, event | category | flops | bytes accessed | tf_op | source)
XLA Modules:
  0.0 139.3 jit_solution(7501652967405291499)
XLA Ops:
  0.0 2.4 %begin.1 = (bf16[128,3712]{1,0:T(8,128)(2,1)S(1)}, bf16[3584,512]{1,0:T(8,128)(2,1)S(1)}) custom-call(bf16[2,64,3584]{2,1,0:T(8,128)(2,1)} %bitcast.23, f32[1,3584]{1,0:T(1,128)} %refs_1_.1, s32[2,2,64]{2,1,0:T(2,128)} %bitcast.24, f32[2,2,64]{2,1,0:T(2,128)} %bitcast.25, bf16[3584,512]{1,0:T(8,128)(2,1)} %bitcast.22, ...), custom_call_target="tpu_custom_call" | custom-call | flops 1024 | bytes 1024 | tf_op jit(solution)/shard_map/begin/pallas_call | solution.py:48
  2.5 3.2 %load.1 = (bf16[3584,512]{1,0:T(8,128)(2,1)S(1)}, bf16[512,3584]{1,0:T(8,128)(2,1)S(1)}) custom-call(bf16[3584,512]{1,0:T(8,128)(2,1)} %bitcast.26, bf16[512,3584]{1,0:T(8,128)(2,1)} %bitcast.27, bf16[128,3712]{1,0:T(8,128)(2,1)S(1)} %get-tuple-element.15.refs_2_.refs_0_), custom_call_target="tpu_custom_call" | custom-call | flops 99999997952 | bytes 1024 | tf_op jit(solution)/shard_map/load/pallas_call | solution.py:48
  7.0 3.5 %collective-permute-start.5 = (bf16[64,3712]{1,0:T(8,128)(2,1)S(1)}, bf16[64,3712]{1,0:T(8,128)(2,1)S(1)}, u32[]{:S(2)}, u32[]{:S(2)}) collective-permute-start(bf16[64,3712]{1,0:T(8,128)(2,1)S(1)} %stack.16.refs_2_), channel_id=1, source_target_pairs={{0,2},{2,4},{4,6},{3,1},{5,3},{7,5},{8,10},{10,12},{12,14},{11,9},... | collective-permute-start | bytes 1425416 | tf_op jit(solution)/shard_map/ppermute | solution.py:31
  10.5 1.9 %collective-permute-start.4 = (bf16[64,3712]{1,0:T(8,128)(2,1)S(1)}, bf16[64,3712]{1,0:T(8,128)(2,1)S(1)}, u32[]{:S(2)}, u32[]{:S(2)}) collective-permute-start(bf16[64,3712]{1,0:T(8,128)(2,1)S(1)} %stack.17.refs_2_), channel_id=1, source_target_pairs={{0,2},{2,4},{4,6},{3,1},{5,3},{7,5},{8,10},{10,12},{12,14},{11,9},... | collective-permute-start | bytes 1425416 | tf_op jit(solution)/shard_map/ppermute | solution.py:31
  12.4 5.1 %collective-permute-done.5.refs_0_ = bf16[64,3712]{1,0:T(8,128)(2,1)S(1)} collective-permute-done((bf16[64,3712]{1,0:T(8,128)(2,1)S(1)}, bf16[64,3712]{1,0:T(8,128)(2,1)S(1)}, u32[]{:S(2)}, u32[]{:S(2)}) %collective-permute-start.5) | collective-permute-done | bytes 475168 | tf_op jit(solution)/shard_map/ppermute | solution.py:31
  17.5 3.5 %collective-permute-start.7 = (bf16[64,3712]{1,0:T(8,128)(2,1)S(1)}, bf16[64,3712]{1,0:T(8,128)(2,1)S(1)}, u32[]{:S(2)}, u32[]{:S(2)}) collective-permute-start(bf16[64,3712]{1,0:T(8,128)(2,1)S(1)} %arrived.30.refs_1_.refs_0_), channel_id=1, source_target_pairs={{2,4},{4,6},{3,1},{5,3},{10,12},{12,14},{11,9},{13,11},{18,20},{20... | collective-permute-start | bytes 1425416 | tf_op jit(solution)/shard_map/ppermute | solution.py:31
  22.6 3.5 %collective-permute-start.6 = (bf16[64,3712]{1,0:T(8,128)(2,1)S(1)}, bf16[64,3712]{1,0:T(8,128)(2,1)S(1)}, u32[]{:S(2)}, u32[]{:S(2)}) collective-permute-start(bf16[64,3712]{1,0:T(8,128)(2,1)S(1)} %arrived.31.refs_1_), channel_id=1, source_target_pairs={{2,4},{4,6},{3,1},{5,3},{10,12},{12,14},{11,9},{13,11},{18,20},{20... | collective-permute-start | bytes 1425416 | tf_op jit(solution)/shard_map/ppermute | solution.py:31
  26.1 2.0 %collective-permute-done.7.refs_0_ = bf16[64,3712]{1,0:T(8,128)(2,1)S(1)} collective-permute-done((bf16[64,3712]{1,0:T(8,128)(2,1)S(1)}, bf16[64,3712]{1,0:T(8,128)(2,1)S(1)}, u32[]{:S(2)}, u32[]{:S(2)}) %collective-permute-start.7) | collective-permute-done | bytes 475168 | tf_op jit(solution)/shard_map/ppermute | solution.py:31
  28.0 3.5 %collective-permute-start.9 = (bf16[64,3712]{1,0:T(8,128)(2,1)S(1)}, bf16[64,3712]{1,0:T(8,128)(2,1)S(1)}, u32[]{:S(2)}, u32[]{:S(2)}) collective-permute-start(bf16[64,3712]{1,0:T(8,128)(2,1)S(1)} %arrived.32.refs_1_.refs_0_), channel_id=1, source_target_pairs={{4,6},{3,1},{12,14},{11,9},{20,22},{19,17},{28,30},{27,25}} | collective-permute-start | bytes 1425416 | tf_op jit(solution)/shard_map/ppermute | solution.py:31
  33.1 3.5 %collective-permute-start.10 = (bf16[64,3712]{1,0:T(8,128)(2,1)S(1)}, bf16[64,3712]{1,0:T(8,128)(2,1)S(1)}, u32[]{:S(2)}, u32[]{:S(2)}) collective-permute-start(bf16[64,3712]{1,0:T(8,128)(2,1)S(1)} %arrived.33.refs_1_), channel_id=1, source_target_pairs={{4,6},{3,1},{12,14},{11,9},{20,22},{19,17},{28,30},{27,25}} | collective-permute-start | bytes 1425416 | tf_op jit(solution)/shard_map/ppermute | solution.py:31
  36.7 1.9 %collective-permute-start.8 = (bf16[64,3712]{1,0:T(8,128)(2,1)S(1)}, bf16[64,3712]{1,0:T(8,128)(2,1)S(1)}, u32[]{:S(2)}, u32[]{:S(2)}) collective-permute-start(bf16[64,3712]{1,0:T(8,128)(2,1)S(1)} %arrived.34.refs_1_), channel_id=1, source_target_pairs={{0,2},{2,4},{4,6},{3,1},{5,3},{7,5},{8,10},{10,12},{12,14},{11,9},... | collective-permute-start | bytes 1425416 | tf_op jit(solution)/shard_map/ppermute | solution.py:31
  40.6 3.2 %expert.7.refs_1_.refs_0_ = bf16[128,3584]{1,0:T(8,128)(2,1)S(1)} custom-call(bf16[64,3712]{1,0:T(8,128)(2,1)S(1)} %arrived.32.refs_1_.refs_0_, bf16[64,3712]{1,0:T(8,128)(2,1)S(1)} %arrived.33.refs_1_, f32[1,128]{1,0:T(1,128)S(1)} %and_convert_fusion.refs_5_.refs_2_.refs_1_, bf16[3584,512]{1,0:T(8,128)(2,1)S(1)} %arrived.27.refs_1_.refs_3_.refs_2_, ...), custom_call_target="tpu_custom_call" | custom-call | flops 1024 | bytes 1024 | tf_op jit(solution)/shard_map/expert/pallas_call | solution.py:48
  43.8 3.2 %expert.8.refs_1_ = bf16[128,3584]{1,0:T(8,128)(2,1)S(1)} custom-call(bf16[64,3712]{1,0:T(8,128)(2,1)S(1)} %arrived.36.refs_1_.refs_0_, bf16[64,3712]{1,0:T(8,128)(2,1)S(1)} %arrived.37.refs_1_.refs_9_, f32[1,128]{1,0:T(1,128)S(1)} %and_convert_fusion.refs_5_.refs_2_.refs_1_, bf16[3584,512]{1,0:T(8,128)(2,1)S(1)} %arrived.27.refs_1_.refs_3_.refs_2_, ...), custom_call_target="tpu_custom_call" | custom-call | flops 1024 | bytes 1024 | tf_op jit(solution)/shard_map/expert/pallas_call | solution.py:48
  48.3 4.6 %collective-permute-start.12 = (bf16[64,3712]{1,0:T(8,128)(2,1)S(1)}, bf16[64,3712]{1,0:T(8,128)(2,1)S(1)}, u32[]{:S(2)}, u32[]{:S(2)}) collective-permute-start(bf16[64,3712]{1,0:T(8,128)(2,1)S(1)} %arrived.38.refs_1_.refs_0_), channel_id=1, source_target_pairs={{2,4},{4,6},{3,1},{5,3},{10,12},{12,14},{11,9},{13,11},{18,20},{20... | collective-permute-start | bytes 1425416 | tf_op jit(solution)/shard_map/ppermute | solution.py:31
  53.0 4.4 %collective-permute-start.14 = (bf16[64,3712]{1,0:T(8,128)(2,1)S(1)}, bf16[64,3712]{1,0:T(8,128)(2,1)S(1)}, u32[]{:S(2)}, u32[]{:S(2)}) collective-permute-start(bf16[64,3712]{1,0:T(8,128)(2,1)S(1)} %arrived.39.refs_9_.refs_1_), channel_id=1, source_target_pairs={{2,4},{4,6},{3,1},{5,3},{10,12},{12,14},{11,9},{13,11},{18,20},{20... | collective-permute-start | bytes 1425416 | tf_op jit(solution)/shard_map/ppermute | solution.py:31
  57.3 3.2 %expert.9.refs_1_.refs_0_ = bf16[128,3584]{1,0:T(8,128)(2,1)S(1)} custom-call(bf16[64,3712]{1,0:T(8,128)(2,1)S(1)} %arrived.30.refs_1_.refs_0_, bf16[64,3712]{1,0:T(8,128)(2,1)S(1)} %arrived.31.refs_1_, f32[1,128]{1,0:T(1,128)S(1)} %and_convert_fusion.refs_5_.refs_2_.refs_1_, bf16[3584,512]{1,0:T(8,128)(2,1)S(1)} %arrived.27.refs_1_.refs_3_.refs_2_, ...), custom_call_target="tpu_custom_call" | custom-call | flops 1024 | bytes 1024 | tf_op jit(solution)/shard_map/expert/pallas_call | solution.py:48
  64.1 4.4 %collective-permute-start.17 = (bf16[64,3712]{1,0:T(8,128)(2,1)S(1)}, bf16[64,3712]{1,0:T(8,128)(2,1)S(1)}, u32[]{:S(2)}, u32[]{:S(2)}) collective-permute-start(bf16[64,3712]{1,0:T(8,128)(2,1)S(1)} %arrived.42.refs_1_), channel_id=1, source_target_pairs={{4,6},{3,1},{12,14},{11,9},{20,22},{19,17},{28,30},{27,25}} | collective-permute-start | bytes 1425416 | tf_op jit(solution)/shard_map/ppermute | solution.py:31
  68.6 2.1 %collective-permute-start.15 = (bf16[128,3584]{1,0:T(8,128)(2,1)S(1)}, bf16[128,3584]{1,0:T(8,128)(2,1)S(1)}, u32[]{:S(2)}, u32[]{:S(2)}) collective-permute-start(bf16[128,3584]{1,0:T(8,128)(2,1)S(1)} %sum.9.refs_1_), channel_id=1, source_target_pairs={{4,2},{6,4},{1,3},{3,5},{12,10},{14,12},{9,11},{11,13},{20,18},{22... | collective-permute-start | bytes 2752520 | tf_op jit(solution)/shard_map/ppermute | solution.py:35
  70.7 4.5 %collective-permute-done.17.refs_0_ = bf16[64,3712]{1,0:T(8,128)(2,1)S(1)} collective-permute-done((bf16[64,3712]{1,0:T(8,128)(2,1)S(1)}, bf16[64,3712]{1,0:T(8,128)(2,1)S(1)}, u32[]{:S(2)}, u32[]{:S(2)}) %collective-permute-start.17) | collective-permute-done | bytes 475168 | tf_op jit(solution)/shard_map/ppermute | solution.py:31
  75.2 3.2 %expert.10 = (bf16[64,3584]{1,0:T(8,128)(2,1)S(1)}, bf16[64,3584]{1,0:T(8,128)(2,1)S(1)}) custom-call(bf16[64,3712]{1,0:T(8,128)(2,1)S(1)} %arrived.43.refs_1_.refs_0_, bf16[64,3712]{1,0:T(8,128)(2,1)S(1)} %arrived.44.refs_1_.refs_9_, f32[1,128]{1,0:T(1,128)S(1)} %and_convert_fusion.refs_5_.refs_2_.refs_1_, ...), custom_call_target="tpu_custom_call" | custom-call | flops 1024 | bytes 1024 | tf_op jit(solution)/shard_map/expert/pallas_call | solution.py:48
  79.7 4.2 %collective-permute-done.15.refs_0_ = bf16[128,3584]{1,0:T(8,128)(2,1)S(1)} collective-permute-done((bf16[128,3584]{1,0:T(8,128)(2,1)S(1)}, bf16[128,3584]{1,0:T(8,128)(2,1)S(1)}, u32[]{:S(2)}, u32[]{:S(2)}) %collective-permute-start.15) | collective-permute-done | bytes 917536 | tf_op jit(solution)/shard_map/ppermute | solution.py:35
  85.4 2.1 %collective-permute-start.20 = (bf16[128,3584]{1,0:T(8,128)(2,1)S(1)}, bf16[128,3584]{1,0:T(8,128)(2,1)S(1)}, u32[]{:S(2)}, u32[]{:S(2)}) collective-permute-start(bf16[128,3584]{1,0:T(8,128)(2,1)S(1)} %sum.10.refs_9_), channel_id=1, source_target_pairs={{2,0},{4,2},{6,4},{1,3},{3,5},{5,7},{10,8},{12,10},{14,12},{9,11},... | collective-permute-start | bytes 2752520 | tf_op jit(solution)/shard_map/ppermute | solution.py:35
  87.4 3.2 %expert.11 = (bf16[64,3584]{1,0:T(8,128)(2,1)S(1)}, bf16[64,3584]{1,0:T(8,128)(2,1)S(1)}) custom-call(bf16[64,3712]{1,0:T(8,128)(2,1)S(1)} %arrived.41.refs_1_.refs_0_, bf16[64,3712]{1,0:T(8,128)(2,1)S(1)} %arrived.42.refs_1_, f32[1,128]{1,0:T(1,128)S(1)} %and_convert_fusion.refs_5_.refs_2_.refs_1_, bf16[3584,512]{1,0:T(8,128)(2,1)S(1)} %arrived.27.refs_1_.refs_3_.refs_2_, ...), custom_call_target="tpu_custom_call" | custom-call | flops 1024 | bytes 1024 | tf_op jit(solution)/shard_map/expert/pallas_call | solution.py:48
  94.3 2.1 %collective-permute-start.23 = (bf16[64,3584]{1,0:T(8,128)(2,1)S(1)}, bf16[64,3584]{1,0:T(8,128)(2,1)S(1)}, u32[]{:S(2)}, u32[]{:S(2)}) collective-permute-start(bf16[64,3584]{1,0:T(8,128)(2,1)S(1)} %sum.12.refs_9_), channel_id=1, source_target_pairs={{4,2},{6,4},{1,3},{3,5},{12,10},{14,12},{9,11},{11,13},{20,18},{22... | collective-permute-start | bytes 1376264 | tf_op jit(solution)/shard_map/ppermute | solution.py:35
  96.5 3.2 %expert.12 = (bf16[64,3584]{1,0:T(8,128)(2,1)S(1)}, bf16[64,3584]{1,0:T(8,128)(2,1)S(1)}) custom-call(bf16[64,3712]{1,0:T(8,128)(2,1)S(1)} %arrived.38.refs_1_.refs_0_, bf16[64,3712]{1,0:T(8,128)(2,1)S(1)} %arrived.39.refs_9_.refs_1_, f32[1,128]{1,0:T(1,128)S(1)} %and_convert_fusion.refs_5_.refs_2_.refs_1_, ...), custom_call_target="tpu_custom_call" | custom-call | flops 1024 | bytes 1024 | tf_op jit(solution)/shard_map/expert/pallas_call | solution.py:48
  99.7 3.2 %expert.13.refs_1_ = bf16[128,3584]{1,0:T(8,128)(2,1)S(1)} custom-call(bf16[128,3712]{1,0:T(8,128)(2,1)S(1)} %get-tuple-element.15.refs_2_.refs_0_, f32[1,128]{1,0:T(1,128)S(1)} %and_convert_fusion.refs_5_.refs_2_.refs_1_, bf16[3584,512]{1,0:T(8,128)(2,1)S(1)} %arrived.27.refs_1_.refs_3_.refs_2_, bf16[3584,512]{1,0:T(8,128)(2,1)S(1)} %arrived.28.refs_1_.refs_4_.refs_3_, ...), custom_call_target="tpu_custom_call" | custom-call | flops 1024 | bytes 1024 | tf_op jit(solution)/shard_map/expert/pallas_call | solution.py:48
  106.8 2.2 %collective-permute-done.24.refs_0_ = bf16[64,3584]{1,0:T(8,128)(2,1)S(1)} collective-permute-done((bf16[64,3584]{1,0:T(8,128)(2,1)S(1)}, bf16[64,3584]{1,0:T(8,128)(2,1)S(1)}, u32[]{:S(2)}, u32[]{:S(2)}) %collective-permute-start.24) | collective-permute-done | bytes 458784 | tf_op jit(solution)/shard_map/ppermute | solution.py:35
  111.0 2.9 %collective-permute-done.23.refs_0_ = bf16[64,3584]{1,0:T(8,128)(2,1)S(1)} collective-permute-done((bf16[64,3584]{1,0:T(8,128)(2,1)S(1)}, bf16[64,3584]{1,0:T(8,128)(2,1)S(1)}, u32[]{:S(2)}, u32[]{:S(2)}) %collective-permute-start.23) | collective-permute-done | bytes 458784 | tf_op jit(solution)/shard_map/ppermute | solution.py:35
  115.9 3.0 %collective-permute-done.22.refs_0_ = bf16[64,3584]{1,0:T(8,128)(2,1)S(1)} collective-permute-done((bf16[64,3584]{1,0:T(8,128)(2,1)S(1)}, bf16[64,3584]{1,0:T(8,128)(2,1)S(1)}, u32[]{:S(2)}, u32[]{:S(2)}) %collective-permute-start.22) | collective-permute-done | bytes 458784 | tf_op jit(solution)/shard_map/ppermute | solution.py:313
  121.1 3.2 %collective-permute-done.28.refs_0_ = bf16[64,3584]{1,0:T(8,128)(2,1)S(1)} collective-permute-done((bf16[64,3584]{1,0:T(8,128)(2,1)S(1)}, bf16[64,3584]{1,0:T(8,128)(2,1)S(1)}, u32[]{:S(2)}, u32[]{:S(2)}) %collective-permute-start.28) | collective-permute-done | bytes 458784 | tf_op jit(solution)/shard_map/ppermute | solution.py:35
  126.7 7.2 %collective-permute-done.27 = bf16[32,3584]{1,0:T(8,128)(2,1)S(1)} collective-permute-done((bf16[32,3584]{1,0:T(8,128)(2,1)S(1)}, bf16[32,3584]{1,0:T(8,128)(2,1)S(1)}, u32[]{:S(2)}, u32[]{:S(2)}) %collective-permute-start.27) | collective-permute-done | bytes 229408 | tf_op jit(solution)/shard_map/ppermute | solution.py:313
  133.8 4.5 %collective-permute-done.30 = bf16[32,3584]{1,0:T(8,128)(2,1)S(1)} collective-permute-done((bf16[32,3584]{1,0:T(8,128)(2,1)S(1)}, bf16[32,3584]{1,0:T(8,128)(2,1)S(1)}, u32[]{:S(2)}, u32[]{:S(2)}) %collective-permute-start.30) | collective-permute-done | bytes 229408 | tf_op jit(solution)/shard_map/ppermute | solution.py:313
  (91 shorter events, 31.3 us)
Async XLA Ops:
  2.4 3.3 %collective-permute-start = (bf16[128,3712]{1,0:T(8,128)(2,1)S(1)}, bf16[128,3712]{1,0:T(8,128)(2,1)S(1)}, u32[]{:S(2)}, u32[]{:S(2)}) collective-permute-start(bf16[128,3712]{1,0:T(8,128)(2,1)S(1)} %get-tuple-element.15.refs_2_.refs_0_), channel_id=1, source_target_pairs={{0,1},{1,0},{2,3},{3,2},{4,5},{5,4},{6,7},{7,6},{8,9},{9,8},{10,11... | collective-permute-start | bytes 2850824 | tf_op jit(solution)/shard_map/ppermute | solution.py:20
  5.9 30.8 %collective-permute-start.3 = (bf16[512,3584]{1,0:T(8,128)(2,1)S(1)}, bf16[512,3584]{1,0:T(8,128)(2,1)S(1)}, u32[]{:S(2)}, u32[]{:S(2)}) collective-permute-start(bf16[512,3584]{1,0:T(8,128)(2,1)S(1)} %arrived.29.refs_1_.refs_5_.refs_4_), channel_id=1, source_target_pairs={{0,1},{1,0},{2,3},{3,2},{4,5},{5,4},{6,7},{7,6},{8,9},{9,8},{10,11... | collective-permute-start | bytes 11010056 | tf_op jit(solution)/shard_map/ppermute | solution.py:20
  6.5 32.1 %collective-permute-start.2 = (bf16[3584,512]{1,0:T(8,128)(2,1)S(1)}, bf16[3584,512]{1,0:T(8,128)(2,1)S(1)}, u32[]{:S(2)}, u32[]{:S(2)}) collective-permute-start(bf16[3584,512]{1,0:T(8,128)(2,1)S(1)} %arrived.28.refs_1_.refs_4_.refs_3_), channel_id=1, source_target_pairs={{0,1},{1,0},{2,3},{3,2},{4,5},{5,4},{6,7},{7,6},{8,9},{9,8},{10,11... | collective-permute-start | bytes 11010056 | tf_op jit(solution)/shard_map/ppermute | solution.py:20
  6.5 34.0 %collective-permute-start.1 = (bf16[3584,512]{1,0:T(8,128)(2,1)S(1)}, bf16[3584,512]{1,0:T(8,128)(2,1)S(1)}, u32[]{:S(2)}, u32[]{:S(2)}) collective-permute-start(bf16[3584,512]{1,0:T(8,128)(2,1)S(1)} %arrived.27.refs_1_.refs_3_.refs_2_), channel_id=1, source_target_pairs={{0,1},{1,0},{2,3},{3,2},{4,5},{5,4},{6,7},{7,6},{8,9},{9,8},{10,11... | collective-permute-start | bytes 11010056 | tf_op jit(solution)/shard_map/ppermute | solution.py:20
  7.0 10.5 %collective-permute-start.5 = (bf16[64,3712]{1,0:T(8,128)(2,1)S(1)}, bf16[64,3712]{1,0:T(8,128)(2,1)S(1)}, u32[]{:S(2)}, u32[]{:S(2)}) collective-permute-start(bf16[64,3712]{1,0:T(8,128)(2,1)S(1)} %stack.16.refs_2_), channel_id=1, source_target_pairs={{0,2},{2,4},{4,6},{3,1},{5,3},{7,5},{8,10},{10,12},{12,14},{11,9},... | collective-permute-start | bytes 1425416 | tf_op jit(solution)/shard_map/ppermute | solution.py:31
  10.5 12.1 %collective-permute-start.4 = (bf16[64,3712]{1,0:T(8,128)(2,1)S(1)}, bf16[64,3712]{1,0:T(8,128)(2,1)S(1)}, u32[]{:S(2)}, u32[]{:S(2)}) collective-permute-start(bf16[64,3712]{1,0:T(8,128)(2,1)S(1)} %stack.17.refs_2_), channel_id=1, source_target_pairs={{0,2},{2,4},{4,6},{3,1},{5,3},{7,5},{8,10},{10,12},{12,14},{11,9},... | collective-permute-start | bytes 1425416 | tf_op jit(solution)/shard_map/ppermute | solution.py:31
  17.5 10.5 %collective-permute-start.7 = (bf16[64,3712]{1,0:T(8,128)(2,1)S(1)}, bf16[64,3712]{1,0:T(8,128)(2,1)S(1)}, u32[]{:S(2)}, u32[]{:S(2)}) collective-permute-start(bf16[64,3712]{1,0:T(8,128)(2,1)S(1)} %arrived.30.refs_1_.refs_0_), channel_id=1, source_target_pairs={{2,4},{4,6},{3,1},{5,3},{10,12},{12,14},{11,9},{13,11},{18,20},{20... | collective-permute-start | bytes 1425416 | tf_op jit(solution)/shard_map/ppermute | solution.py:31
  22.6 10.5 %collective-permute-start.6 = (bf16[64,3712]{1,0:T(8,128)(2,1)S(1)}, bf16[64,3712]{1,0:T(8,128)(2,1)S(1)}, u32[]{:S(2)}, u32[]{:S(2)}) collective-permute-start(bf16[64,3712]{1,0:T(8,128)(2,1)S(1)} %arrived.31.refs_1_), channel_id=1, source_target_pairs={{2,4},{4,6},{3,1},{5,3},{10,12},{12,14},{11,9},{13,11},{18,20},{20... | collective-permute-start | bytes 1425416 | tf_op jit(solution)/shard_map/ppermute | solution.py:31
  28.0 15.7 %collective-permute-start.9 = (bf16[64,3712]{1,0:T(8,128)(2,1)S(1)}, bf16[64,3712]{1,0:T(8,128)(2,1)S(1)}, u32[]{:S(2)}, u32[]{:S(2)}) collective-permute-start(bf16[64,3712]{1,0:T(8,128)(2,1)S(1)} %arrived.32.refs_1_.refs_0_), channel_id=1, source_target_pairs={{4,6},{3,1},{12,14},{11,9},{20,22},{19,17},{28,30},{27,25}} | collective-permute-start | bytes 1425416 | tf_op jit(solution)/shard_map/ppermute | solution.py:31
  33.1 10.6 %collective-permute-start.10 = (bf16[64,3712]{1,0:T(8,128)(2,1)S(1)}, bf16[64,3712]{1,0:T(8,128)(2,1)S(1)}, u32[]{:S(2)}, u32[]{:S(2)}) collective-permute-start(bf16[64,3712]{1,0:T(8,128)(2,1)S(1)} %arrived.33.refs_1_), channel_id=1, source_target_pairs={{4,6},{3,1},{12,14},{11,9},{20,22},{19,17},{28,30},{27,25}} | collective-permute-start | bytes 1425416 | tf_op jit(solution)/shard_map/ppermute | solution.py:31
  36.7 11.6 %collective-permute-start.8 = (bf16[64,3712]{1,0:T(8,128)(2,1)S(1)}, bf16[64,3712]{1,0:T(8,128)(2,1)S(1)}, u32[]{:S(2)}, u32[]{:S(2)}) collective-permute-start(bf16[64,3712]{1,0:T(8,128)(2,1)S(1)} %arrived.34.refs_1_), channel_id=1, source_target_pairs={{0,2},{2,4},{4,6},{3,1},{5,3},{7,5},{8,10},{10,12},{12,14},{11,9},... | collective-permute-start | bytes 1425416 | tf_op jit(solution)/shard_map/ppermute | solution.py:31
  38.6 14.3 %collective-permute-start.11 = (bf16[64,3712]{1,0:T(8,128)(2,1)S(1)}, bf16[64,3712]{1,0:T(8,128)(2,1)S(1)}, u32[]{:S(2)}, u32[]{:S(2)}) collective-permute-start(bf16[64,3712]{1,0:T(8,128)(2,1)S(1)} %arrived.35.refs_9_), channel_id=1, source_target_pairs={{0,2},{2,4},{4,6},{3,1},{5,3},{7,5},{8,10},{10,12},{12,14},{11,9},... | collective-permute-start | bytes 1425416 | tf_op jit(solution)/shard_map/ppermute | solution.py:31
  47.0 15.3 %collective-permute-start.13 = (bf16[128,3584]{1,0:T(8,128)(2,1)S(1)}, bf16[128,3584]{1,0:T(8,128)(2,1)S(1)}, u32[]{:S(2)}, u32[]{:S(2)}) collective-permute-start(bf16[128,3584]{1,0:T(8,128)(2,1)S(1)} %expert.8.refs_1_), channel_id=1, source_target_pairs={{6,4},{1,3},{14,12},{9,11},{22,20},{17,19},{30,28},{25,27}} | collective-permute-start | bytes 2752520 | tf_op jit(solution)/shard_map/ppermute | solution.py:35
  48.3 14.2 %collective-permute-start.12 = (bf16[64,3712]{1,0:T(8,128)(2,1)S(1)}, bf16[64,3712]{1,0:T(8,128)(2,1)S(1)}, u32[]{:S(2)}, u32[]{:S(2)}) collective-permute-start(bf16[64,3712]{1,0:T(8,128)(2,1)S(1)} %arrived.38.refs_1_.refs_0_), channel_id=1, source_target_pairs={{2,4},{4,6},{3,1},{5,3},{10,12},{12,14},{11,9},{13,11},{18,20},{20... | collective-permute-start | bytes 1425416 | tf_op jit(solution)/shard_map/ppermute | solution.py:31
  53.0 11.2 %collective-permute-start.14 = (bf16[64,3712]{1,0:T(8,128)(2,1)S(1)}, bf16[64,3712]{1,0:T(8,128)(2,1)S(1)}, u32[]{:S(2)}, u32[]{:S(2)}) collective-permute-start(bf16[64,3712]{1,0:T(8,128)(2,1)S(1)} %arrived.39.refs_9_.refs_1_), channel_id=1, source_target_pairs={{2,4},{4,6},{3,1},{5,3},{10,12},{12,14},{11,9},{13,11},{18,20},{20... | collective-permute-start | bytes 1425416 | tf_op jit(solution)/shard_map/ppermute | solution.py:31
  62.5 8.2 %collective-permute-start.16 = (bf16[64,3712]{1,0:T(8,128)(2,1)S(1)}, bf16[64,3712]{1,0:T(8,128)(2,1)S(1)}, u32[]{:S(2)}, u32[]{:S(2)}) collective-permute-start(bf16[64,3712]{1,0:T(8,128)(2,1)S(1)} %arrived.41.refs_1_.refs_0_), channel_id=1, source_target_pairs={{4,6},{3,1},{12,14},{11,9},{20,22},{19,17},{28,30},{27,25}} | collective-permute-start | bytes 1425416 | tf_op jit(solution)/shard_map/ppermute | solution.py:31
  64.1 11.0 %collective-permute-start.17 = (bf16[64,3712]{1,0:T(8,128)(2,1)S(1)}, bf16[64,3712]{1,0:T(8,128)(2,1)S(1)}, u32[]{:S(2)}, u32[]{:S(2)}) collective-permute-start(bf16[64,3712]{1,0:T(8,128)(2,1)S(1)} %arrived.42.refs_1_), channel_id=1, source_target_pairs={{4,6},{3,1},{12,14},{11,9},{20,22},{19,17},{28,30},{27,25}} | collective-permute-start | bytes 1425416 | tf_op jit(solution)/shard_map/ppermute | solution.py:31
  68.6 15.3 %collective-permute-start.15 = (bf16[128,3584]{1,0:T(8,128)(2,1)S(1)}, bf16[128,3584]{1,0:T(8,128)(2,1)S(1)}, u32[]{:S(2)}, u32[]{:S(2)}) collective-permute-start(bf16[128,3584]{1,0:T(8,128)(2,1)S(1)} %sum.9.refs_1_), channel_id=1, source_target_pairs={{4,2},{6,4},{1,3},{3,5},{12,10},{14,12},{9,11},{11,13},{20,18},{22... | collective-permute-start | bytes 2752520 | tf_op jit(solution)/shard_map/ppermute | solution.py:35
  78.4 12.2 %collective-permute-start.19 = (bf16[64,3584]{1,0:T(8,128)(2,1)S(1)}, bf16[64,3584]{1,0:T(8,128)(2,1)S(1)}, u32[]{:S(2)}, u32[]{:S(2)}) collective-permute-start(bf16[64,3584]{1,0:T(8,128)(2,1)S(1)} %get-tuple-element.19.refs_1_), channel_id=1, source_target_pairs={{6,4},{1,3},{14,12},{9,11},{22,20},{17,19},{30,28},{25,27}} | collective-permute-start | bytes 1376264 | tf_op jit(solution)/shard_map/ppermute | solution.py:35
  83.8 10.4 %collective-permute-start.18 = (bf16[64,3584]{1,0:T(8,128)(2,1)S(1)}, bf16[64,3584]{1,0:T(8,128)(2,1)S(1)}, u32[]{:S(2)}, u32[]{:S(2)}) collective-permute-start(bf16[64,3584]{1,0:T(8,128)(2,1)S(1)} %get-tuple-element.21), channel_id=1, source_target_pairs={{6,4},{1,3},{14,12},{9,11},{22,20},{17,19},{30,28},{25,27}} | collective-permute-start | bytes 1376264 | tf_op jit(solution)/shard_map/ppermute | solution.py:35
  85.4 5.3 %copy-start = (bf16[1,2,64,3584]{3,2,1,0:T(8,128)(2,1)S(1)}, bf16[1,2,64,3584]{3,2,1,0:T(8,128)(2,1)}, u32[]{:S(2)}) copy-start(bf16[1,2,64,3584]{3,2,1,0:T(8,128)(2,1)} %param.7) | copy-start | bytes 2752516
  85.4 18.7 %collective-permute-start.20 = (bf16[128,3584]{1,0:T(8,128)(2,1)S(1)}, bf16[128,3584]{1,0:T(8,128)(2,1)S(1)}, u32[]{:S(2)}, u32[]{:S(2)}) collective-permute-start(bf16[128,3584]{1,0:T(8,128)(2,1)S(1)} %sum.10.refs_9_), channel_id=1, source_target_pairs={{2,0},{4,2},{6,4},{1,3},{3,5},{5,7},{10,8},{12,10},{14,12},{9,11},... | collective-permute-start | bytes 2752520 | tf_op jit(solution)/shard_map/ppermute | solution.py:35
  90.8 18.2 %collective-permute-start.24 = (bf16[64,3584]{1,0:T(8,128)(2,1)S(1)}, bf16[64,3584]{1,0:T(8,128)(2,1)S(1)}, u32[]{:S(2)}, u32[]{:S(2)}) collective-permute-start(bf16[64,3584]{1,0:T(8,128)(2,1)S(1)} %sum.11.refs_1_), channel_id=1, source_target_pairs={{4,2},{6,4},{1,3},{3,5},{12,10},{14,12},{9,11},{11,13},{20,18},{22... | collective-permute-start | bytes 1376264 | tf_op jit(solution)/shard_map/ppermute | solution.py:35
  94.3 19.6 %collective-permute-start.23 = (bf16[64,3584]{1,0:T(8,128)(2,1)S(1)}, bf16[64,3584]{1,0:T(8,128)(2,1)S(1)}, u32[]{:S(2)}, u32[]{:S(2)}) collective-permute-start(bf16[64,3584]{1,0:T(8,128)(2,1)S(1)} %sum.12.refs_9_), channel_id=1, source_target_pairs={{4,2},{6,4},{1,3},{3,5},{12,10},{14,12},{9,11},{11,13},{20,18},{22... | collective-permute-start | bytes 1376264 | tf_op jit(solution)/shard_map/ppermute | solution.py:35
  104.1 1.9 %collective-permute-start.21 = (bf16[64,3584]{1,0:T(8,128)(2,1)S(1)}, bf16[64,3584]{1,0:T(8,128)(2,1)S(1)}, u32[]{:S(2)}, u32[]{:S(2)}) collective-permute-start(bf16[64,3584]{1,0:T(8,128)(2,1)S(1)} %pad_maximum_fusion.1), channel_id=1, source_target_pairs={{0,1},{1,0},{2,3},{3,2},{4,5},{5,4},{6,7},{7,6},{8,9},{9,8},{10,11... | collective-permute-start | bytes 1376264 | tf_op jit(solution)/shard_map/ppermute | solution.py:20
  106.3 12.6 %collective-permute-start.22 = (bf16[64,3584]{1,0:T(8,128)(2,1)S(1)}, bf16[64,3584]{1,0:T(8,128)(2,1)S(1)}, u32[]{:S(2)}, u32[]{:S(2)}) collective-permute-start(bf16[64,3584]{1,0:T(8,128)(2,1)S(1)} %sum.13.refs_1_), channel_id=1, source_target_pairs={{0,8},{8,16},{16,24},{24,0},{1,9},{9,17},{17,25},{25,1},{2,10},{10... | collective-permute-start | bytes 1376264 | tf_op jit(solution)/shard_map/ppermute | solution.py:313
  109.1 10.4 %collective-permute-start.25 = (bf16[64,3584]{1,0:T(8,128)(2,1)S(1)}, bf16[64,3584]{1,0:T(8,128)(2,1)S(1)}, u32[]{:S(2)}, u32[]{:S(2)}) collective-permute-start(bf16[64,3584]{1,0:T(8,128)(2,1)S(1)} %sum.14.refs_1_), channel_id=1, source_target_pairs={{2,0},{4,2},{6,4},{1,3},{3,5},{5,7},{10,8},{12,10},{14,12},{9,11},... | collective-permute-start | bytes 1376264 | tf_op jit(solution)/shard_map/ppermute | solution.py:35
  114.0 10.4 %collective-permute-start.28 = (bf16[64,3584]{1,0:T(8,128)(2,1)S(1)}, bf16[64,3584]{1,0:T(8,128)(2,1)S(1)}, u32[]{:S(2)}, u32[]{:S(2)}) collective-permute-start(bf16[64,3584]{1,0:T(8,128)(2,1)S(1)} %sum.15.refs_1_), channel_id=1, source_target_pairs={{2,0},{4,2},{6,4},{1,3},{3,5},{5,7},{10,8},{12,10},{14,12},{9,11},... | collective-permute-start | bytes 1376264 | tf_op jit(solution)/shard_map/ppermute | solution.py:35
  119.5 1.6 %collective-permute-start.26 = (bf16[32,3584]{1,0:T(8,128)(2,1)S(1)}, bf16[32,3584]{1,0:T(8,128)(2,1)S(1)}, u32[]{:S(2)}, u32[]{:S(2)}) collective-permute-start(bf16[32,3584]{1,0:T(8,128)(2,1)S(1)} %get-tuple-element.33), channel_id=1, source_target_pairs={{0,1},{1,0},{2,3},{3,2},{4,5},{5,4},{6,7},{7,6},{8,9},{9,8},{10,11... | collective-permute-start | bytes 688136 | tf_op jit(solution)/shard_map/ppermute | solution.py:20
  124.4 1.6 %collective-permute-start.29 = (bf16[32,3584]{1,0:T(8,128)(2,1)S(1)}, bf16[32,3584]{1,0:T(8,128)(2,1)S(1)}, u32[]{:S(2)}, u32[]{:S(2)}) collective-permute-start(bf16[32,3584]{1,0:T(8,128)(2,1)S(1)} %get-tuple-element.31), channel_id=1, source_target_pairs={{0,1},{1,0},{2,3},{3,2},{4,5},{5,4},{6,7},{7,6},{8,9},{9,8},{10,11... | collective-permute-start | bytes 688136 | tf_op jit(solution)/shard_map/ppermute | solution.py:20
  124.5 9.4 %collective-permute-start.27 = (bf16[32,3584]{1,0:T(8,128)(2,1)S(1)}, bf16[32,3584]{1,0:T(8,128)(2,1)S(1)}, u32[]{:S(2)}, u32[]{:S(2)}) collective-permute-start(bf16[32,3584]{1,0:T(8,128)(2,1)S(1)} %sum.16.refs_1_), channel_id=1, source_target_pairs={{0,24},{8,0},{16,8},{24,16},{1,25},{9,1},{17,9},{25,17},{2,26},{10... | collective-permute-start | bytes 688136 | tf_op jit(solution)/shard_map/ppermute | solution.py:313
  126.1 12.2 %collective-permute-start.30 = (bf16[32,3584]{1,0:T(8,128)(2,1)S(1)}, bf16[32,3584]{1,0:T(8,128)(2,1)S(1)}, u32[]{:S(2)}, u32[]{:S(2)}) collective-permute-start(bf16[32,3584]{1,0:T(8,128)(2,1)S(1)} %sum.17), channel_id=1, source_target_pairs={{0,24},{8,0},{16,8},{24,16},{1,25},{9,1},{17,9},{25,17},{2,26},{10... | collective-permute-start | bytes 688136 | tf_op jit(solution)/shard_map/ppermute | solution.py:313

commit v5 on v4

--- a/solution.py
+++ b/solution.py
@@ -354,13 +354,12 @@
     one.gather(last)
     one.work(last)
     one.send_back()
-    for step in range(last):
+    two.gather(0)
+    one.work(0)
+    for step in range(1, last + 1):
         two.gather(step)
-        if step == 0:
-            one.work(0)
-        if step < last - 1:
-            one.go_on(last - 1 - step)
-    two.gather(last)
+        if step < last:
+            one.go_on(last - step)
     two.work(last)
     two.send_back()
     one.go_on(0)

time: 140 us -> 140 us (level)
  starting transfers between devices: 57 us -> 58.5 us
    ppermute x12, starting transfers between devices: 38 us -> 39.5 us  [gather_hop(): return lax.ppermute(value, 'expert', hop_pairs(step))]
  transfers between devices with their start and end apart: 31 -> 31, of which waited for: 20 -> 19; matrix products, arithmetic and copies ran while one was open for 0% -> 0% of each run, Pallas kernels for 19% -> 19%
where the time goes in v5:
time: 140 us
  starting transfers between devices  58.5 us (42%)
  waiting for transfers between devices  49.9 us (36%)
  Pallas kernels  29.3 us (21%)
    ppermute x12, starting transfers between devices, gather_hop(): return lax.ppermute(value, 'expert', hop_pairs(step))  39.5 us
    pallas_call x49, Pallas kernels, call(): pl.pallas_call(lambda *refs: kernel(*refs[:count], *refs[count + len(befo...  29.3 us
    ppermute x9, waiting for transfers between devices, reduce_hop(): lax.ppermute(value, 'expert', [(target, source) for source, target in hop...  16.4 us
    ppermute x9, starting transfers between devices, reduce_hop(): lax.ppermute(value, 'expert', [(target, source) for source, target in hop...  15.9 us
    ppermute x12, waiting for transfers between devices, gather_hop(): return lax.ppermute(value, 'expert', hop_pairs(step))  14.8 us
    ppermute x3, waiting for transfers between devices, finish(): self.shifted.append(lax.ppermute(mixed, 'pipe', self.pairs))  14.6 us
    ppermute x7, waiting for transfers between devices, swap_cores(): return lax.ppermute(value, 'expert', [(i, i ^ 1) for i in range(count)])  4.1 us
  transfers between devices with their start and end apart: 31, of which 19 were waited for; matrix products, arithmetic and copies ran while one was open for 0% of the time, Pallas kernels for 19%

profile of v5, /device:TPU:22, one launch (start us, length us, event | category | flops | bytes accessed | tf_op | source)
XLA Modules:
  0.0 139.6 jit_solution(2045980174241824852)
XLA Ops:
  0.0 2.4 %begin.1 = (bf16[128,3712]{1,0:T(8,128)(2,1)S(1)}, bf16[3584,512]{1,0:T(8,128)(2,1)S(1)}) custom-call(bf16[2,64,3584]{2,1,0:T(8,128)(2,1)} %bitcast.23, f32[1,3584]{1,0:T(1,128)} %refs_1_.1, s32[2,2,64]{2,1,0:T(2,128)} %bitcast.24, f32[2,2,64]{2,1,0:T(2,128)} %bitcast.25, bf16[3584,512]{1,0:T(8,128)(2,1)} %bitcast.22, ...), custom_call_target="tpu_custom_call" | custom-call | flops 1024 | bytes 1024 | tf_op jit(solution)/shard_map/begin/pallas_call | solution.py:48
  2.5 3.2 %load.1 = (bf16[3584,512]{1,0:T(8,128)(2,1)S(1)}, bf16[512,3584]{1,0:T(8,128)(2,1)S(1)}) custom-call(bf16[3584,512]{1,0:T(8,128)(2,1)} %bitcast.26, bf16[512,3584]{1,0:T(8,128)(2,1)} %bitcast.27, bf16[128,3712]{1,0:T(8,128)(2,1)S(1)} %get-tuple-element.15.refs_2_.refs_0_), custom_call_target="tpu_custom_call" | custom-call | flops 99999997952 | bytes 1024 | tf_op jit(solution)/shard_map/load/pallas_call | solution.py:48
  7.0 3.5 %collective-permute-start.5 = (bf16[64,3712]{1,0:T(8,128)(2,1)S(1)}, bf16[64,3712]{1,0:T(8,128)(2,1)S(1)}, u32[]{:S(2)}, u32[]{:S(2)}) collective-permute-start(bf16[64,3712]{1,0:T(8,128)(2,1)S(1)} %stack.16.refs_2_), channel_id=1, source_target_pairs={{0,2},{2,4},{4,6},{3,1},{5,3},{7,5},{8,10},{10,12},{12,14},{11,9},... | collective-permute-start | bytes 1425416 | tf_op jit(solution)/shard_map/ppermute | solution.py:31
  12.4 5.1 %collective-permute-done.5.refs_0_ = bf16[64,3712]{1,0:T(8,128)(2,1)S(1)} collective-permute-done((bf16[64,3712]{1,0:T(8,128)(2,1)S(1)}, bf16[64,3712]{1,0:T(8,128)(2,1)S(1)}, u32[]{:S(2)}, u32[]{:S(2)}) %collective-permute-start.5) | collective-permute-done | bytes 475168 | tf_op jit(solution)/shard_map/ppermute | solution.py:31
  17.5 3.5 %collective-permute-start.7 = (bf16[64,3712]{1,0:T(8,128)(2,1)S(1)}, bf16[64,3712]{1,0:T(8,128)(2,1)S(1)}, u32[]{:S(2)}, u32[]{:S(2)}) collective-permute-start(bf16[64,3712]{1,0:T(8,128)(2,1)S(1)} %arrived.30.refs_1_.refs_0_), channel_id=1, source_target_pairs={{2,4},{4,6},{3,1},{5,3},{10,12},{12,14},{11,9},{13,11},{18,20},{20... | collective-permute-start | bytes 1425416 | tf_op jit(solution)/shard_map/ppermute | solution.py:31
  22.6 3.5 %collective-permute-start.6 = (bf16[64,3712]{1,0:T(8,128)(2,1)S(1)}, bf16[64,3712]{1,0:T(8,128)(2,1)S(1)}, u32[]{:S(2)}, u32[]{:S(2)}) collective-permute-start(bf16[64,3712]{1,0:T(8,128)(2,1)S(1)} %arrived.31.refs_1_), channel_id=1, source_target_pairs={{2,4},{4,6},{3,1},{5,3},{10,12},{12,14},{11,9},{13,11},{18,20},{20... | collective-permute-start | bytes 1425416 | tf_op jit(solution)/shard_map/ppermute | solution.py:31
  26.1 2.0 %collective-permute-done.7.refs_0_ = bf16[64,3712]{1,0:T(8,128)(2,1)S(1)} collective-permute-done((bf16[64,3712]{1,0:T(8,128)(2,1)S(1)}, bf16[64,3712]{1,0:T(8,128)(2,1)S(1)}, u32[]{:S(2)}, u32[]{:S(2)}) %collective-permute-start.7) | collective-permute-done | bytes 475168 | tf_op jit(solution)/shard_map/ppermute | solution.py:31
  28.0 3.5 %collective-permute-start.9 = (bf16[64,3712]{1,0:T(8,128)(2,1)S(1)}, bf16[64,3712]{1,0:T(8,128)(2,1)S(1)}, u32[]{:S(2)}, u32[]{:S(2)}) collective-permute-start(bf16[64,3712]{1,0:T(8,128)(2,1)S(1)} %arrived.32.refs_1_.refs_0_), channel_id=1, source_target_pairs={{4,6},{3,1},{12,14},{11,9},{20,22},{19,17},{28,30},{27,25}} | collective-permute-start | bytes 1425416 | tf_op jit(solution)/shard_map/ppermute | solution.py:31
  33.1 3.5 %collective-permute-start.10 = (bf16[64,3712]{1,0:T(8,128)(2,1)S(1)}, bf16[64,3712]{1,0:T(8,128)(2,1)S(1)}, u32[]{:S(2)}, u32[]{:S(2)}) collective-permute-start(bf16[64,3712]{1,0:T(8,128)(2,1)S(1)} %arrived.33.refs_1_), channel_id=1, source_target_pairs={{4,6},{3,1},{12,14},{11,9},{20,22},{19,17},{28,30},{27,25}} | collective-permute-start | bytes 1425416 | tf_op jit(solution)/shard_map/ppermute | solution.py:31
  36.7 1.9 %collective-permute-start.8 = (bf16[64,3712]{1,0:T(8,128)(2,1)S(1)}, bf16[64,3712]{1,0:T(8,128)(2,1)S(1)}, u32[]{:S(2)}, u32[]{:S(2)}) collective-permute-start(bf16[64,3712]{1,0:T(8,128)(2,1)S(1)} %arrived.34.refs_1_), channel_id=1, source_target_pairs={{0,2},{2,4},{4,6},{3,1},{5,3},{7,5},{8,10},{10,12},{12,14},{11,9},... | collective-permute-start | bytes 1425416 | tf_op jit(solution)/shard_map/ppermute | solution.py:31
  40.6 3.2 %expert.7.refs_1_.refs_0_ = bf16[128,3584]{1,0:T(8,128)(2,1)S(1)} custom-call(bf16[64,3712]{1,0:T(8,128)(2,1)S(1)} %arrived.32.refs_1_.refs_0_, bf16[64,3712]{1,0:T(8,128)(2,1)S(1)} %arrived.33.refs_1_, f32[1,128]{1,0:T(1,128)S(1)} %and_convert_fusion.refs_5_.refs_2_.refs_1_, bf16[3584,512]{1,0:T(8,128)(2,1)S(1)} %arrived.27.refs_1_.refs_3_.refs_2_, ...), custom_call_target="tpu_custom_call" | custom-call | flops 1024 | bytes 1024 | tf_op jit(solution)/shard_map/expert/pallas_call | solution.py:48
  43.8 3.2 %expert.8.refs_1_ = bf16[128,3584]{1,0:T(8,128)(2,1)S(1)} custom-call(bf16[64,3712]{1,0:T(8,128)(2,1)S(1)} %arrived.36.refs_1_.refs_0_, bf16[64,3712]{1,0:T(8,128)(2,1)S(1)} %arrived.37.refs_1_.refs_9_, f32[1,128]{1,0:T(1,128)S(1)} %and_convert_fusion.refs_5_.refs_2_.refs_1_, bf16[3584,512]{1,0:T(8,128)(2,1)S(1)} %arrived.27.refs_1_.refs_3_.refs_2_, ...), custom_call_target="tpu_custom_call" | custom-call | flops 1024 | bytes 1024 | tf_op jit(solution)/shard_map/expert/pallas_call | solution.py:48
  48.3 4.6 %collective-permute-start.12 = (bf16[64,3712]{1,0:T(8,128)(2,1)S(1)}, bf16[64,3712]{1,0:T(8,128)(2,1)S(1)}, u32[]{:S(2)}, u32[]{:S(2)}) collective-permute-start(bf16[64,3712]{1,0:T(8,128)(2,1)S(1)} %arrived.38.refs_1_.refs_0_), channel_id=1, source_target_pairs={{2,4},{4,6},{3,1},{5,3},{10,12},{12,14},{11,9},{13,11},{18,20},{20... | collective-permute-start | bytes 1425416 | tf_op jit(solution)/shard_map/ppermute | solution.py:31
  53.0 4.4 %collective-permute-start.13 = (bf16[64,3712]{1,0:T(8,128)(2,1)S(1)}, bf16[64,3712]{1,0:T(8,128)(2,1)S(1)}, u32[]{:S(2)}, u32[]{:S(2)}) collective-permute-start(bf16[64,3712]{1,0:T(8,128)(2,1)S(1)} %arrived.39.refs_9_.refs_1_), channel_id=1, source_target_pairs={{2,4},{4,6},{3,1},{5,3},{10,12},{12,14},{11,9},{13,11},{18,20},{20... | collective-permute-start | bytes 1425416 | tf_op jit(solution)/shard_map/ppermute | solution.py:31
  57.3 3.2 %expert.9.refs_1_.refs_0_ = bf16[128,3584]{1,0:T(8,128)(2,1)S(1)} custom-call(bf16[64,3712]{1,0:T(8,128)(2,1)S(1)} %arrived.30.refs_1_.refs_0_, bf16[64,3712]{1,0:T(8,128)(2,1)S(1)} %arrived.31.refs_1_, f32[1,128]{1,0:T(1,128)S(1)} %and_convert_fusion.refs_5_.refs_2_.refs_1_, bf16[3584,512]{1,0:T(8,128)(2,1)S(1)} %arrived.27.refs_1_.refs_3_.refs_2_, ...), custom_call_target="tpu_custom_call" | custom-call | flops 1024 | bytes 1024 | tf_op jit(solution)/shard_map/expert/pallas_call | solution.py:48
  60.5 2.9 %collective-permute-start.16 = (bf16[64,3712]{1,0:T(8,128)(2,1)S(1)}, bf16[64,3712]{1,0:T(8,128)(2,1)S(1)}, u32[]{:S(2)}, u32[]{:S(2)}) collective-permute-start(bf16[64,3712]{1,0:T(8,128)(2,1)S(1)} %arrived.40.refs_1_.refs_0_), channel_id=1, source_target_pairs={{4,6},{3,1},{12,14},{11,9},{20,22},{19,17},{28,30},{27,25}} | collective-permute-start | bytes 1425416 | tf_op jit(solution)/shard_map/ppermute | solution.py:31
  64.1 4.4 %collective-permute-start.17 = (bf16[64,3712]{1,0:T(8,128)(2,1)S(1)}, bf16[64,3712]{1,0:T(8,128)(2,1)S(1)}, u32[]{:S(2)}, u32[]{:S(2)}) collective-permute-start(bf16[64,3712]{1,0:T(8,128)(2,1)S(1)} %arrived.41.refs_1_), channel_id=1, source_target_pairs={{4,6},{3,1},{12,14},{11,9},{20,22},{19,17},{28,30},{27,25}} | collective-permute-start | bytes 1425416 | tf_op jit(solution)/shard_map/ppermute | solution.py:31
  68.8 2.1 %collective-permute-start.15 = (bf16[128,3584]{1,0:T(8,128)(2,1)S(1)}, bf16[128,3584]{1,0:T(8,128)(2,1)S(1)}, u32[]{:S(2)}, u32[]{:S(2)}) collective-permute-start(bf16[128,3584]{1,0:T(8,128)(2,1)S(1)} %sum.9.refs_1_), channel_id=1, source_target_pairs={{4,2},{6,4},{1,3},{3,5},{12,10},{14,12},{9,11},{11,13},{20,18},{22... | collective-permute-start | bytes 2752520 | tf_op jit(solution)/shard_map/ppermute | solution.py:35
  70.9 3.8 %collective-permute-done.17.refs_0_ = bf16[64,3712]{1,0:T(8,128)(2,1)S(1)} collective-permute-done((bf16[64,3712]{1,0:T(8,128)(2,1)S(1)}, bf16[64,3712]{1,0:T(8,128)(2,1)S(1)}, u32[]{:S(2)}, u32[]{:S(2)}) %collective-permute-start.17) | collective-permute-done | bytes 475168 | tf_op jit(solution)/shard_map/ppermute | solution.py:31
  74.7 3.2 %expert.10 = (bf16[64,3584]{1,0:T(8,128)(2,1)S(1)}, bf16[64,3584]{1,0:T(8,128)(2,1)S(1)}) custom-call(bf16[64,3712]{1,0:T(8,128)(2,1)S(1)} %arrived.43.refs_1_.refs_0_, bf16[64,3712]{1,0:T(8,128)(2,1)S(1)} %arrived.44.refs_1_.refs_9_, f32[1,128]{1,0:T(1,128)S(1)} %and_convert_fusion.refs_5_.refs_2_.refs_1_, ...), custom_call_target="tpu_custom_call" | custom-call | flops 1024 | bytes 1024 | tf_op jit(solution)/shard_map/expert/pallas_call | solution.py:48
  79.2 4.9 %collective-permute-done.15.refs_0_ = bf16[128,3584]{1,0:T(8,128)(2,1)S(1)} collective-permute-done((bf16[128,3584]{1,0:T(8,128)(2,1)S(1)}, bf16[128,3584]{1,0:T(8,128)(2,1)S(1)}, u32[]{:S(2)}, u32[]{:S(2)}) %collective-permute-start.15) | collective-permute-done | bytes 917536 | tf_op jit(solution)/shard_map/ppermute | solution.py:35
  85.6 2.1 %collective-permute-start.20 = (bf16[128,3584]{1,0:T(8,128)(2,1)S(1)}, bf16[128,3584]{1,0:T(8,128)(2,1)S(1)}, u32[]{:S(2)}, u32[]{:S(2)}) collective-permute-start(bf16[128,3584]{1,0:T(8,128)(2,1)S(1)} %sum.10.refs_9_), channel_id=1, source_target_pairs={{2,0},{4,2},{6,4},{1,3},{3,5},{5,7},{10,8},{12,10},{14,12},{9,11},... | collective-permute-start | bytes 2752520 | tf_op jit(solution)/shard_map/ppermute | solution.py:35
  87.7 3.2 %expert.11 = (bf16[64,3584]{1,0:T(8,128)(2,1)S(1)}, bf16[64,3584]{1,0:T(8,128)(2,1)S(1)}) custom-call(bf16[64,3712]{1,0:T(8,128)(2,1)S(1)} %arrived.40.refs_1_.refs_0_, bf16[64,3712]{1,0:T(8,128)(2,1)S(1)} %arrived.41.refs_1_, f32[1,128]{1,0:T(1,128)S(1)} %and_convert_fusion.refs_5_.refs_2_.refs_1_, bf16[3584,512]{1,0:T(8,128)(2,1)S(1)} %arrived.27.refs_1_.refs_3_.refs_2_, ...), custom_call_target="tpu_custom_call" | custom-call | flops 1024 | bytes 1024 | tf_op jit(solution)/shard_map/expert/pallas_call | solution.py:48
  94.6 2.1 %collective-permute-start.23 = (bf16[64,3584]{1,0:T(8,128)(2,1)S(1)}, bf16[64,3584]{1,0:T(8,128)(2,1)S(1)}, u32[]{:S(2)}, u32[]{:S(2)}) collective-permute-start(bf16[64,3584]{1,0:T(8,128)(2,1)S(1)} %sum.12.refs_9_), channel_id=1, source_target_pairs={{4,2},{6,4},{1,3},{3,5},{12,10},{14,12},{9,11},{11,13},{20,18},{22... | collective-permute-start | bytes 1376264 | tf_op jit(solution)/shard_map/ppermute | solution.py:35
  96.7 3.2 %expert.12 = (bf16[64,3584]{1,0:T(8,128)(2,1)S(1)}, bf16[64,3584]{1,0:T(8,128)(2,1)S(1)}) custom-call(bf16[64,3712]{1,0:T(8,128)(2,1)S(1)} %arrived.38.refs_1_.refs_0_, bf16[64,3712]{1,0:T(8,128)(2,1)S(1)} %arrived.39.refs_9_.refs_1_, f32[1,128]{1,0:T(1,128)S(1)} %and_convert_fusion.refs_5_.refs_2_.refs_1_, ...), custom_call_target="tpu_custom_call" | custom-call | flops 1024 | bytes 1024 | tf_op jit(solution)/shard_map/expert/pallas_call | solution.py:48
  99.9 3.2 %expert.13.refs_1_ = bf16[128,3584]{1,0:T(8,128)(2,1)S(1)} custom-call(bf16[128,3712]{1,0:T(8,128)(2,1)S(1)} %get-tuple-element.15.refs_2_.refs_0_, f32[1,128]{1,0:T(1,128)S(1)} %and_convert_fusion.refs_5_.refs_2_.refs_1_, bf16[3584,512]{1,0:T(8,128)(2,1)S(1)} %arrived.27.refs_1_.refs_3_.refs_2_, bf16[3584,512]{1,0:T(8,128)(2,1)S(1)} %arrived.28.refs_1_.refs_4_.refs_3_, ...), custom_call_target="tpu_custom_call" | custom-call | flops 1024 | bytes 1024 | tf_op jit(solution)/shard_map/expert/pallas_call | solution.py:48
  107.0 2.2 %collective-permute-done.24.refs_0_ = bf16[64,3584]{1,0:T(8,128)(2,1)S(1)} collective-permute-done((bf16[64,3584]{1,0:T(8,128)(2,1)S(1)}, bf16[64,3584]{1,0:T(8,128)(2,1)S(1)}, u32[]{:S(2)}, u32[]{:S(2)}) %collective-permute-start.24) | collective-permute-done | bytes 458784 | tf_op jit(solution)/shard_map/ppermute | solution.py:35
  111.2 2.9 %collective-permute-done.23.refs_0_ = bf16[64,3584]{1,0:T(8,128)(2,1)S(1)} collective-permute-done((bf16[64,3584]{1,0:T(8,128)(2,1)S(1)}, bf16[64,3584]{1,0:T(8,128)(2,1)S(1)}, u32[]{:S(2)}, u32[]{:S(2)}) %collective-permute-start.23) | collective-permute-done | bytes 458784 | tf_op jit(solution)/shard_map/ppermute | solution.py:35
  116.1 3.0 %collective-permute-done.22.refs_0_ = bf16[64,3584]{1,0:T(8,128)(2,1)S(1)} collective-permute-done((bf16[64,3584]{1,0:T(8,128)(2,1)S(1)}, bf16[64,3584]{1,0:T(8,128)(2,1)S(1)}, u32[]{:S(2)}, u32[]{:S(2)}) %collective-permute-start.22) | collective-permute-done | bytes 458784 | tf_op jit(solution)/shard_map/ppermute | solution.py:313
  121.4 3.2 %collective-permute-done.28.refs_0_ = bf16[64,3584]{1,0:T(8,128)(2,1)S(1)} collective-permute-done((bf16[64,3584]{1,0:T(8,128)(2,1)S(1)}, bf16[64,3584]{1,0:T(8,128)(2,1)S(1)}, u32[]{:S(2)}, u32[]{:S(2)}) %collective-permute-start.28) | collective-permute-done | bytes 458784 | tf_op jit(solution)/shard_map/ppermute | solution.py:35
  126.9 7.2 %collective-permute-done.27 = bf16[32,3584]{1,0:T(8,128)(2,1)S(1)} collective-permute-done((bf16[32,3584]{1,0:T(8,128)(2,1)S(1)}, bf16[32,3584]{1,0:T(8,128)(2,1)S(1)}, u32[]{:S(2)}, u32[]{:S(2)}) %collective-permute-start.27) | collective-permute-done | bytes 229408 | tf_op jit(solution)/shard_map/ppermute | solution.py:313
  134.1 4.5 %collective-permute-done.30 = bf16[32,3584]{1,0:T(8,128)(2,1)S(1)} collective-permute-done((bf16[32,3584]{1,0:T(8,128)(2,1)S(1)}, bf16[32,3584]{1,0:T(8,128)(2,1)S(1)}, u32[]{:S(2)}, u32[]{:S(2)}) %collective-permute-start.30) | collective-permute-done | bytes 229408 | tf_op jit(solution)/shard_map/ppermute | solution.py:313
  (91 shorter events, 30.6 us)
Async XLA Ops:
  2.4 3.3 %collective-permute-start = (bf16[128,3712]{1,0:T(8,128)(2,1)S(1)}, bf16[128,3712]{1,0:T(8,128)(2,1)S(1)}, u32[]{:S(2)}, u32[]{:S(2)}) collective-permute-start(bf16[128,3712]{1,0:T(8,128)(2,1)S(1)} %get-tuple-element.15.refs_2_.refs_0_), channel_id=1, source_target_pairs={{0,1},{1,0},{2,3},{3,2},{4,5},{5,4},{6,7},{7,6},{8,9},{9,8},{10,11... | collective-permute-start | bytes 2850824 | tf_op jit(solution)/shard_map/ppermute | solution.py:20
  5.9 30.8 %collective-permute-start.3 = (bf16[512,3584]{1,0:T(8,128)(2,1)S(1)}, bf16[512,3584]{1,0:T(8,128)(2,1)S(1)}, u32[]{:S(2)}, u32[]{:S(2)}) collective-permute-start(bf16[512,3584]{1,0:T(8,128)(2,1)S(1)} %arrived.29.refs_1_.refs_5_.refs_4_), channel_id=1, source_target_pairs={{0,1},{1,0},{2,3},{3,2},{4,5},{5,4},{6,7},{7,6},{8,9},{9,8},{10,11... | collective-permute-start | bytes 11010056 | tf_op jit(solution)/shard_map/ppermute | solution.py:20
  6.5 32.1 %collective-permute-start.2 = (bf16[3584,512]{1,0:T(8,128)(2,1)S(1)}, bf16[3584,512]{1,0:T(8,128)(2,1)S(1)}, u32[]{:S(2)}, u32[]{:S(2)}) collective-permute-start(bf16[3584,512]{1,0:T(8,128)(2,1)S(1)} %arrived.28.refs_1_.refs_4_.refs_3_), channel_id=1, source_target_pairs={{0,1},{1,0},{2,3},{3,2},{4,5},{5,4},{6,7},{7,6},{8,9},{9,8},{10,11... | collective-permute-start | bytes 11010056 | tf_op jit(solution)/shard_map/ppermute | solution.py:20
  6.5 34.0 %collective-permute-start.1 = (bf16[3584,512]{1,0:T(8,128)(2,1)S(1)}, bf16[3584,512]{1,0:T(8,128)(2,1)S(1)}, u32[]{:S(2)}, u32[]{:S(2)}) collective-permute-start(bf16[3584,512]{1,0:T(8,128)(2,1)S(1)} %arrived.27.refs_1_.refs_3_.refs_2_), channel_id=1, source_target_pairs={{0,1},{1,0},{2,3},{3,2},{4,5},{5,4},{6,7},{7,6},{8,9},{9,8},{10,11... | collective-permute-start | bytes 11010056 | tf_op jit(solution)/shard_map/ppermute | solution.py:20
  7.0 10.5 %collective-permute-start.5 = (bf16[64,3712]{1,0:T(8,128)(2,1)S(1)}, bf16[64,3712]{1,0:T(8,128)(2,1)S(1)}, u32[]{:S(2)}, u32[]{:S(2)}) collective-permute-start(bf16[64,3712]{1,0:T(8,128)(2,1)S(1)} %stack.16.refs_2_), channel_id=1, source_target_pairs={{0,2},{2,4},{4,6},{3,1},{5,3},{7,5},{8,10},{10,12},{12,14},{11,9},... | collective-permute-start | bytes 1425416 | tf_op jit(solution)/shard_map/ppermute | solution.py:31
  10.5 12.1 %collective-permute-start.4 = (bf16[64,3712]{1,0:T(8,128)(2,1)S(1)}, bf16[64,3712]{1,0:T(8,128)(2,1)S(1)}, u32[]{:S(2)}, u32[]{:S(2)}) collective-permute-start(bf16[64,3712]{1,0:T(8,128)(2,1)S(1)} %stack.17.refs_2_), channel_id=1, source_target_pairs={{0,2},{2,4},{4,6},{3,1},{5,3},{7,5},{8,10},{10,12},{12,14},{11,9},... | collective-permute-start | bytes 1425416 | tf_op jit(solution)/shard_map/ppermute | solution.py:31
  17.5 10.5 %collective-permute-start.7 = (bf16[64,3712]{1,0:T(8,128)(2,1)S(1)}, bf16[64,3712]{1,0:T(8,128)(2,1)S(1)}, u32[]{:S(2)}, u32[]{:S(2)}) collective-permute-start(bf16[64,3712]{1,0:T(8,128)(2,1)S(1)} %arrived.30.refs_1_.refs_0_), channel_id=1, source_target_pairs={{2,4},{4,6},{3,1},{5,3},{10,12},{12,14},{11,9},{13,11},{18,20},{20... | collective-permute-start | bytes 1425416 | tf_op jit(solution)/shard_map/ppermute | solution.py:31
  22.6 10.5 %collective-permute-start.6 = (bf16[64,3712]{1,0:T(8,128)(2,1)S(1)}, bf16[64,3712]{1,0:T(8,128)(2,1)S(1)}, u32[]{:S(2)}, u32[]{:S(2)}) collective-permute-start(bf16[64,3712]{1,0:T(8,128)(2,1)S(1)} %arrived.31.refs_1_), channel_id=1, source_target_pairs={{2,4},{4,6},{3,1},{5,3},{10,12},{12,14},{11,9},{13,11},{18,20},{20... | collective-permute-start | bytes 1425416 | tf_op jit(solution)/shard_map/ppermute | solution.py:31
  28.0 15.7 %collective-permute-start.9 = (bf16[64,3712]{1,0:T(8,128)(2,1)S(1)}, bf16[64,3712]{1,0:T(8,128)(2,1)S(1)}, u32[]{:S(2)}, u32[]{:S(2)}) collective-permute-start(bf16[64,3712]{1,0:T(8,128)(2,1)S(1)} %arrived.32.refs_1_.refs_0_), channel_id=1, source_target_pairs={{4,6},{3,1},{12,14},{11,9},{20,22},{19,17},{28,30},{27,25}} | collective-permute-start | bytes 1425416 | tf_op jit(solution)/shard_map/ppermute | solution.py:31
  33.1 10.6 %collective-permute-start.10 = (bf16[64,3712]{1,0:T(8,128)(2,1)S(1)}, bf16[64,3712]{1,0:T(8,128)(2,1)S(1)}, u32[]{:S(2)}, u32[]{:S(2)}) collective-permute-start(bf16[64,3712]{1,0:T(8,128)(2,1)S(1)} %arrived.33.refs_1_), channel_id=1, source_target_pairs={{4,6},{3,1},{12,14},{11,9},{20,22},{19,17},{28,30},{27,25}} | collective-permute-start | bytes 1425416 | tf_op jit(solution)/shard_map/ppermute | solution.py:31
  36.7 11.6 %collective-permute-start.8 = (bf16[64,3712]{1,0:T(8,128)(2,1)S(1)}, bf16[64,3712]{1,0:T(8,128)(2,1)S(1)}, u32[]{:S(2)}, u32[]{:S(2)}) collective-permute-start(bf16[64,3712]{1,0:T(8,128)(2,1)S(1)} %arrived.34.refs_1_), channel_id=1, source_target_pairs={{0,2},{2,4},{4,6},{3,1},{5,3},{7,5},{8,10},{10,12},{12,14},{11,9},... | collective-permute-start | bytes 1425416 | tf_op jit(solution)/shard_map/ppermute | solution.py:31
  38.6 14.3 %collective-permute-start.11 = (bf16[64,3712]{1,0:T(8,128)(2,1)S(1)}, bf16[64,3712]{1,0:T(8,128)(2,1)S(1)}, u32[]{:S(2)}, u32[]{:S(2)}) collective-permute-start(bf16[64,3712]{1,0:T(8,128)(2,1)S(1)} %arrived.35.refs_9_), channel_id=1, source_target_pairs={{0,2},{2,4},{4,6},{3,1},{5,3},{7,5},{8,10},{10,12},{12,14},{11,9},... | collective-permute-start | bytes 1425416 | tf_op jit(solution)/shard_map/ppermute | solution.py:31
  47.0 21.6 %collective-permute-start.14 = (bf16[128,3584]{1,0:T(8,128)(2,1)S(1)}, bf16[128,3584]{1,0:T(8,128)(2,1)S(1)}, u32[]{:S(2)}, u32[]{:S(2)}) collective-permute-start(bf16[128,3584]{1,0:T(8,128)(2,1)S(1)} %expert.8.refs_1_), channel_id=1, source_target_pairs={{6,4},{1,3},{14,12},{9,11},{22,20},{17,19},{30,28},{25,27}} | collective-permute-start | bytes 2752520 | tf_op jit(solution)/shard_map/ppermute | solution.py:35
  48.3 12.2 %collective-permute-start.12 = (bf16[64,3712]{1,0:T(8,128)(2,1)S(1)}, bf16[64,3712]{1,0:T(8,128)(2,1)S(1)}, u32[]{:S(2)}, u32[]{:S(2)}) collective-permute-start(bf16[64,3712]{1,0:T(8,128)(2,1)S(1)} %arrived.38.refs_1_.refs_0_), channel_id=1, source_target_pairs={{2,4},{4,6},{3,1},{5,3},{10,12},{12,14},{11,9},{13,11},{18,20},{20... | collective-permute-start | bytes 1425416 | tf_op jit(solution)/shard_map/ppermute | solution.py:31
  53.0 11.2 %collective-permute-start.13 = (bf16[64,3712]{1,0:T(8,128)(2,1)S(1)}, bf16[64,3712]{1,0:T(8,128)(2,1)S(1)}, u32[]{:S(2)}, u32[]{:S(2)}) collective-permute-start(bf16[64,3712]{1,0:T(8,128)(2,1)S(1)} %arrived.39.refs_9_.refs_1_), channel_id=1, source_target_pairs={{2,4},{4,6},{3,1},{5,3},{10,12},{12,14},{11,9},{13,11},{18,20},{20... | collective-permute-start | bytes 1425416 | tf_op jit(solution)/shard_map/ppermute | solution.py:31
  60.5 10.4 %collective-permute-start.16 = (bf16[64,3712]{1,0:T(8,128)(2,1)S(1)}, bf16[64,3712]{1,0:T(8,128)(2,1)S(1)}, u32[]{:S(2)}, u32[]{:S(2)}) collective-permute-start(bf16[64,3712]{1,0:T(8,128)(2,1)S(1)} %arrived.40.refs_1_.refs_0_), channel_id=1, source_target_pairs={{4,6},{3,1},{12,14},{11,9},{20,22},{19,17},{28,30},{27,25}} | collective-permute-start | bytes 1425416 | tf_op jit(solution)/shard_map/ppermute | solution.py:31
  64.1 10.5 %collective-permute-start.17 = (bf16[64,3712]{1,0:T(8,128)(2,1)S(1)}, bf16[64,3712]{1,0:T(8,128)(2,1)S(1)}, u32[]{:S(2)}, u32[]{:S(2)}) collective-permute-start(bf16[64,3712]{1,0:T(8,128)(2,1)S(1)} %arrived.41.refs_1_), channel_id=1, source_target_pairs={{4,6},{3,1},{12,14},{11,9},{20,22},{19,17},{28,30},{27,25}} | collective-permute-start | bytes 1425416 | tf_op jit(solution)/shard_map/ppermute | solution.py:31
  68.8 15.3 %collective-permute-start.15 = (bf16[128,3584]{1,0:T(8,128)(2,1)S(1)}, bf16[128,3584]{1,0:T(8,128)(2,1)S(1)}, u32[]{:S(2)}, u32[]{:S(2)}) collective-permute-start(bf16[128,3584]{1,0:T(8,128)(2,1)S(1)} %sum.9.refs_1_), channel_id=1, source_target_pairs={{4,2},{6,4},{1,3},{3,5},{12,10},{14,12},{9,11},{11,13},{20,18},{22... | collective-permute-start | bytes 2752520 | tf_op jit(solution)/shard_map/ppermute | solution.py:35
  77.9 13.0 %collective-permute-start.19 = (bf16[64,3584]{1,0:T(8,128)(2,1)S(1)}, bf16[64,3584]{1,0:T(8,128)(2,1)S(1)}, u32[]{:S(2)}, u32[]{:S(2)}) collective-permute-start(bf16[64,3584]{1,0:T(8,128)(2,1)S(1)} %get-tuple-element.19.refs_1_), channel_id=1, source_target_pairs={{6,4},{1,3},{14,12},{9,11},{22,20},{17,19},{30,28},{25,27}} | collective-permute-start | bytes 1376264 | tf_op jit(solution)/shard_map/ppermute | solution.py:35
  84.1 10.4 %collective-permute-start.18 = (bf16[64,3584]{1,0:T(8,128)(2,1)S(1)}, bf16[64,3584]{1,0:T(8,128)(2,1)S(1)}, u32[]{:S(2)}, u32[]{:S(2)}) collective-permute-start(bf16[64,3584]{1,0:T(8,128)(2,1)S(1)} %get-tuple-element.21), channel_id=1, source_target_pairs={{6,4},{1,3},{14,12},{9,11},{22,20},{17,19},{30,28},{25,27}} | collective-permute-start | bytes 1376264 | tf_op jit(solution)/shard_map/ppermute | solution.py:35
  85.6 5.3 %copy-start = (bf16[1,2,64,3584]{3,2,1,0:T(8,128)(2,1)S(1)}, bf16[1,2,64,3584]{3,2,1,0:T(8,128)(2,1)}, u32[]{:S(2)}) copy-start(bf16[1,2,64,3584]{3,2,1,0:T(8,128)(2,1)} %param.7) | copy-start | bytes 2752516
  85.6 18.7 %collective-permute-start.20 = (bf16[128,3584]{1,0:T(8,128)(2,1)S(1)}, bf16[128,3584]{1,0:T(8,128)(2,1)S(1)}, u32[]{:S(2)}, u32[]{:S(2)}) collective-permute-start(bf16[128,3584]{1,0:T(8,128)(2,1)S(1)} %sum.10.refs_9_), channel_id=1, source_target_pairs={{2,0},{4,2},{6,4},{1,3},{3,5},{5,7},{10,8},{12,10},{14,12},{9,11},... | collective-permute-start | bytes 2752520 | tf_op jit(solution)/shard_map/ppermute | solution.py:35
  91.0 18.2 %collective-permute-start.24 = (bf16[64,3584]{1,0:T(8,128)(2,1)S(1)}, bf16[64,3584]{1,0:T(8,128)(2,1)S(1)}, u32[]{:S(2)}, u32[]{:S(2)}) collective-permute-start(bf16[64,3584]{1,0:T(8,128)(2,1)S(1)} %sum.11.refs_1_), channel_id=1, source_target_pairs={{4,2},{6,4},{1,3},{3,5},{12,10},{14,12},{9,11},{11,13},{20,18},{22... | collective-permute-start | bytes 1376264 | tf_op jit(solution)/shard_map/ppermute | solution.py:35
  94.6 19.6 %collective-permute-start.23 = (bf16[64,3584]{1,0:T(8,128)(2,1)S(1)}, bf16[64,3584]{1,0:T(8,128)(2,1)S(1)}, u32[]{:S(2)}, u32[]{:S(2)}) collective-permute-start(bf16[64,3584]{1,0:T(8,128)(2,1)S(1)} %sum.12.refs_9_), channel_id=1, source_target_pairs={{4,2},{6,4},{1,3},{3,5},{12,10},{14,12},{9,11},{11,13},{20,18},{22... | collective-permute-start | bytes 1376264 | tf_op jit(solution)/shard_map/ppermute | solution.py:35
  104.4 1.9 %collective-permute-start.21 = (bf16[64,3584]{1,0:T(8,128)(2,1)S(1)}, bf16[64,3584]{1,0:T(8,128)(2,1)S(1)}, u32[]{:S(2)}, u32[]{:S(2)}) collective-permute-start(bf16[64,3584]{1,0:T(8,128)(2,1)S(1)} %pad_maximum_fusion.1), channel_id=1, source_target_pairs={{0,1},{1,0},{2,3},{3,2},{4,5},{5,4},{6,7},{7,6},{8,9},{9,8},{10,11... | collective-permute-start | bytes 1376264 | tf_op jit(solution)/shard_map/ppermute | solution.py:20
  106.5 12.6 %collective-permute-start.22 = (bf16[64,3584]{1,0:T(8,128)(2,1)S(1)}, bf16[64,3584]{1,0:T(8,128)(2,1)S(1)}, u32[]{:S(2)}, u32[]{:S(2)}) collective-permute-start(bf16[64,3584]{1,0:T(8,128)(2,1)S(1)} %sum.13.refs_1_), channel_id=1, source_target_pairs={{0,8},{8,16},{16,24},{24,0},{1,9},{9,17},{17,25},{25,1},{2,10},{10... | collective-permute-start | bytes 1376264 | tf_op jit(solution)/shard_map/ppermute | solution.py:313
  109.3 10.4 %collective-permute-start.25 = (bf16[64,3584]{1,0:T(8,128)(2,1)S(1)}, bf16[64,3584]{1,0:T(8,128)(2,1)S(1)}, u32[]{:S(2)}, u32[]{:S(2)}) collective-permute-start(bf16[64,3584]{1,0:T(8,128)(2,1)S(1)} %sum.14.refs_1_), channel_id=1, source_target_pairs={{2,0},{4,2},{6,4},{1,3},{3,5},{5,7},{10,8},{12,10},{14,12},{9,11},... | collective-permute-start | bytes 1376264 | tf_op jit(solution)/shard_map/ppermute | solution.py:35
  114.2 10.4 %collective-permute-start.28 = (bf16[64,3584]{1,0:T(8,128)(2,1)S(1)}, bf16[64,3584]{1,0:T(8,128)(2,1)S(1)}, u32[]{:S(2)}, u32[]{:S(2)}) collective-permute-start(bf16[64,3584]{1,0:T(8,128)(2,1)S(1)} %sum.15.refs_1_), channel_id=1, source_target_pairs={{2,0},{4,2},{6,4},{1,3},{3,5},{5,7},{10,8},{12,10},{14,12},{9,11},... | collective-permute-start | bytes 1376264 | tf_op jit(solution)/shard_map/ppermute | solution.py:35
  119.7 1.6 %collective-permute-start.26 = (bf16[32,3584]{1,0:T(8,128)(2,1)S(1)}, bf16[32,3584]{1,0:T(8,128)(2,1)S(1)}, u32[]{:S(2)}, u32[]{:S(2)}) collective-permute-start(bf16[32,3584]{1,0:T(8,128)(2,1)S(1)} %get-tuple-element.33), channel_id=1, source_target_pairs={{0,1},{1,0},{2,3},{3,2},{4,5},{5,4},{6,7},{7,6},{8,9},{9,8},{10,11... | collective-permute-start | bytes 688136 | tf_op jit(solution)/shard_map/ppermute | solution.py:20
  124.6 1.6 %collective-permute-start.29 = (bf16[32,3584]{1,0:T(8,128)(2,1)S(1)}, bf16[32,3584]{1,0:T(8,128)(2,1)S(1)}, u32[]{:S(2)}, u32[]{:S(2)}) collective-permute-start(bf16[32,3584]{1,0:T(8,128)(2,1)S(1)} %get-tuple-element.31), channel_id=1, source_target_pairs={{0,1},{1,0},{2,3},{3,2},{4,5},{5,4},{6,7},{7,6},{8,9},{9,8},{10,11... | collective-permute-start | bytes 688136 | tf_op jit(solution)/shard_map/ppermute | solution.py:20
  124.7 9.4 %collective-permute-start.27 = (bf16[32,3584]{1,0:T(8,128)(2,1)S(1)}, bf16[32,3584]{1,0:T(8,128)(2,1)S(1)}, u32[]{:S(2)}, u32[]{:S(2)}) collective-permute-start(bf16[32,3584]{1,0:T(8,128)(2,1)S(1)} %sum.16.refs_1_), channel_id=1, source_target_pairs={{0,24},{8,0},{16,8},{24,16},{1,25},{9,1},{17,9},{25,17},{2,26},{10... | collective-permute-start | bytes 688136 | tf_op jit(solution)/shard_map/ppermute | solution.py:313
  126.3 12.2 %collective-permute-start.30 = (bf16[32,3584]{1,0:T(8,128)(2,1)S(1)}, bf16[32,3584]{1,0:T(8,128)(2,1)S(1)}, u32[]{:S(2)}, u32[]{:S(2)}) collective-permute-start(bf16[32,3584]{1,0:T(8,128)(2,1)S(1)} %sum.17), channel_id=1, source_target_pairs={{0,24},{8,0},{16,8},{24,16},{1,25},{9,1},{17,9},{25,17},{2,26},{10... | collective-permute-start | bytes 688136 | tf_op jit(solution)/shard_map/ppermute | solution.py:313
